TPU v7x, 32 devices: a whole 2x2x4 slice. The times are simulated.
32 devices in a mesh: dp: 16 (over z, y, core), blk: 2 (over x).
Axes of the slice: x: 2, y: 2, z: 4, core: 2. Of those that a mesh axis runs over, the one named last changes fastest.
Arguments:
- inputs: bfloat16 [16, 1024, 512], P('dp', 'blk'), may hold values from -6 to 6
- memory: bfloat16 [16, 1024, 512], P('dp', 'blk'), may hold values from -6 to 6
- cotangent: bfloat16 [16, 1024, 512], P('dp', 'blk'), may hold values from -6 to 6
- target_segments: int32 [16, 1024], P('dp'), may hold values from 0 to 16, as said below
- memory_segments: int32 [16, 1024], P('dp'), may hold values from 0 to 16, as said below
- self_in_weight: bfloat16 [512, 1536], replicated, may hold values from -0.25 to 0.25
- self_in_bias: float32 [2, 512], replicated, may hold values from -1.75 to 1.75
- self_out_weight: bfloat16 [512, 512], replicated, may hold values from -1 to 1
- self_out_bias: float32 [512], replicated, may hold values from -1.75 to 1.75
- first_gain: float32 [512], replicated, may hold values from 0.5 to 1.5
- first_shift: float32 [512], replicated, may hold values from -1.75 to 1.75
- cross_query_weight: bfloat16 [512, 512], replicated, may hold values from -0.25 to 0.25
- cross_pair_weight: bfloat16 [512, 1024], replicated, may hold values from -0.25 to 0.25
- cross_bias: float32 [2, 512], replicated, may hold values from -1.75 to 1.75
- cross_out_weight: bfloat16 [512, 512], replicated, may hold values from -1 to 1
- cross_out_bias: float32 [512], replicated, may hold values from -1.75 to 1.75
- second_gain: float32 [512], replicated, may hold values from 0.5 to 1.5
- second_shift: float32 [512], replicated, may hold values from -1.75 to 1.75
- feed_in_weight: bfloat16 [512, 2048], replicated, may hold values from -0.25 to 0.25
- feed_in_bias: float32 [2048], replicated, may hold values from -1.75 to 1.75
- feed_out_weight: bfloat16 [2048, 512], replicated, may hold values from -0.125 to 0.125
- feed_out_bias: float32 [512], replicated, may hold values from -1.75 to 1.75
- third_gain: float32 [512], replicated, may hold values from 0.5 to 1.5
- third_shift: float32 [512], replicated, may hold values from -1.75 to 1.75
Outputs:
- layer_output: bfloat16 [16, 1024, 512], P('dp', 'blk')
- input_grad: float32 [16, 1024, 512], P('dp', 'blk')
- memory_grad: float32 [16, 1024, 512], P('dp', 'blk')
- self_in_weight_grad: float32 [512, 1536], P('blk')
- self_in_bias_grad: float32 [2, 512], P(None, 'blk')
- self_out_weight_grad: float32 [512, 512], P('blk')
- self_out_bias_grad: float32 [512], P('blk')
- first_gain_grad: float32 [512], P('blk')
- first_shift_grad: float32 [512], P('blk')
- cross_query_weight_grad: float32 [512, 512], P('blk')
- cross_pair_weight_grad: float32 [512, 1024], P('blk')
- cross_bias_grad: float32 [2, 512], P(None, 'blk')
- cross_out_weight_grad: float32 [512, 512], P('blk')
- cross_out_bias_grad: float32 [512], P('blk')
- second_gain_grad: float32 [512], P('blk')
- second_shift_grad: float32 [512], P('blk')
- feed_in_weight_grad: float32 [512, 2048], P('blk')
- feed_in_bias_grad: float32 [2048], P('blk')
- feed_out_weight_grad: float32 [2048, 512], P('blk')
- feed_out_bias_grad: float32 [512], P('blk')
- third_gain_grad: float32 [512], P('blk')
- third_shift_grad: float32 [512], P('blk')
Inputs may be any that keep to these rules, and one draw needn't show every extreme that they name: `target_segments`: numbers never fall along a row, every number occurs in every row, most sentences are short, and one sentence of each row begins among its first 512 positions and ends among its last 512. `memory_segments`: numbers never fall along a row, every number occurs in every row, most sentences are short, and one sentence of each row begins among its first 512 positions and ends among its last 512.
All inputs are finite; a program needn't handle non-finite values.
Results may differ from a plain program's by a relative error of at most 0.03.
Values may be sent and summed in bfloat16 or wider, within the bound.
A program may use at most 192 MiB of HBM per device.

v0:
```python
import jax
import jax.numpy as jnp
from jax import lax
from jax.sharding import PartitionSpec as P

HEADS = 8
HEAD = 64


highest = lax.Precision.HIGHEST


def layer_norm(field, gain, shift):
    centre = field - jnp.mean(field, axis=-1, keepdims=True)
    spread = jnp.mean(centre * centre, axis=-1, keepdims=True)
    return centre * lax.rsqrt(spread + 1e-05) * gain + shift


def smooth_gate(field):
    return jax.nn.gelu(field, approximate=False)


def exact_dot(left, right):
    return jnp.dot(left, right, precision=highest)


def attend(queries, key_rows, value_rows, allowed):
    heads = queries.shape[1]
    count = queries.shape[0]
    key_count = key_rows.shape[0]
    block_size = min(key_count, 512)
    score_scale = HEAD ** (-0.5)

    def block_step(state_carry, block_index):
        running_max, denominator, accumulator = state_carry
        begin = block_index * block_size
        key_block = lax.dynamic_slice_in_dim(key_rows, begin, block_size, 0)
        value_block = lax.dynamic_slice_in_dim(value_rows, begin, block_size, 0)
        scores = (
            jnp.einsum("qhd,khd->hqk", queries, key_block, preferred_element_type=jnp.float32)
            * score_scale
        )
        permitted = allowed(begin, block_size)[None]
        masked = jnp.where(permitted, scores, -1e30)
        new_max = jnp.maximum(running_max, jnp.max(masked, axis=-1))
        factor = jnp.exp(running_max - new_max)
        weights = jnp.where(permitted, jnp.exp(masked - new_max[..., None]), 0.0)
        denominator = denominator * factor + jnp.sum(weights, axis=-1)
        accumulator = accumulator * factor[..., None] + jnp.einsum(
            "hqk,khd->hqd",
            weights.astype(jnp.bfloat16),
            value_block,
            preferred_element_type=jnp.float32,
        )
        return ((new_max, denominator, accumulator), None)

    start_state = (
        jnp.full((heads, count), -1e30, jnp.float32),
        jnp.zeros((heads, count), jnp.float32),
        jnp.zeros((heads, count, queries.shape[2]), jnp.float32),
    )
    final_state, unused = lax.scan(
        block_step, start_state, jnp.arange(key_count // block_size, dtype=jnp.int32)
    )
    running_max, denominator, accumulator = final_state
    output = jnp.transpose(accumulator / denominator[..., None], (1, 0, 2))
    return (output, running_max + jnp.log(denominator))


def attend_back(queries, key_rows, value_rows, allowed, log_total, output, output_grad):
    key_count = key_rows.shape[0]
    block_size = min(key_count, 512)
    score_scale = HEAD ** (-0.5)
    delta_rows = jnp.transpose(jnp.sum(output_grad.astype(jnp.float32) * output, axis=-1))

    def block_step(query_grad, block_index):
        begin = block_index * block_size
        key_block = lax.dynamic_slice_in_dim(key_rows, begin, block_size, 0)
        value_block = lax.dynamic_slice_in_dim(value_rows, begin, block_size, 0)
        scores = (
            jnp.einsum("qhd,khd->hqk", queries, key_block, preferred_element_type=jnp.float32)
            * score_scale
        )
        permitted = allowed(begin, block_size)[None]
        probs = jnp.where(
            permitted, jnp.exp(jnp.where(permitted, scores, -1e30) - log_total[..., None]), 0.0
        )
        prob_grad = jnp.einsum(
            "qhd,khd->hqk", output_grad, value_block, preferred_element_type=jnp.float32
        )
        score_grad = (probs * (prob_grad - delta_rows[..., None])).astype(jnp.bfloat16)
        value_grad = jnp.einsum(
            "hqk,qhd->khd",
            probs.astype(jnp.bfloat16),
            output_grad,
            preferred_element_type=jnp.float32,
        )
        key_grad = (
            jnp.einsum("hqk,qhd->khd", score_grad, queries, preferred_element_type=jnp.float32)
            * score_scale
        )
        query_grad = (
            query_grad
            + jnp.einsum("hqk,khd->qhd", score_grad, key_block, preferred_element_type=jnp.float32)
            * score_scale
        )
        pair_block = jnp.concatenate(
            [key_grad.reshape(block_size, -1), value_grad.reshape(block_size, -1)], axis=1
        )
        return (query_grad, pair_block)

    query_grad, pair_grads = lax.scan(
        block_step,
        jnp.zeros(queries.shape, jnp.float32),
        jnp.arange(key_count // block_size, dtype=jnp.int32),
    )
    return (query_grad, pair_grads.reshape(key_count, -1))


def column_sums(matrix):
    return jnp.sum(matrix.astype(jnp.float32), axis=0)


def on_device(
    inputs,
    memory,
    cotangent,
    target_segments,
    memory_segments,
    self_in_weight,
    self_in_bias,
    self_out_weight,
    self_out_bias,
    first_gain,
    first_shift,
    cross_query_weight,
    cross_pair_weight,
    cross_bias,
    cross_out_weight,
    cross_out_bias,
    second_gain,
    second_shift,
    feed_in_weight,
    feed_in_bias,
    feed_out_weight,
    feed_out_bias,
    third_gain,
    third_shift,
):
    input_rows = inputs[0]
    memory_rows = memory[0]
    output_grad_rows = cotangent[0].astype(jnp.float32)
    tokens_here, features = input_rows.shape
    offset = lax.axis_index("blk") * tokens_here
    target_all = target_segments[0]
    source_all = memory_segments[0]
    target_here = lax.dynamic_slice_in_dim(target_all, offset, tokens_here, 0)
    position_here = offset + jnp.arange(tokens_here, dtype=jnp.int32)

    def self_allowed(begin, block_size):
        key_segment = lax.dynamic_slice_in_dim(target_all, begin, block_size, 0)
        key_position = begin + jnp.arange(block_size, dtype=jnp.int32)
        return (target_here[:, None] == key_segment[None, :]) & (
            key_position[None, :] <= position_here[:, None]
        )

    def cross_allowed(begin, block_size):
        key_segment = lax.dynamic_slice_in_dim(source_all, begin, block_size, 0)
        return target_here[:, None] == key_segment[None, :]

    blank_row = jnp.zeros((features,), jnp.float32)
    query_bias = self_in_bias[0]
    self_pair_bias = jnp.concatenate([blank_row, self_in_bias[1]])
    memory_pair_bias = jnp.concatenate([blank_row, cross_bias[1]])
    projected = (
        jnp.dot(input_rows, self_in_weight, preferred_element_type=jnp.float32)
        + jnp.concatenate([query_bias, self_pair_bias])
    ).astype(jnp.bfloat16)
    self_queries = projected[:, :features]
    local_memory_pairs = (
        jnp.dot(memory_rows, cross_pair_weight, preferred_element_type=jnp.float32)
        + memory_pair_bias
    ).astype(jnp.bfloat16)
    self_pairs, memory_pairs = (
        lax.all_gather(projected[:, features:], "blk", axis=0, tiled=True),
        lax.all_gather(local_memory_pairs, "blk", axis=0, tiled=True),
    )
    key_total = self_pairs.shape[0]
    self_keys = self_pairs[:, :features].reshape(key_total, HEADS, HEAD)
    self_values = self_pairs[:, features:].reshape(key_total, HEADS, HEAD)
    memory_keys = memory_pairs[:, :features].reshape(key_total, HEADS, HEAD)
    memory_values = memory_pairs[:, features:].reshape(key_total, HEADS, HEAD)
    self_heads = self_queries.reshape(tokens_here, HEADS, HEAD)
    attended_one, total_one = attend(self_heads, self_keys, self_values, self_allowed)
    attended_one_low = attended_one.reshape(tokens_here, features).astype(jnp.bfloat16)
    first_input = (
        input_rows.astype(jnp.float32)
        + jnp.dot(attended_one_low, self_out_weight, preferred_element_type=jnp.float32)
        + self_out_bias
    )
    first, first_back = jax.vjp(layer_norm, first_input, first_gain, first_shift)
    first_low = first.astype(jnp.bfloat16)
    cross_queries = (
        jnp.dot(first_low, cross_query_weight, preferred_element_type=jnp.float32) + cross_bias[0]
    ).astype(jnp.bfloat16)
    cross_heads = cross_queries.reshape(tokens_here, HEADS, HEAD)
    attended_two, total_two = attend(cross_heads, memory_keys, memory_values, cross_allowed)
    attended_two_low = attended_two.reshape(tokens_here, features).astype(jnp.bfloat16)
    second_input = (
        first
        + jnp.dot(attended_two_low, cross_out_weight, preferred_element_type=jnp.float32)
        + cross_out_bias
    )
    second, second_back = jax.vjp(layer_norm, second_input, second_gain, second_shift)
    second_low = second.astype(jnp.bfloat16)
    hidden = jnp.dot(second_low, feed_in_weight, preferred_element_type=jnp.float32) + feed_in_bias
    active, active_back = jax.vjp(smooth_gate, hidden)
    active_low = active.astype(jnp.bfloat16)
    third_input = (
        second
        + jnp.dot(active_low, feed_out_weight, preferred_element_type=jnp.float32)
        + feed_out_bias
    )
    layer_output, third_back = jax.vjp(layer_norm, third_input, third_gain, third_shift)
    third_grad, third_gain_grad, third_shift_grad = third_back(output_grad_rows)
    branch_three = third_grad.astype(jnp.bfloat16)
    feed_out_weight_grad = jnp.dot(active_low.T, branch_three, preferred_element_type=jnp.float32)
    feed_out_bias_grad = column_sums(branch_three)
    (hidden_grad,) = active_back(
        jnp.dot(branch_three, feed_out_weight.T, preferred_element_type=jnp.float32)
    )
    hidden_low = hidden_grad.astype(jnp.bfloat16)
    feed_in_weight_grad = jnp.dot(second_low.T, hidden_low, preferred_element_type=jnp.float32)
    feed_in_bias_grad = column_sums(hidden_low)
    second_grad_in = third_grad + jnp.dot(
        hidden_low, feed_in_weight.T, preferred_element_type=jnp.float32
    )
    second_grad, second_gain_grad, second_shift_grad = second_back(second_grad_in)
    branch_two = second_grad.astype(jnp.bfloat16)
    cross_out_weight_grad = jnp.dot(
        attended_two_low.T, branch_two, preferred_element_type=jnp.float32
    )
    cross_out_bias_grad = column_sums(branch_two)
    attended_two_grad = (
        jnp.dot(branch_two, cross_out_weight.T, preferred_element_type=jnp.float32)
        .astype(jnp.bfloat16)
        .reshape(tokens_here, HEADS, HEAD)
    )
    cross_query_grad, memory_pair_terms = attend_back(
        cross_heads,
        memory_keys,
        memory_values,
        cross_allowed,
        total_two,
        attended_two,
        attended_two_grad,
    )
    pair_weight_wide = cross_pair_weight.astype(jnp.float32)
    memory_pair_grad = lax.psum_scatter(
        memory_pair_terms.astype(jnp.bfloat16), "blk", scatter_dimension=0, tiled=True
    ).astype(jnp.float32)
    cross_pair_weight_grad = exact_dot(memory_rows.astype(jnp.float32).T, memory_pair_grad)
    memory_value_sum = column_sums(memory_pair_grad[:, features:])
    memory_grad = exact_dot(memory_pair_grad, pair_weight_wide.T)
    cross_query_low = cross_query_grad.reshape(tokens_here, features).astype(jnp.bfloat16)
    cross_query_weight_grad = jnp.dot(
        first_low.T, cross_query_low, preferred_element_type=jnp.float32
    )
    cross_bias_grad = jnp.stack([column_sums(cross_query_low), memory_value_sum])
    first_grad_in = second_grad + jnp.dot(
        cross_query_low, cross_query_weight.T, preferred_element_type=jnp.float32
    )
    first_grad, first_gain_grad, first_shift_grad = first_back(first_grad_in)
    branch_one = first_grad.astype(jnp.bfloat16)
    self_out_weight_grad = jnp.dot(
        attended_one_low.T, branch_one, preferred_element_type=jnp.float32
    )
    self_out_bias_grad = column_sums(branch_one)
    attended_one_grad = (
        jnp.dot(branch_one, self_out_weight.T, preferred_element_type=jnp.float32)
        .astype(jnp.bfloat16)
        .reshape(tokens_here, HEADS, HEAD)
    )
    self_query_grad, self_pair_terms = attend_back(
        self_heads, self_keys, self_values, self_allowed, total_one, attended_one, attended_one_grad
    )
    query_grad_rows = self_query_grad.reshape(tokens_here, features)
    self_weight_wide = self_in_weight.astype(jnp.float32)
    input_wide = input_rows.astype(jnp.float32)
    self_pair_grad = lax.psum_scatter(
        self_pair_terms.astype(jnp.bfloat16), "blk", scatter_dimension=0, tiled=True
    ).astype(jnp.float32)
    projected_grad = jnp.concatenate([query_grad_rows, self_pair_grad], axis=1)
    self_in_weight_grad = exact_dot(input_wide.T, projected_grad)
    self_value_sum = column_sums(self_pair_grad[:, features:])
    pair_input_grad = exact_dot(self_pair_grad, self_weight_wide[:, features:].T)
    self_in_bias_grad = jnp.stack([column_sums(query_grad_rows), self_value_sum])
    input_grad = (
        first_grad + exact_dot(query_grad_rows, self_weight_wide[:, :features].T) + pair_input_grad
    )
    shares = (
        lax.psum_scatter(
            self_in_weight_grad.astype(jnp.bfloat16), "blk", scatter_dimension=0, tiled=True
        ).astype(jnp.float32),
        lax.psum_scatter(
            self_in_bias_grad.astype(jnp.bfloat16), "blk", scatter_dimension=1, tiled=True
        ).astype(jnp.float32),
        lax.psum_scatter(
            self_out_weight_grad.astype(jnp.bfloat16), "blk", scatter_dimension=0, tiled=True
        ).astype(jnp.float32),
        lax.psum_scatter(
            self_out_bias_grad.astype(jnp.bfloat16), "blk", scatter_dimension=0, tiled=True
        ).astype(jnp.float32),
        lax.psum_scatter(
            first_gain_grad.astype(jnp.bfloat16), "blk", scatter_dimension=0, tiled=True
        ).astype(jnp.float32),
        lax.psum_scatter(
            first_shift_grad.astype(jnp.bfloat16), "blk", scatter_dimension=0, tiled=True
        ).astype(jnp.float32),
        lax.psum_scatter(
            cross_query_weight_grad.astype(jnp.bfloat16), "blk", scatter_dimension=0, tiled=True
        ).astype(jnp.float32),
        lax.psum_scatter(
            cross_pair_weight_grad.astype(jnp.bfloat16), "blk", scatter_dimension=0, tiled=True
        ).astype(jnp.float32),
        lax.psum_scatter(
            cross_bias_grad.astype(jnp.bfloat16), "blk", scatter_dimension=1, tiled=True
        ).astype(jnp.float32),
        lax.psum_scatter(
            cross_out_weight_grad.astype(jnp.bfloat16), "blk", scatter_dimension=0, tiled=True
        ).astype(jnp.float32),
        lax.psum_scatter(
            cross_out_bias_grad.astype(jnp.bfloat16), "blk", scatter_dimension=0, tiled=True
        ).astype(jnp.float32),
        lax.psum_scatter(
            second_gain_grad.astype(jnp.bfloat16), "blk", scatter_dimension=0, tiled=True
        ).astype(jnp.float32),
        lax.psum_scatter(
            second_shift_grad.astype(jnp.bfloat16), "blk", scatter_dimension=0, tiled=True
        ).astype(jnp.float32),
        lax.psum_scatter(
            feed_in_weight_grad.astype(jnp.bfloat16), "blk", scatter_dimension=0, tiled=True
        ).astype(jnp.float32),
        lax.psum_scatter(
            feed_in_bias_grad.astype(jnp.bfloat16), "blk", scatter_dimension=0, tiled=True
        ).astype(jnp.float32),
        lax.psum_scatter(
            feed_out_weight_grad.astype(jnp.bfloat16), "blk", scatter_dimension=0, tiled=True
        ).astype(jnp.float32),
        lax.psum_scatter(
            feed_out_bias_grad.astype(jnp.bfloat16), "blk", scatter_dimension=0, tiled=True
        ).astype(jnp.float32),
        lax.psum_scatter(
            third_gain_grad.astype(jnp.bfloat16), "blk", scatter_dimension=0, tiled=True
        ).astype(jnp.float32),
        lax.psum_scatter(
            third_shift_grad.astype(jnp.bfloat16), "blk", scatter_dimension=0, tiled=True
        ).astype(jnp.float32),
    )
    totals = (
        lax.psum(shares[0].astype(jnp.bfloat16), "dp").astype(jnp.float32),
        lax.psum(shares[1].astype(jnp.bfloat16), "dp").astype(jnp.float32),
        lax.psum(shares[2].astype(jnp.bfloat16), "dp").astype(jnp.float32),
        lax.psum(shares[3].astype(jnp.bfloat16), "dp").astype(jnp.float32),
        lax.psum(shares[4].astype(jnp.bfloat16), "dp").astype(jnp.float32),
        lax.psum(shares[5].astype(jnp.bfloat16), "dp").astype(jnp.float32),
        lax.psum(shares[6].astype(jnp.bfloat16), "dp").astype(jnp.float32),
        lax.psum(shares[7].astype(jnp.bfloat16), "dp").astype(jnp.float32),
        lax.psum(shares[8].astype(jnp.bfloat16), "dp").astype(jnp.float32),
        lax.psum(shares[9].astype(jnp.bfloat16), "dp").astype(jnp.float32),
        lax.psum(shares[10].astype(jnp.bfloat16), "dp").astype(jnp.float32),
        lax.psum(shares[11].astype(jnp.bfloat16), "dp").astype(jnp.float32),
        lax.psum(shares[12].astype(jnp.bfloat16), "dp").astype(jnp.float32),
        lax.psum(shares[13].astype(jnp.bfloat16), "dp").astype(jnp.float32),
        lax.psum(shares[14].astype(jnp.bfloat16), "dp").astype(jnp.float32),
        lax.psum(shares[15].astype(jnp.bfloat16), "dp").astype(jnp.float32),
        lax.psum(shares[16].astype(jnp.bfloat16), "dp").astype(jnp.float32),
        lax.psum(shares[17].astype(jnp.bfloat16), "dp").astype(jnp.float32),
        lax.psum(shares[18].astype(jnp.bfloat16), "dp").astype(jnp.float32),
    )
    return (
        layer_output.astype(jnp.bfloat16)[None],
        input_grad[None],
        memory_grad[None],
        totals[0],
        totals[1],
        totals[2],
        totals[3],
        totals[4],
        totals[5],
        totals[6],
        totals[7],
        totals[8],
        totals[9],
        totals[10],
        totals[11],
        totals[12],
        totals[13],
        totals[14],
        totals[15],
        totals[16],
        totals[17],
        totals[18],
    )


def solution(mesh):
    return jax.shard_map(
        on_device,
        mesh=mesh,
        in_specs=(
            P("dp", "blk", None),
            P("dp", "blk", None),
            P("dp", "blk", None),
            P("dp", None),
            P("dp", None),
            P(),
            P(),
            P(),
            P(),
            P(),
            P(),
            P(),
            P(),
            P(),
            P(),
            P(),
            P(),
            P(),
            P(),
            P(),
            P(),
            P(),
            P(),
            P(),
        ),
        out_specs=(
            P("dp", "blk", None),
            P("dp", "blk", None),
            P("dp", "blk", None),
            P("blk", None),
            P(None, "blk"),
            P("blk", None),
            P("blk"),
            P("blk"),
            P("blk"),
            P("blk", None),
            P("blk", None),
            P(None, "blk"),
            P("blk", None),
            P("blk"),
            P("blk"),
            P("blk"),
            P("blk", None),
            P("blk"),
            P("blk", None),
            P("blk"),
            P("blk"),
            P("blk"),
        ),
        check_vma=False,
    )
```

profile of v0, /device:TPU:0, one launch (start us, length us, event | category | flops | bytes accessed | tf_op | source)
XLA Modules:
  0.0 637.7 jit_solution(17868409040769950057)
XLA Ops:
  13.1 3.1 add_convert_fusion.1
  18.8 30.1 %all-gather.3.cloned.1.call-done = bf16[1024,1024]{1,0:T(8,128)(2,1)} async-done(((bf16[512,1024]{1,0:T(8,128)(2,1)}), bf16[1024,1024]{1,0:T(8,128)(2,1)}) %all-gather.3.cloned.1.call-update) | async-done | bytes 2097168 | tf_op jit(solution)/shard_map/all_gather | solution.py:185
  48.9 3.0 fusion.137
  56.5 35.1 %while.56 = (s32[]{:T(128)}, f32[8,512]{1,0:T(8,128)S(1)}, f32[8,512]{1,0:T(8,128)S(1)}, f32[8,512,64]{1,2,0:T(8,128)}, s32[512]{0:T(512)S(1)}, /*index=5*/s32[2...) while((s32[]{:T(128)}, f32[8,512]{1,0:T(8,128)S(1)}, ...), condition=%wide.region_3.4_spmd.clone, body=%wide.region_0.3_spmd.clone.sunk | while | flops 565728256 | bytes 63717632 | solution.py:62
  58.1 5.8 fusion.235
  63.9 4.6 fusion.236
  69.8 4.2 fusion.238
  75.6 5.8 fusion.235
  81.3 4.6 fusion.236
  87.2 4.4 fusion.238
  96.8 3.0 fusion.136
  106.4 35.1 %while.57 = (s32[]{:T(128)}, f32[8,512]{1,0:T(8,128)S(1)}, f32[8,512]{1,0:T(8,128)S(1)}, f32[8,512,64]{1,2,0:T(8,128)}, s32[512]{0:T(512)S(1)}, /*index=5*/s32[2...) while((s32[]{:T(128)}, f32[8,512]{1,0:T(8,128)S(1)}, ...), condition=%wide.region_9.10_spmd.clone, body=%wide.region_6.9_spmd.clone.sunk | while | flops 565202944 | bytes 63709424 | solution.py:62
  107.9 5.8 fusion.242
  113.7 4.6 fusion.243
  119.6 4.2 fusion.245
  125.3 5.8 fusion.242
  131.1 4.6 fusion.243
  136.9 4.4 fusion.245
  146.0 10.2 %multiply_convert_fusion = (bf16[512,2048]{1,0:T(8,128)(2,1)S(1)}, f32[512,2048]{1,0:T(8,128)S(1)}, f32[512,2048]{1,0:T(8,128)S(1)}) fusion(f32[2048]{0:T(1024)S(1)} %copy-done.72, bf16[512,2048]{1,0:T(8,128)(2,1)S(1)} %copy-done, f32[512,512]{0,1:T(8,128)S(1)} %get-tuple-element.739, f32[512]{0:T(512)S(1)} %copy-done.77, f32[512]{0:T(512)S(1)} %copy-done.66, ...), kind=kOutput, calls=%fused_computation.105 | convolution fusion | flops 1144258560 | bytes 13647872 | tf_op jit(solution)/shard_map/dot_general | solution.py:216
  156.2 11.9 %fusion.142 = (f32[512]{0:T(512)S(1)}, f32[512,512]{0,1:T(8,128)S(1)}) fusion(f32[512]{0:T(512)S(1)} %copy-done.74, bf16[512,2048]{1,0:T(8,128)(2,1)S(1)} %get-tuple-element.715, bf16[2048,512]{1,0:T(8,128)(2,1)S(1)} %copy-done.70, f32[512]{0:T(512)S(1)} %copy-done.77, f32[512]{0:T(512)S(1)} %copy-done.66, f32[512]{0:T(512)S(1)} %fusion.119, ...), kind=kOutput, calls=%fused_computation.229 | convolution fusion | flops 1075576320 | bytes 6303744 | tf_op jit(solution)/shard_map/dot_general | solution.py:221
  171.5 3.4 fusion.130
  181.8 37.4 %while.58 = (s32[]{:T(128)}, f32[512,8,64]{0,2,1:T(8,128)}, bf16[2,512,1024]{2,1,0:T(8,128)(2,1)}, s32[2]{0:T(128)S(1)}, bf16[1024,8,64]{0,2,1:T(8,128)(2,1)}, /...) while((s32[]{:T(128)}, f32[512,8,64]{0,2,1:T(8,128)}, ...), condition=%wide.region_20.21_spmd.clone, body=%wide.region_19.20_spmd.clone.sunk | while | flops 1371013120 | bytes 74769208 | solution.py:112
  185.9 3.1 fusion.257
  196.2 4.1 fusion.258
  204.4 3.1 fusion.257
  214.7 4.4 fusion.258
  226.1 40.5 %while.59 = (s32[]{:T(128)}, f32[512,8,64]{0,2,1:T(8,128)}, bf16[2,512,1024]{2,1,0:T(8,128)(2,1)}, s32[2]{0:T(128)S(1)}, bf16[1024,8,64]{0,2,1:T(8,128)(2,1)}, /...) while((s32[]{:T(128)}, f32[512,8,64]{0,2,1:T(8,128)}, ...), condition=%wide.region_25.26_spmd.clone, body=%wide.region_24.25_spmd.clone.sunk | while | flops 1371538432 | bytes 72680264 | solution.py:112
  230.4 4.5 fusion.271
  242.1 4.2 fusion.272
  250.4 4.4 fusion.271
  262.1 4.5 fusion.272
  272.4 4.8 convolution_convert_fusion
  277.3 4.3 convolution_convert_fusion.1
  281.7 3.1 fusion.100
  285.2 13.5 %reduce-scatter.16.cloned.1.call-done = bf16[512,1024]{1,0:T(8,128)(2,1)} async-done(((bf16[1024,1024]{1,0:T(8,128)(2,1)}), bf16[512,1024]{1,0:T(8,128)(2,1)}) %reduce-scatter.16.cloned.1.call-update) | async-done | bytes 1048592 | tf_op jit(solution)/shard_map/reduce_scatter | solution.py:290
  301.5 4.1 fusion.94
  310.4 5.5 reduce-scatter.24.cloned.1.call-done
  315.9 17.3 %reduce-scatter.28.cloned.1.call-done = bf16[256,512]{1,0:T(8,128)(2,1)} async-done(((bf16[512,512]{1,0:T(8,128)(2,1)}), bf16[256,512]{1,0:T(8,128)(2,1)}) %reduce-scatter.28.cloned.1.call-update) | async-done | bytes 262160 | tf_op jit(solution)/shard_map/reduce_scatter | solution.py:329
  333.3 17.4 %reduce-scatter.22.cloned.1.call-done = bf16[256,512]{1,0:T(8,128)(2,1)} async-done(((bf16[512,512]{1,0:T(8,128)(2,1)}), bf16[256,512]{1,0:T(8,128)(2,1)}) %reduce-scatter.22.cloned.1.call-update) | async-done | bytes 262160 | tf_op jit(solution)/shard_map/reduce_scatter | solution.py:308
  350.7 34.2 %reduce-scatter.32.cloned.1.call-done = bf16[1024,512]{1,0:T(8,128)(2,1)} async-done(((bf16[2048,512]{1,0:T(8,128)(2,1)}), bf16[1024,512]{1,0:T(8,128)(2,1)}) %reduce-scatter.32.cloned.1.call-update) | async-done | bytes 1048592 | tf_op jit(solution)/shard_map/reduce_scatter | solution.py:347
  384.9 34.1 %reduce-scatter.30.cloned.1.call-done = bf16[256,2048]{1,0:T(8,128)(2,1)} async-done(((bf16[512,2048]{1,0:T(8,128)(2,1)}), bf16[256,2048]{1,0:T(8,128)(2,1)}) %reduce-scatter.30.cloned.1.call-update) | async-done | bytes 1048592 | tf_op jit(solution)/shard_map/reduce_scatter | solution.py:341
  419.0 23.1 %reduce-scatter.26.cloned.1.call-done = bf16[256,1024]{0,1:T(8,128)(2,1)} async-done(((bf16[512,1024]{0,1:T(8,128)(2,1)}), bf16[256,1024]{0,1:T(8,128)(2,1)}) %reduce-scatter.26.cloned.1.call-update) | async-done | bytes 524304 | tf_op jit(solution)/shard_map/reduce_scatter | solution.py:323
  442.1 28.9 %reduce-scatter.20.cloned.1.call-done = bf16[256,1536]{0,1:T(8,128)(2,1)} async-done(((bf16[512,1536]{0,1:T(8,128)(2,1)}), bf16[256,1536]{0,1:T(8,128)(2,1)}) %reduce-scatter.20.cloned.1.call-update) | async-done | bytes 786448 | tf_op jit(solution)/shard_map/reduce_scatter | solution.py:302
  474.2 7.0 %all-reduce.13 = (bf16[512]{0:T(512)(128)(2,1)S(1)}, bf16[512]{0:T(512)(128)(2,1)S(1)}, bf16[512]{0:T(512)(128)(2,1)S(1)}, bf16[512]{0:T(512)(128)(2,1)S(1)}, bf...) all-reduce(bf16[512]{0:T(512)(128)(2,1)S(1)} %get-tuple-element.709, ...), channel_id=7, replica_groups=mesh['dp'=16,'blk'=2] {'blk'}, use_global_device_ids=true, to_apply=%region_37.38.clone | all-reduce | flops 6656 | bytes 26624
  493.3 3.9 reduce-scatter.34.cloned.1.call-done
  498.2 35.9 %all-reduce.11 = (bf16[2,256]{1,0:T(2,128)(2,1)S(1)}, bf16[256]{0:T(256)(128)(2,1)S(1)}, bf16[256]{0:T(256)(128)(2,1)S(1)}, bf16[256]{0:T(256)(128)(2,1)S(1)}, b...) all-reduce(bf16[2,256]{1,0:T(2,128)(2,1)S(1)} %copy.171, ...), channel_id=1, replica_groups=mesh['dp'=16,'blk'=2] {'dp'}, use_global_device_ids=true, to_apply=%region_33.34 | all-reduce | flops 4352 | bytes 17408 | tf_op jit(solution)/shard_map/psum | solution.py:362
  541.0 75.8 %all-reduce.16.cloned.1.call-done = (bf16[256,1536]{0,1:T(8,128)(2,1)}, bf16[256,1024]{0,1:T(8,128)(2,1)}, bf16[256,512]{1,0:T(8,128)(2,1)}, bf16[256,512]{1,0:T...) async-done(((bf16[256,1536]{0,1:T(8,128)(2,1)}, bf16[256,1024]{0,1:T(8,128)(2,1)}, bf16[256,512]{1,0:T(8,128)(2,1)}, ...) | async-done | bytes 4194320 | tf_op jit(solution)/shard_map/psum | solution.py:361
  619.7 3.0 convert_element_type.321
  (391 shorter events, 143.0 us)
Async XLA Ops:
  7.2 138.7 %copy-start = (bf16[512,2048]{1,0:T(8,128)(2,1)S(1)}, bf16[512,2048]{1,0:T(8,128)(2,1)}, u32[]{:S(2)}) copy-start(bf16[512,2048]{1,0:T(8,128)(2,1)} %param.50) | copy-start | bytes 6291460
  7.2 41.7 %all-gather.3.cloned.1.call-start = ((), (), s32[]{:S(2)}) async-start(), calls=%async_computation.11 | async-start | bytes 3145728 | tf_op jit(solution)/shard_map/all_gather | solution.py:185
  13.0 83.3 %all-gather.5.cloned.1.call-start = ((), (), s32[]{:S(2)}) async-start(), calls=%async_computation.12 | async-start | bytes 3145728 | tf_op jit(solution)/shard_map/all_gather | solution.py:186
  16.2 265.5 %reduce-scatter.18.cloned.1.call-start = ((), (), s32[]{:S(2)}) async-start(), calls=%async_computation.14 | async-start | bytes 3145728 | tf_op jit(solution)/shard_map/reduce_scatter | solution.py:259
  56.5 36.7 %copy-start.64 = (f32[512]{0:T(512)S(1)}, f32[512]{0:T(512)}, u32[]{:S(2)}) copy-start(f32[512]{0:T(512)} %param.40) | copy-start | bytes 6148
  91.5 8.2 %copy-start.6 = (bf16[512,8,64]{0,2,1:T(8,128)(2,1)}, bf16[512,8,64]{0,2,1:T(8,128)(2,1)S(1)}, u32[]{:S(2)}) copy-start(bf16[512,8,64]{0,2,1:T(8,128)(2,1)S(1)} %get-tuple-element.1266) | copy-start | bytes 1572868
  91.5 8.2 %copy-start.33 = (f32[8,512]{1,0:T(8,128)}, f32[8,512]{1,0:T(8,128)S(1)}, u32[]{:S(2)}) copy-start(f32[8,512]{1,0:T(8,128)S(1)} %get-tuple-element.272) | copy-start | bytes 49156
  91.6 8.2 %copy-start.36 = (f32[8,512]{1,0:T(8,128)}, f32[8,512]{1,0:T(8,128)S(1)}, u32[]{:S(2)}) copy-start(f32[8,512]{1,0:T(8,128)S(1)} %get-tuple-element.267) | copy-start | bytes 49156
  96.2 8.1 %copy-start.56 = (f32[512]{0:T(512)S(1)}, f32[512]{0:T(512)}, u32[]{:S(2)}) copy-start(f32[512]{0:T(512)} %param.41) | copy-start | bytes 6148
  96.3 8.1 %copy-start.75 = (f32[512]{0:T(512)S(1)}, f32[512]{0:T(512)}, u32[]{:S(2)}) copy-start(f32[512]{0:T(512)} %param.42) | copy-start | bytes 6148
  99.8 6.6 %copy-start.50 = (s32[1,1024]{1,0:T(1,128)S(1)}, s32[1,1024]{1,0:T(1,128)}, u32[]{:S(2)}) copy-start(s32[1,1024]{1,0:T(1,128)} %param.36) | copy-start | bytes 12292
  106.4 37.4 %copy-start.73 = (f32[512]{0:T(512)S(1)}, f32[512]{0:T(512)}, u32[]{:S(2)}) copy-start(f32[512]{0:T(512)} %param.47) | copy-start | bytes 6148
  145.7 31.7 %copy-start.22 = (f32[512,512]{0,1:T(8,128)}, f32[512,512]{0,1:T(8,128)S(1)}, u32[]{:S(2)}) copy-start(f32[512,512]{0,1:T(8,128)S(1)} %get-tuple-element.739) | copy-start | bytes 3145732
  145.7 31.7 %copy-start.54 = (f32[512]{0:T(512)}, f32[512]{0:T(512)S(1)}, u32[]{:S(2)}) copy-start(f32[512]{0:T(512)S(1)} %broadcast_multiply_fusion.1) | copy-start | bytes 6148
  146.0 31.5 %copy-start.57 = (f32[512]{0:T(512)}, f32[512]{0:T(512)S(1)}, u32[]{:S(2)}) copy-start(f32[512]{0:T(512)S(1)} %fusion.119) | copy-start | bytes 6148
  146.0 10.2 %copy-start.70 = (bf16[2048,512]{1,0:T(8,128)(2,1)S(1)}, bf16[2048,512]{1,0:T(8,128)(2,1)}, u32[]{:S(2)}) copy-start(bf16[2048,512]{1,0:T(8,128)(2,1)} %param.52) | copy-start | bytes 6291460
  146.0 10.2 %copy-start.74 = (f32[512]{0:T(512)S(1)}, f32[512]{0:T(512)}, u32[]{:S(2)}) copy-start(f32[512]{0:T(512)} %param.53) | copy-start | bytes 6148
  156.2 11.9 %copy-start.80 = (bf16[512,2048]{1,0:T(8,128)(2,1)}, bf16[512,2048]{1,0:T(8,128)(2,1)S(1)}, u32[]{:S(2)}) copy-start(bf16[512,2048]{1,0:T(8,128)(2,1)S(1)} %get-tuple-element.715) | copy-start | bytes 6291460
  156.2 11.9 %copy-start.53 = (f32[512]{0:T(512)S(1)}, f32[512]{0:T(512)}, u32[]{:S(2)}) copy-start(f32[512]{0:T(512)} %param.54) | copy-start | bytes 6148
  156.2 12.2 %copy-start.65 = (f32[512]{0:T(512)S(1)}, f32[512]{0:T(512)}, u32[]{:S(2)}) copy-start(f32[512]{0:T(512)} %param.55) | copy-start | bytes 6148
  181.8 38.9 %copy-start.39 = (bf16[512,512]{1,0:T(8,128)(2,1)S(1)}, bf16[512,512]{1,0:T(8,128)(2,1)}, u32[]{:S(2)}) copy-start(bf16[512,512]{1,0:T(8,128)(2,1)} %param.43) | copy-start | bytes 1572868
  224.4 74.2 %reduce-scatter.16.cloned.1.call-start = ((), (), s32[]{:S(2)}) async-start(), calls=%async_computation.13 | async-start | bytes 3145728 | tf_op jit(solution)/shard_map/reduce_scatter | solution.py:290
  226.1 40.6 %copy-start.76 = (f32[512]{0:T(512)S(1)}, f32[512]{0:T(512)}, u32[]{:S(2)}) copy-start(f32[512]{0:T(512)} %param.42) | copy-start | bytes 6148
  226.3 11.8 %copy-start.44 = (bf16[512,8,64]{0,2,1:T(8,128)(2,1)}, bf16[512,8,64]{0,2,1:T(8,128)(2,1)S(1)}, u32[]{:S(2)}) copy-start(bf16[512,8,64]{0,2,1:T(8,128)(2,1)S(1)} %get-tuple-element.1232) | copy-start | bytes 1572868 | tf_op jit(solution)/shard_map/while
  246.4 11.7 %copy-start.44 = (bf16[512,8,64]{0,2,1:T(8,128)(2,1)}, bf16[512,8,64]{0,2,1:T(8,128)(2,1)S(1)}, u32[]{:S(2)}) copy-start(bf16[512,8,64]{0,2,1:T(8,128)(2,1)S(1)} %get-tuple-element.1232) | copy-start | bytes 1572868 | tf_op jit(solution)/shard_map/while
  266.7 49.3 %reduce-scatter.24.cloned.1.call-start = ((), (), s32[]{:S(2)}) async-start(), calls=%async_computation.17 | async-start | bytes 786432 | tf_op jit(solution)/shard_map/reduce_scatter | solution.py:320
  269.6 63.7 %reduce-scatter.28.cloned.1.call-start = ((), (), s32[]{:S(2)}) async-start(), calls=%async_computation.19 | async-start | bytes 786432 | tf_op jit(solution)/shard_map/reduce_scatter | solution.py:329
  270.9 79.8 %reduce-scatter.22.cloned.1.call-start = ((), (), s32[]{:S(2)}) async-start(), calls=%async_computation.16 | async-start | bytes 786432 | tf_op jit(solution)/shard_map/reduce_scatter | solution.py:308
  272.3 112.5 %reduce-scatter.32.cloned.1.call-start = ((), (), s32[]{:S(2)}) async-start(), calls=%async_computation.21 | async-start | bytes 3145728 | tf_op jit(solution)/shard_map/reduce_scatter | solution.py:347
  277.2 141.8 %reduce-scatter.30.cloned.1.call-start = ((), (), s32[]{:S(2)}) async-start(), calls=%async_computation.20 | async-start | bytes 3145728 | tf_op jit(solution)/shard_map/reduce_scatter | solution.py:341
  281.6 19.9 %copy-start.29 = (bf16[1,512,512]{2,1,0:T(8,128)(2,1)S(1)}, bf16[1,512,512]{2,1,0:T(8,128)(2,1)}, u32[]{:S(2)}) copy-start(bf16[1,512,512]{2,1,0:T(8,128)(2,1)} %param.32) | copy-start | bytes 1572868
  281.6 160.5 %reduce-scatter.26.cloned.1.call-start = ((), (), s32[]{:S(2)}) async-start(), calls=%async_computation.18 | async-start | bytes 1572864 | tf_op jit(solution)/shard_map/reduce_scatter | solution.py:323
  284.8 186.2 %reduce-scatter.20.cloned.1.call-start = ((), (), s32[]{:S(2)}) async-start(), calls=%async_computation.15 | async-start | bytes 2359296 | tf_op jit(solution)/shard_map/reduce_scatter | solution.py:302
  305.5 166.8 %copy-start.79 = (u32[32]{0:T(128)S(1)}, u32[32]{0:T(128)}, u32[]{:S(2)}) copy-start(u32[32]{0:T(128)} %constant.193) | copy-start | bytes 388
  305.5 168.6 %copy-start.59 = (bf16[512]{0:T(512)(128)(2,1)S(1)}, bf16[512]{0:T(512)(128)(2,1)}, u32[]{:S(2)}) copy-start(bf16[512]{0:T(512)(128)(2,1)} %get-tuple-element.570) | copy-start | bytes 3076
  305.6 168.6 %copy-start.60 = (bf16[512]{0:T(512)(128)(2,1)S(1)}, bf16[512]{0:T(512)(128)(2,1)}, u32[]{:S(2)}) copy-start(bf16[512]{0:T(512)(128)(2,1)} %get-tuple-element.703) | copy-start | bytes 3076
  305.6 168.6 %copy-start.62 = (bf16[2048]{0:T(1024)(128)(2,1)S(1)}, bf16[2048]{0:T(1024)(128)(2,1)}, u32[]{:S(2)}) copy-start(bf16[2048]{0:T(1024)(128)(2,1)} %get-tuple-element.705) | copy-start | bytes 12292
  305.6 168.6 %copy-start.63 = (bf16[512]{0:T(512)(128)(2,1)S(1)}, bf16[512]{0:T(512)(128)(2,1)}, u32[]{:S(2)}) copy-start(bf16[512]{0:T(512)(128)(2,1)} %get-tuple-element.707) | copy-start | bytes 3076
  305.6 168.6 %copy-start.68 = (bf16[512]{0:T(512)(128)(2,1)S(1)}, bf16[512]{0:T(512)(128)(2,1)}, u32[]{:S(2)}) copy-start(bf16[512]{0:T(512)(128)(2,1)} %get-tuple-element.566) | copy-start | bytes 3076
  305.6 168.6 %copy-start.69 = (bf16[512]{0:T(512)(128)(2,1)S(1)}, bf16[512]{0:T(512)(128)(2,1)}, u32[]{:S(2)}) copy-start(bf16[512]{0:T(512)(128)(2,1)} %get-tuple-element.574) | copy-start | bytes 3076
  305.6 186.8 %reduce-scatter.36.cloned.1.call-start = ((), (), s32[]{:S(2)}) async-start(), calls=%async_computation.23 | async-start | bytes 196608
  305.9 178.1 %copy-start.13 = (f32[512,512]{0,1:T(8,128)S(1)}, f32[512,512]{0,1:T(8,128)}, u32[]{:S(2)}) copy-start(f32[512,512]{0,1:T(8,128)} %copy-done.12) | copy-start | bytes 3145732
  309.4 187.9 %reduce-scatter.34.cloned.1.call-start = ((), (), s32[]{:S(2)}) async-start(), calls=%async_computation.22 | async-start | bytes 196608
  310.3 306.4 %all-reduce.16.cloned.1.call-start = ((), (), s32[]{:S(2)}) async-start(), calls=%async_computation.24 | async-start | bytes 8388608 | tf_op jit(solution)/shard_map/psum | solution.py:361
  471.0 15.1 %copy-start.21 = (bf16[512,1024]{1,0:T(8,128)(2,1)S(1)}, bf16[512,1024]{1,0:T(8,128)(2,1)}, u32[]{:S(2)}) copy-start(bf16[512,1024]{1,0:T(8,128)(2,1)} %reduce-scatter.16.cloned.1.call-done) | copy-start | bytes 3145732
  616.8 5.9 copy-start.38
  616.8 7.3 %copy-start.42 = (bf16[256,1024]{0,1:T(8,128)(2,1)S(1)}, bf16[256,1024]{0,1:T(8,128)(2,1)}, u32[]{:S(2)}) copy-start(bf16[256,1024]{0,1:T(8,128)(2,1)} %get-tuple-element.681) | copy-start | bytes 1572868
  619.7 11.0 %copy-start.1 = (bf16[512,2048]{1,0:T(8,128)(2,1)S(1)}, bf16[512,2048]{1,0:T(8,128)(2,1)}, u32[]{:S(2)}) copy-start(bf16[512,2048]{1,0:T(8,128)(2,1)} %param.50) | copy-start | bytes 6291460
  (57 other events, 195.1 us)
Sparse Core Ops, SparseCore 0:
  13.1 35.8 all-gather.2
  51.1 33.1 all-gather.4
  224.5 31.8 reduce-scatter.17
  266.8 31.8 reduce-scatter.15
  301.3 14.5 reduce-scatter.23
  318.7 14.5 reduce-scatter.27
  336.1 14.5 reduce-scatter.21
  353.0 31.8 reduce-scatter.31
  387.1 31.8 reduce-scatter.29
  421.8 20.3 reduce-scatter.25
  444.9 26.0 reduce-scatter.19
  473.7 10.3 reduce-scatter.35
  486.9 10.3 reduce-scatter.33
  502.5 114.2 all-reduce.15
where the time goes:
time: 649 us; the launch traced here: 638 us
  waiting for transfers between devices  284 us (44%)
  matrix products  169 us (26%)
  local copies, waits for them, and re-layouts  63.7 us (10%)
  other arithmetic  54.1 us (8%)
  blocking collectives  42.9 us (7%)
  between operations  16.8 us (3%)
    psum x1, waiting for transfers between devices, on_device(): lax.psum(shares[0].astype(jnp.bfloat16), 'dp').astype(jnp.float32)  75.8 us
    psum x1, blocking collectives, on_device(): lax.psum(shares[1].astype(jnp.bfloat16), 'dp').astype(jnp.float32)  35.9 us
    reduce_scatter x1, waiting for transfers between devices, on_device(): lax.psum_scatter(feed_out_weight_grad.astype(jnp.bfloat16), 'blk', scatte...  34.2 us
    reduce_scatter x1, waiting for transfers between devices, on_device(): lax.psum_scatter(feed_in_weight_grad.astype(jnp.bfloat16), 'blk', scatter...  34.1 us
    dot_general x8, matrix products, block_step(): jnp.einsum('qhd,khd->hqk', queries, key_block, preferred_element_type=jnp...  32.7 us
    all_gather x1, waiting for transfers between devices, on_device(): lax.all_gather(projected[:, features:], 'blk', axis=0, tiled=True)  30.1 us
    reduce_scatter x1, waiting for transfers between devices, on_device(): lax.psum_scatter(self_in_weight_grad.astype(jnp.bfloat16), 'blk', scatter...  28.9 us
    reduce_scatter x1, waiting for transfers between devices, on_device(): lax.psum_scatter(cross_pair_weight_grad.astype(jnp.bfloat16), 'blk', scat...  23.1 us
  transfers between devices with their start and end apart: 14, of which 11 were waited for; matrix products, arithmetic and copies ran while one was open for 21% of the time, Pallas kernels for 0%

commit v1 on v0

v1 whole, which is shorter than its diff:
```python
import functools

import jax
import jax.numpy as jnp
from jax import lax
from jax.experimental import pallas as pl
from jax.experimental.pallas import tpu as pltpu
from jax.sharding import PartitionSpec as P

HEAD = 64
TILE = 128
PAIR = 2 * HEAD
WIDE = 512
SCALE = HEAD ** (-0.5)
MASKED = -1e30
F32 = jnp.float32
BF16 = jnp.bfloat16
VMEM_LIMIT = 58 << 20


def nn(left, right):
    return lax.dot_general(left, right, (((1,), (0,)), ((), ())), preferred_element_type=F32)


def nt(left, right):
    return lax.dot_general(left, right, (((1,), (1,)), ((), ())), preferred_element_type=F32)


def tn(left, right):
    return lax.dot_general(left, right, (((0,), (0,)), ((), ())), preferred_element_type=F32)


def col_sum(field):
    return jnp.sum(field, axis=0, keepdims=True)


def normalize(field):
    centre = field - jnp.mean(field, axis=-1, keepdims=True)
    spread = jnp.mean(centre * centre, axis=-1, keepdims=True)
    rstd = lax.rsqrt(spread + 1e-05)
    return centre * rstd, rstd


def normalize_back(grad, gain, normal, rstd):
    scaled = grad * gain
    mean = jnp.mean(scaled, axis=-1, keepdims=True)
    along = jnp.mean(scaled * normal, axis=-1, keepdims=True)
    return (scaled - mean - normal * along) * rstd


def gate(hidden):
    size = jnp.abs(hidden)
    bell = jnp.exp(hidden * hidden * -0.5)
    ratio = 1.0 / (1.0 + (0.3275911 * 0.7071067811865476) * size)
    series = 1.061405429 * ratio - 1.453152027
    series = series * ratio + 1.421413741
    series = series * ratio - 0.284496736
    series = series * ratio + 0.254829592
    tail = (0.5 * series) * ratio * bell
    phi = jnp.where(hidden > 0.0, 1.0 - tail, tail)
    return hidden * phi, phi + hidden * (bell * 0.3989422804014327)


def dyn(index, size):
    return pl.ds(pl.multiple_of(index * size, size), size)


def even_lanes(rows, width):
    return (lax.broadcasted_iota(jnp.int32, (rows, width), 1) // HEAD) % 2 == 0


def even_rows(rows, width):
    return (lax.broadcasted_iota(jnp.int32, (rows, width), 0) // HEAD) % 2 == 0


def split_columns(tile_t, out_ref, tile):
    chosen = even_rows(*tile_t.shape)
    blank = jnp.zeros_like(tile_t)
    out_ref[:, pl.ds(pl.multiple_of(tile * 2 * TILE, 2 * TILE), TILE)] = jnp.where(chosen, tile_t, blank)
    out_ref[:, pl.ds(pl.multiple_of(tile * 2 * TILE + TILE, TILE), TILE)] = jnp.where(
        chosen, blank, tile_t
    )


def split_rows(tile_n, out_ref, tile):
    chosen = even_lanes(*tile_n.shape)
    blank = jnp.zeros_like(tile_n)
    out_ref[pl.ds(pl.multiple_of(tile * 2 * TILE, 2 * TILE), TILE), :] = jnp.where(chosen, tile_n, blank)
    out_ref[pl.ds(pl.multiple_of(tile * 2 * TILE + TILE, TILE), TILE), :] = jnp.where(
        chosen, blank, tile_n
    )


def spread_segments(column_ref, wide_ref):
    total = column_ref.shape[0]
    step = min(total, 512)

    @pl.loop(0, total // step)
    def _(block):
        rows = dyn(block, step)
        wide_ref[rows, :] = jnp.broadcast_to(column_ref[rows, :], (step, TILE))


def tile_bias(query_row, key_wide_ref, tile, key_tile, offset, causal):
    allowed = key_wide_ref[dyn(key_tile, TILE), :] == query_row
    if causal:
        key_position = key_tile * TILE + lax.broadcasted_iota(jnp.int32, (TILE, TILE), 0)
        query_position = offset + tile * TILE + lax.broadcasted_iota(jnp.int32, (TILE, TILE), 1)
        allowed = allowed & (key_position <= query_position)
    return jnp.where(allowed, 0.0, MASKED)


def attend(
    tiles, ranges_ref, query_row_ref, key_wide_ref, offset, causal,
    query_cols, keys, values_t, attended_t, lse_ref, peak, total, sums,
):
    pairs = WIDE // PAIR

    @pl.loop(0, tiles)
    def _(tile):
        peak[...] = jnp.full(peak.shape, MASKED, F32)
        total[...] = jnp.zeros(total.shape, F32)
        sums[...] = jnp.zeros(sums.shape, F32)
        query_row = query_row_ref[:, dyn(tile, TILE)]

        @pl.loop(ranges_ref[0, tile], ranges_ref[1, tile])
        def _(key_tile):
            rows = dyn(key_tile, TILE)
            bias = tile_bias(query_row, key_wide_ref, tile, key_tile, offset, causal)
            bias = jnp.concatenate([bias, bias], axis=1)
            for pair in range(pairs):
                lanes = slice(pair * PAIR, (pair + 1) * PAIR)
                scores = nn(keys[rows, lanes], query_cols[lanes, dyn(tile, 2 * TILE)]) + bias
                before = peak[pair : pair + 1, :]
                after = jnp.maximum(before, jnp.max(scores, axis=0, keepdims=True))
                factor = jnp.exp(before - after)
                weights = jnp.exp(scores - after)
                peak[pair : pair + 1, :] = after
                total[pair : pair + 1, :] = total[pair : pair + 1, :] * factor + col_sum(weights)
                mixed = nn(values_t[lanes, rows], weights.astype(BF16))
                first = slice(pair * PAIR, pair * PAIR + HEAD)
                second = slice(pair * PAIR + HEAD, (pair + 1) * PAIR)
                sums[first, :] = sums[first, :] * factor[:, :TILE] + mixed[:HEAD, :TILE]
                sums[second, :] = sums[second, :] * factor[:, TILE:] + mixed[HEAD:, TILE:]

        for pair in range(pairs):
            amount = total[pair : pair + 1, :]
            lse_ref[pair : pair + 1, dyn(tile, 2 * TILE)] = peak[pair : pair + 1, :] + jnp.log(amount)
            share = 1.0 / amount
            first = slice(pair * PAIR, pair * PAIR + HEAD)
            second = slice(pair * PAIR + HEAD, (pair + 1) * PAIR)
            attended_t[first, dyn(tile, TILE)] = (sums[first, :] * share[:, :TILE]).astype(BF16)
            attended_t[second, dyn(tile, TILE)] = (sums[second, :] * share[:, TILE:]).astype(BF16)


def attend_back(
    tiles, ranges_ref, query_row_ref, key_wide_ref, offset, causal,
    query_cols, query_rows, grad_cols, grad_rows, keys, keys_t, values, lse_ref, delta_ref,
    query_grad_t, key_grad, value_grad,
):
    pairs = WIDE // PAIR

    @pl.loop(0, tiles)
    def _(tile):
        query_row = query_row_ref[:, dyn(tile, TILE)]
        both = dyn(tile, 2 * TILE)

        @pl.loop(ranges_ref[0, tile], ranges_ref[1, tile])
        def _(key_tile):
            rows = dyn(key_tile, TILE)
            bias = tile_bias(query_row, key_wide_ref, tile, key_tile, offset, causal)
            bias = jnp.concatenate([bias, bias], axis=1)
            for pair in range(pairs):
                lanes = slice(pair * PAIR, (pair + 1) * PAIR)
                scores = nn(keys[rows, lanes], query_cols[lanes, both]) + bias
                probs = jnp.exp(scores - lse_ref[pair : pair + 1, both])
                prob_grad = nn(values[rows, lanes], grad_cols[lanes, both])
                score_grad = (probs * (prob_grad - delta_ref[pair : pair + 1, both])).astype(BF16)
                value_grad[rows, lanes] += nn(probs.astype(BF16), grad_rows[both, lanes])
                key_grad[rows, lanes] += nn(score_grad, query_rows[both, lanes])
                mixed = nn(keys_t[lanes, rows], score_grad)
                first = slice(pair * PAIR, pair * PAIR + HEAD)
                second = slice(pair * PAIR + HEAD, (pair + 1) * PAIR)
                query_grad_t[first, dyn(tile, TILE)] += mixed[:HEAD, :TILE]
                query_grad_t[second, dyn(tile, TILE)] += mixed[HEAD:, TILE:]


def clear(ref):
    rows = ref.shape[0]
    step = min(rows, 256)

    @pl.loop(0, rows // step)
    def _(block):
        ref[dyn(block, step), :] = jnp.zeros((step, ref.shape[1]), ref.dtype)


def transpose_rows(source, target):
    @pl.loop(0, source.shape[0] // TILE)
    def _(block):
        target[:, dyn(block, TILE)] = source[dyn(block, TILE), :].T


def out_like(shape, dtype):
    return jax.ShapeDtypeStruct(shape, dtype)


def run(body, ins, smem_count, outs, scratch, flops, bytes_accessed):
    vm = pl.BlockSpec(memory_space=pltpu.VMEM)
    sm = pl.BlockSpec(memory_space=pltpu.SMEM)
    return pl.pallas_call(
        body,
        in_specs=[sm] * smem_count + [vm] * (len(ins) - smem_count),
        out_specs=[vm] * len(outs),
        out_shape=outs,
        scratch_shapes=scratch,
        cost_estimate=pl.CostEstimate(
            flops=flops, bytes_accessed=bytes_accessed, transcendentals=0
        ),
        compiler_params=pltpu.CompilerParams(vmem_limit_bytes=VMEM_LIMIT),
    )(*ins)


def self_forward(n, rows_block, place_ref, ranges_ref, *refs):
    pieces, refs = refs[:n], refs[n:]
    (
        query_segment, key_segment, weight, bias, out_weight, out_bias, gain, shift,
        cross_weight, cross_bias,
        query_out, keys, values, attended_t, lse_ref, normal_out, rstd_out, first_low, cross_query,
        wide, values_t, query_cols, peak, total, sums,
    ) = refs
    count = pieces[0].shape[0]
    place = place_ref[0]
    spread_segments(key_segment, wide)

    for step in range(n):
        spot = lax.rem(place + n - step, n)

        @pl.when(spot <= place)
        def _():
            @pl.loop(0, count // rows_block)
            def _(block):
                source = pieces[step][dyn(block, rows_block), :]
                rows = dyn(spot * (count // rows_block) + block, rows_block)
                keys[rows, :] = nn(source, weight[:, WIDE : 2 * WIDE]).astype(BF16)
                values[rows, :] = (nn(source, weight[:, 2 * WIDE :]) + bias[1:2, :]).astype(BF16)
                if step == 0:
                    query = (nn(source, weight[:, :WIDE]) + bias[0:1, :]).astype(BF16)
                    query_out[dyn(block, rows_block), :] = (query.astype(F32) * SCALE).astype(BF16)

        @pl.when(spot > place)
        def _():
            @pl.loop(0, count // rows_block)
            def _(block):
                rows = dyn(spot * (count // rows_block) + block, rows_block)
                keys[rows, :] = jnp.zeros((rows_block, WIDE), BF16)
                values[rows, :] = jnp.zeros((rows_block, WIDE), BF16)

    transpose_rows(values, values_t)
    tiles = count // TILE

    @pl.loop(0, tiles)
    def _(tile):
        split_columns(query_out[dyn(tile, TILE), :].T, query_cols, tile)

    attend(
        tiles, ranges_ref, query_segment, wide, place * count, True,
        query_cols, keys, values_t, attended_t, lse_ref, peak, total, sums,
    )

    @pl.loop(0, count // rows_block)
    def _(block):
        rows = dyn(block, rows_block)
        attended = attended_t[:, rows].T
        field = pieces[0][rows, :].astype(F32) + nn(attended, out_weight[...]) + out_bias[...]
        normal, rstd = normalize(field)
        normal_out[rows, :] = normal
        rstd_out[rows, :] = rstd
        low = (normal * gain[...] + shift[...]).astype(BF16)
        first_low[rows, :] = low
        query = (nn(low, cross_weight[...]) + cross_bias[0:1, :]).astype(BF16)
        cross_query[rows, :] = (query.astype(F32) * SCALE).astype(BF16)


def cross_and_feed(n, rows_block, place_ref, ranges_ref, *refs):
    pieces, refs = refs[:n], refs[n:]
    (
        query_segment, key_segment, cotangent, cross_query, first_normal, first_gain, first_shift,
        pair_weight, cross_bias, out_weight, out_bias, gain, shift,
        in_weight, in_bias, down_weight, down_bias, last_gain, last_shift,
        layer_output, keys, values, lse_ref, delta_ref, out_grad, grad_out, g2_out,
        in_grad, down_grad, cross_out_grad, sums_out, in_bias_grad,
        wide, values_t, query_cols, peak, total, sums, attended_t, second_normal, second_rstd,
        second_low, second_low_t, active, slope, third, branch, branch_t,
    ) = refs
    count = pieces[0].shape[0]
    place = place_ref[0]
    spread_segments(key_segment, wide)
    blocks = count // rows_block

    for step in range(n):
        spot = lax.rem(place + n - step, n)

        @pl.loop(0, blocks)
        def _(block):
            source = pieces[step][dyn(block, rows_block), :]
            rows = dyn(spot * blocks + block, rows_block)
            keys[rows, :] = nn(source, pair_weight[:, :WIDE]).astype(BF16)
            values[rows, :] = (nn(source, pair_weight[:, WIDE:]) + cross_bias[1:2, :]).astype(BF16)

    transpose_rows(values, values_t)
    tiles = count // TILE

    @pl.loop(0, tiles)
    def _(tile):
        split_columns(cross_query[dyn(tile, TILE), :].T, query_cols, tile)

    attend(
        tiles, ranges_ref, query_segment, wide, 0, False,
        query_cols, keys, values_t, attended_t, lse_ref, peak, total, sums,
    )

    @pl.loop(0, blocks)
    def _(block):
        rows = dyn(block, rows_block)
        attended = attended_t[:, rows].T
        first = first_normal[rows, :] * first_gain[...] + first_shift[...]
        field = first + nn(attended, out_weight[...]) + out_bias[...]
        normal, rstd = normalize(field)
        second_normal[rows, :] = normal
        second_rstd[rows, :] = rstd
        second = normal * gain[...] + shift[...]
        third[rows, :] = second + down_bias[...]
        low = second.astype(BF16)
        second_low[rows, :] = low
        second_low_t[:, rows] = low.T

    hidden_size = in_weight.shape[1]
    chunk_size = min(WIDE, hidden_size // n)
    chunks = hidden_size // chunk_size

    @pl.loop(0, chunks)
    def _(chunk):
        lanes = dyn(chunk, chunk_size)

        @pl.loop(0, blocks)
        def _(block):
            rows = dyn(block, rows_block)
            hidden = nn(second_low[rows, :], in_weight[:, lanes]) + in_bias[:, lanes]
            value, derivative = gate(hidden)
            value = value.astype(BF16)
            active[rows, lanes] = value
            slope[rows, lanes] = derivative.astype(slope.dtype)
            third[rows, :] += nn(value, down_weight[dyn(chunk, chunk_size), :])

    sums_out[...] = jnp.zeros(sums_out.shape, F32)
    in_bias_grad[...] = jnp.zeros(in_bias_grad.shape, F32)

    @pl.loop(0, blocks)
    def _(block):
        rows = dyn(block, rows_block)
        normal, rstd = normalize(third[rows, :])
        layer_output[rows, :] = (normal * last_gain[...] + last_shift[...]).astype(BF16)
        outer = cotangent[rows, :].astype(F32)
        grad = normalize_back(outer, last_gain[...], normal, rstd)
        third[rows, :] = grad
        low = grad.astype(BF16)
        branch[rows, :] = low
        sums_out[0:1, :] += col_sum(outer * normal)
        sums_out[1:2, :] += col_sum(outer)
        sums_out[2:3, :] += col_sum(low.astype(F32))

    half = WIDE // n
    down_half = down_weight.shape[0] // n

    @pl.loop(0, chunks)
    def _(chunk):
        lanes = dyn(chunk, chunk_size)
        share = tn(active[:, lanes], branch[...]).astype(BF16)
        per_half = down_half // chunk_size
        down_grad[lax.div(chunk, per_half), dyn(lax.rem(chunk, per_half), chunk_size), :] = share

        @pl.loop(0, blocks)
        def _(block):
            rows = dyn(block, rows_block)
            inner = nt(branch[rows, :], down_weight[dyn(chunk, chunk_size), :])
            hidden_grad = (inner * slope[rows, lanes].astype(F32)).astype(BF16)
            active[rows, lanes] = hidden_grad
            in_bias_grad[:, lanes] += col_sum(hidden_grad.astype(F32))
            third[rows, :] += nt(hidden_grad, in_weight[:, lanes])

        share = nn(second_low_t[...], active[:, lanes]).astype(BF16)
        per_block = WIDE // chunk_size
        block_rows = dyn(lax.div(chunk, per_block), half)
        block_lanes = dyn(lax.rem(chunk, per_block), chunk_size)
        for part in range(n):
            in_grad[part, block_rows, block_lanes] = share[part * half : (part + 1) * half, :]

    @pl.loop(0, blocks)
    def _(block):
        rows = dyn(block, rows_block)
        outer = third[rows, :]
        normal = second_normal[rows, :]
        grad = normalize_back(outer, gain[...], normal, second_rstd[rows, :])
        g2_out[rows, :] = grad
        low = grad.astype(BF16)
        branch[rows, :] = low
        sums_out[3:4, :] += col_sum(outer * normal)
        sums_out[4:5, :] += col_sum(outer)
        sums_out[5:6, :] += col_sum(low.astype(F32))
        grad_out[rows, :] = nt(low, out_weight[...]).astype(BF16)

    share = nn(attended_t[...], branch[...]).astype(BF16)
    for part in range(n):
        cross_out_grad[part] = share[part * half : (part + 1) * half, :]

    write_delta(tiles, grad_out, attended_t, delta_ref)


def write_delta(tiles, grad, attended_t, delta_ref):
    @pl.loop(0, tiles)
    def _(tile):
        product = grad[dyn(tile, TILE), :].astype(F32).T * attended_t[:, dyn(tile, TILE)].astype(F32)
        for pair in range(WIDE // PAIR):
            start = pair * PAIR
            delta_ref[pair : pair + 1, pl.ds(pl.multiple_of(tile * 2 * TILE, 2 * TILE), TILE)] = col_sum(
                product[start : start + HEAD, :]
            )
            delta_ref[
                pair : pair + 1, pl.ds(pl.multiple_of(tile * 2 * TILE + TILE, TILE), TILE)
            ] = col_sum(product[start + HEAD : start + PAIR, :])


def prepare_back(tiles, query, grad, query_cols, query_rows, grad_cols, grad_rows):
    @pl.loop(0, tiles)
    def _(tile):
        here = query[dyn(tile, TILE), :]
        split_columns(here.T, query_cols, tile)
        split_rows(here, query_rows, tile)
        here = grad[dyn(tile, TILE), :]
        split_columns(here.T, grad_cols, tile)
        split_rows(here, grad_rows, tile)


def cross_backward(n, rows_block, place_ref, ranges_ref, *refs):
    pieces, refs = refs[:n], refs[n:]
    (
        query_segment, key_segment, query, grad, keys, values, lse_ref, delta_ref, g2,
        first_normal, first_rstd, first_low, gain, query_weight, pair_weight, self_out_weight,
        self_attended_t,
        own_grad, sent_grad, query_grad_w, pair_grad_w, self_out_grad, self_grad, self_delta, g1_out, sums_out,
        wide, keys_t, query_cols, query_rows, grad_cols, grad_rows, query_grad_t, key_grad, value_grad,
        query_low, branch,
    ) = refs
    count = pieces[0].shape[0]
    place = place_ref[0]
    tiles = count // TILE
    blocks = count // rows_block
    spread_segments(key_segment, wide)
    transpose_rows(keys, keys_t)
    prepare_back(tiles, query, grad, query_cols, query_rows, grad_cols, grad_rows)
    clear(query_grad_t)
    clear(key_grad)
    clear(value_grad)
    attend_back(
        tiles, ranges_ref, query_segment, wide, 0, False,
        query_cols, query_rows, grad_cols, grad_rows, keys, keys_t, values, lse_ref, delta_ref,
        query_grad_t, key_grad, value_grad,
    )
    sums_out[...] = jnp.zeros(sums_out.shape, F32)

    @pl.loop(0, tiles)
    def _(tile):
        rows = dyn(tile, TILE)
        low = (query_grad_t[:, rows].T * SCALE).astype(BF16)
        query_low[rows, :] = low
        sums_out[0:1, :] += col_sum(low.astype(F32))

    half = WIDE // n
    share = tn(first_low[...], query_low[...]).astype(BF16)
    for part in range(n):
        query_grad_w[part] = share[part * half : (part + 1) * half, :]

    for step in range(n):
        spot = lax.rem(place + n - step, n)

        @pl.loop(0, blocks)
        def _(block):
            rows = dyn(spot * blocks + block, rows_block)
            here = dyn(block, rows_block)
            key_low = key_grad[rows, :].astype(BF16)
            value_part = value_grad[rows, :]
            sums_out[1:2, :] += col_sum(value_part)
            value_low = value_part.astype(BF16)
            back = nt(key_low, pair_weight[:, :WIDE]) + nt(value_low, pair_weight[:, WIDE:])
            if step == 0:
                own_grad[here, :] = back
            else:
                sent_grad[step - 1, here, :] = back.astype(BF16)

    half_rows = min(count, 512)
    for side, source in ((0, key_grad), (1, value_grad)):
        share = jnp.zeros((WIDE, WIDE), F32)
        for step in range(n):
            spot = lax.rem(place + n - step, n)
            for block in range(count // half_rows):
                rows = dyn(spot * (count // half_rows) + block, half_rows)
                share += tn(
                    pieces[step][block * half_rows : (block + 1) * half_rows, :],
                    source[rows, :].astype(BF16),
                )
        share = share.astype(BF16)
        for part in range(n):
            pair_grad_w[part, side * half : (side + 1) * half, :] = share[part * half : (part + 1) * half, :]

    @pl.loop(0, blocks)
    def _(block):
        rows = dyn(block, rows_block)
        outer = g2[rows, :] + nt(query_low[rows, :], query_weight[...])
        normal = first_normal[rows, :]
        back = normalize_back(outer, gain[...], normal, first_rstd[rows, :])
        g1_out[rows, :] = back
        low = back.astype(BF16)
        branch[rows, :] = low
        sums_out[2:3, :] += col_sum(outer * normal)
        sums_out[3:4, :] += col_sum(outer)
        sums_out[4:5, :] += col_sum(low.astype(F32))
        self_grad[rows, :] = nt(low, self_out_weight[...]).astype(BF16)

    share = nn(self_attended_t[...], branch[...]).astype(BF16)
    for part in range(n):
        self_out_grad[part] = share[part * half : (part + 1) * half, :]

    write_delta(tiles, self_grad, self_attended_t, self_delta)


def self_backward(n, rows_block, place_ref, ranges_ref, *refs):
    pieces, refs = refs[:n], refs[n:]
    (
        query_segment, key_segment, query, grad, keys, values, lse_ref, delta_ref, g1, weight,
        own_grad, sent_grad, grad_w, sums_out,
        wide, keys_t, query_cols, query_rows, grad_cols, grad_rows, query_grad_t, key_grad, value_grad,
        query_low,
    ) = refs
    count = pieces[0].shape[0]
    place = place_ref[0]
    tiles = count // TILE
    blocks = count // rows_block
    spread_segments(key_segment, wide)
    transpose_rows(keys, keys_t)
    prepare_back(tiles, query, grad, query_cols, query_rows, grad_cols, grad_rows)
    clear(query_grad_t)
    clear(key_grad)
    clear(value_grad)
    attend_back(
        tiles, ranges_ref, query_segment, wide, place * count, True,
        query_cols, query_rows, grad_cols, grad_rows, keys, keys_t, values, lse_ref, delta_ref,
        query_grad_t, key_grad, value_grad,
    )
    sums_out[...] = jnp.zeros(sums_out.shape, F32)

    @pl.loop(0, tiles)
    def _(tile):
        rows = dyn(tile, TILE)
        wide_grad = query_grad_t[:, rows].T * SCALE
        sums_out[0:1, :] += col_sum(wide_grad)
        query_low[rows, :] = wide_grad.astype(BF16)

    for step in range(n):
        spot = lax.rem(place + n - step, n)

        @pl.loop(0, blocks)
        def _(block):
            rows = dyn(spot * blocks + block, rows_block)
            here = dyn(block, rows_block)
            key_low = key_grad[rows, :].astype(BF16)
            value_part = value_grad[rows, :]
            sums_out[1:2, :] += col_sum(value_part)
            value_low = value_part.astype(BF16)
            back = nt(key_low, weight[:, WIDE : 2 * WIDE]) + nt(value_low, weight[:, 2 * WIDE :])
            if step == 0:
                own_grad[here, :] = back + g1[here, :] + nt(query_low[here, :], weight[:, :WIDE])
            else:
                sent_grad[step - 1, here, :] = back.astype(BF16)

    half = WIDE // n
    half_rows = min(count, 512)
    for side, source in ((0, query_low), (1, key_grad), (2, value_grad)):
        share = jnp.zeros((WIDE, WIDE), F32)
        for step in range(1 if side == 0 else n):
            spot = 0 if side == 0 else lax.rem(place + n - step, n)
            for block in range(count // half_rows):
                rows = dyn(spot * (count // half_rows) + block, half_rows)
                share += tn(
                    pieces[step][block * half_rows : (block + 1) * half_rows, :],
                    source[rows, :].astype(BF16),
                )
        share = share.astype(BF16)
        for part in range(n):
            grad_w[part, side * half : (side + 1) * half, :] = share[part * half : (part + 1) * half, :]


def other(value):
    return 1 - value


def reduce_kernel(n, groups, chunk_rows, part_rows, *refs):
    sources, refs = refs[: len(part_rows)], refs[len(part_rows) :]
    (
        small_in, total_out, small_out,
        field, from_core, from_blk, from_y, from_z, total,
        small_held, small_core, small_blk, small_y, small_z,
        load_sem, send, recv, small_send, small_recv, store_sem,
    ) = refs
    depth = groups // 4
    group = lax.axis_index("dp")
    part = lax.axis_index("blk")
    core = lax.rem(group, 2)
    side = lax.rem(lax.div(group, 2), 2)
    level = lax.div(group, 4)
    rows = field.shape[1]
    chunks = rows // chunk_rows
    half = chunk_rows // 2
    quarter = half // 2
    piece = quarter // depth

    loads = []
    start = 0
    for index, source in enumerate(sources):
        loads.append(
            pltpu.make_async_copy(source, field.at[:, pl.ds(start, part_rows[index])], load_sem.at[index])
        )
        loads[-1].start()
        start += part_rows[index]

    core_peer = (group + 1 - 2 * core, part)
    side_peer = (group + 2 - 4 * side, part)
    blk_peers = [(group, lax.rem(part + step, n)) for step in range(1, n)]
    z_peers = [(lax.rem(group + 4 * step, groups), part) for step in range(1, depth)]
    peers = [core_peer, side_peer] + blk_peers + z_peers
    barrier = pltpu.get_barrier_semaphore()
    for peer in peers:
        pl.semaphore_signal(barrier, inc=1, device_id=peer, device_id_type=pl.DeviceIdType.MESH)
    pl.semaphore_wait(barrier, len(peers))

    def remote(source, target, sem, peer, sends=send, receives=recv):
        return pltpu.make_async_remote_copy(
            src_ref=source, dst_ref=target, send_sem=sends.at[sem], recv_sem=receives.at[sem],
            device_id=peer, device_id_type=pl.DeviceIdType.MESH,
        )

    per_chunk = 4 + (n - 1) + 2 * (depth - 1)

    def span(start, size):
        return pl.ds(pl.multiple_of(start, 16), size)

    def core_copy(c):
        theirs = span(c * chunk_rows + other(core) * half, half)
        return remote(
            field.at[:, theirs], from_core.at[:, pl.ds(c * half, half)], c * per_chunk, core_peer
        )

    def blk_copies(c):
        mine = span(c * chunk_rows + core * half, half)
        return [
            remote(
                field.at[lax.rem(part + step, n), mine],
                from_blk.at[step - 1, pl.ds(c * half, half)],
                c * per_chunk + 3 + step,
                blk_peers[step - 1],
            )
            for step in range(1, n)
        ]

    def side_copy(c):
        theirs = span(c * chunk_rows + core * half + other(side) * quarter, quarter)
        return remote(
            field.at[part, theirs], from_y.at[0, pl.ds(c * quarter, quarter)], c * per_chunk + 1, side_peer
        )

    def own_quarter(c):
        return c * chunk_rows + core * half + side * quarter

    def z_copies(c):
        copies = []
        for step in range(1, depth):
            theirs = span(own_quarter(c) + lax.rem(level + step, depth) * piece, piece)
            copies.append(
                remote(
                    field.at[part, theirs], from_z.at[step - 1, pl.ds(c * piece, piece)],
                    c * per_chunk + 3 + n - 1 + step, z_peers[step - 1],
                )
            )
        return copies

    def z_back_copies(c):
        mine = span(own_quarter(c) + level * piece, piece)
        return [
            remote(
                total.at[mine], total.at[mine], c * per_chunk + 3 + n - 1 + depth - 1 + step, z_peers[step - 1]
            )
            for step in range(1, depth)
        ]

    def side_back_copy(c):
        mine = span(own_quarter(c), quarter)
        return remote(total.at[mine], total.at[mine], c * per_chunk + 2, side_peer)

    def core_back_copy(c):
        mine = span(c * chunk_rows + core * half, half)
        return remote(total.at[mine], total.at[mine], c * per_chunk + 3, core_peer)

    def start_all(copies):
        for copy in copies:
            copy.start()

    def wait_all(copies):
        for copy in copies:
            copy.wait()

    def add_rows(target, target_part, start, size, terms, result=None):
        step = min(size, 64)

        @pl.loop(0, size // step)
        def _(block):
            here = span(start + block * step, step)
            value = target[target_part, here, :].astype(F32)
            for ref, index, begin in terms:
                value = value + ref[index, span(begin + block * step, step), :].astype(F32)
            if result is None:
                target[target_part, here, :] = value.astype(BF16)
            else:
                result[here, :] = value.astype(BF16)

    def small_copies(stage):
        if stage == 0:
            return [remote(small_in, small_core, 0, core_peer, small_send, small_recv)]
        if stage == 1:
            return [
                remote(
                    small_held.at[lax.rem(part + step, n)], small_blk.at[step - 1], step,
                    blk_peers[step - 1], small_send, small_recv,
                )
                for step in range(1, n)
            ]
        if stage == 2:
            return [remote(small_held.at[part], small_y, n, side_peer, small_send, small_recv)]
        return [
            remote(small_y, small_z.at[step - 1], n + step, z_peers[step - 1], small_send, small_recv)
            for step in range(1, depth)
        ]

    start_all(small_copies(0))
    waited = 0
    ready = 0
    for c in range(chunks):
        while ready < (c + 1) * chunk_rows:
            loads[waited].wait()
            ready += part_rows[waited]
            waited += 1
        core_copy(c).start()
    for load in loads[waited:]:
        load.wait()
    for c in range(chunks):
        core_copy(c).wait()
        for b in range(n):
            add_rows(field, b, c * chunk_rows + core * half, half, [(from_core, b, c * half)])
        start_all(blk_copies(c))
        if c == 0:
            wait_all(small_copies(0))
            small_held[...] = small_in[...] + small_core[...]
            start_all(small_copies(1))

    for t in range(chunks + 5):
        c = t
        if c < chunks:
            wait_all(blk_copies(c))
            add_rows(
                field, part, c * chunk_rows + core * half, half,
                [(from_blk, step, c * half) for step in range(n - 1)],
            )
            side_copy(c).start()
        c = t - 1
        if 0 <= c < chunks:
            side_copy(c).wait()
            add_rows(field, part, own_quarter(c), quarter, [(from_y, 0, c * quarter)])
            start_all(z_copies(c))
        c = t - 2
        if 0 <= c < chunks:
            wait_all(z_copies(c))
            add_rows(
                field, part, own_quarter(c) + level * piece, piece,
                [(from_z, step, c * piece) for step in range(depth - 1)], total,
            )
            start_all(z_back_copies(c))
        c = t - 3
        if 0 <= c < chunks:
            wait_all(z_back_copies(c))
            side_back_copy(c).start()
        c = t - 4
        if 0 <= c < chunks:
            side_back_copy(c).wait()
            core_back_copy(c).start()
        if t == 0:
            wait_all(small_copies(1))
            held = small_held[part]
            for step in range(n - 1):
                held = held + small_blk[step]
            small_held[part] = held
            start_all(small_copies(2))
        if t == 1:
            wait_all(small_copies(2))
            small_y[...] = small_y[...] + small_held[part]
            start_all(small_copies(3))
        if t == 2:
            wait_all(small_copies(3))
            held = small_y[...]
            for step in range(depth - 1):
                held = held + small_z[step]
            small_out[...] = held
        c = t - 5
        if 0 <= c < chunks:
            core_back_copy(c).wait()
            done = pl.ds(c * chunk_rows, chunk_rows)
            pltpu.make_async_copy(total.at[done], total_out.at[done], store_sem.at[c]).start()
    for c in range(chunks):
        done = pl.ds(c * chunk_rows, chunk_rows)
        pltpu.make_async_copy(total.at[done], total_out.at[done], store_sem.at[c]).wait()


def reduce_all(n, groups, parts, small):
    part_rows = [part.shape[1] for part in parts]
    rows = sum(part_rows)
    depth = groups // 4
    chunk_rows = max(16 * groups, rows // 8)
    chunks = rows // chunk_rows
    small_rows = small.shape[1]
    per_chunk = 4 + (n - 1) + 2 * (depth - 1)
    vm = pl.BlockSpec(memory_space=pltpu.VMEM)
    hbm = pl.BlockSpec(memory_space=pl.ANY)
    small_buffer = pltpu.VMEM((n, small_rows, WIDE), F32)
    return pl.pallas_call(
        functools.partial(reduce_kernel, n, groups, chunk_rows, part_rows),
        in_specs=[hbm] * len(parts) + [vm],
        out_specs=[hbm, vm],
        out_shape=[out_like((rows, WIDE), BF16), out_like((small_rows, WIDE), F32)],
        scratch_shapes=[
            pltpu.VMEM((n, rows, WIDE), BF16),
            pltpu.VMEM((n, rows // 2, WIDE), BF16),
            pltpu.VMEM((n - 1, rows // 2, WIDE), BF16),
            pltpu.VMEM((1, rows // 4, WIDE), BF16),
            pltpu.VMEM((depth - 1, rows // 4 // depth, WIDE), BF16),
            pltpu.VMEM((rows, WIDE), BF16),
            small_buffer, small_buffer, pltpu.VMEM((n - 1, small_rows, WIDE), F32),
            pltpu.VMEM((small_rows, WIDE), F32), pltpu.VMEM((depth - 1, small_rows, WIDE), F32),
            pltpu.SemaphoreType.DMA((len(parts),)),
            pltpu.SemaphoreType.DMA((chunks * per_chunk,)),
            pltpu.SemaphoreType.DMA((chunks * per_chunk,)),
            pltpu.SemaphoreType.DMA((n + depth,)),
            pltpu.SemaphoreType.DMA((n + depth,)),
            pltpu.SemaphoreType.DMA((chunks,)),
        ],
        compiler_params=pltpu.CompilerParams(
            vmem_limit_bytes=VMEM_LIMIT, collective_id=0, has_side_effects=True
        ),
    )(*parts, small)


def widen_kernel(plan, source, *outs):
    for out, (start, columns) in zip(outs, plan):
        height = out.shape[0]
        for column in range(columns):
            out[:, column * WIDE : (column + 1) * WIDE] = source[
                start + column * height : start + (column + 1) * height, :
            ].astype(F32)


def key_ranges(query_segment, key_segment, tiles, limit):
    edges = query_segment.reshape(tiles, TILE)
    low = jnp.sum((key_segment[None, :] < edges[:, :1]).astype(jnp.int32), axis=1)
    high = jnp.sum((key_segment[None, :] <= edges[:, TILE - 1 :]).astype(jnp.int32), axis=1)
    if limit is not None:
        high = jnp.minimum(high, limit)
    return jnp.stack([low // TILE, (high + TILE - 1) // TILE]).astype(jnp.int32)


def on_device(
    n, groups,
    inputs, memory, cotangent, target_segments, memory_segments,
    self_in_weight, self_in_bias, self_out_weight, self_out_bias, first_gain, first_shift,
    cross_query_weight, cross_pair_weight, cross_bias, cross_out_weight, cross_out_bias,
    second_gain, second_shift, feed_in_weight, feed_in_bias, feed_out_weight, feed_out_bias,
    third_gain, third_shift,
):
    input_rows, memory_rows, cotangent_rows = inputs[0], memory[0], cotangent[0]
    count, features = input_rows.shape
    length = n * count
    hidden = feed_in_weight.shape[1]
    rows_block = min(count, 256)
    tiles = count // TILE
    half = features // n
    place = lax.axis_index("blk").astype(jnp.int32)

    def shifted(field, step):
        return lax.ppermute(field, "blk", [(s, (s + step) % n) for s in range(n)])

    def shifted_back(field, step):
        return lax.ppermute(field, "blk", [(s, (s - step) % n) for s in range(n)])

    input_pieces = [input_rows] + [shifted(input_rows, step) for step in range(1, n)]
    memory_pieces = [memory_rows] + [shifted(memory_rows, step) for step in range(1, n)]

    target_row = target_segments[0]
    source_row = memory_segments[0]
    target_here = lax.dynamic_slice_in_dim(target_row, place * count, count, 0)
    self_ranges = key_ranges(
        target_here, target_row, tiles, place * count + TILE * (1 + jnp.arange(tiles, dtype=jnp.int32))
    )
    cross_ranges = key_ranges(target_here, source_row, tiles, None)
    place_one = place[None]
    query_segment = target_here[None, :]
    target_column = target_row[:, None]
    source_column = source_row[:, None]

    def row(vector):
        return vector[None, :]

    stats = out_like((WIDE // PAIR, 2 * count), F32)
    low_rows = out_like((count, features), BF16)
    wide_rows = out_like((count, features), F32)
    low_row_all = out_like((length, features), BF16)
    statistic = out_like((count, 1), F32)
    wide_scratch = pltpu.VMEM((length, TILE), jnp.int32)
    values_t = pltpu.VMEM((features, length), BF16)
    query_cols = pltpu.VMEM((features, 2 * count), BF16)
    query_rows = pltpu.VMEM((2 * count, features), BF16)
    peak = pltpu.VMEM((8, 2 * TILE), F32)
    sums = pltpu.VMEM((features, TILE), F32)
    square = 2 * count * features * features

    (
        query, keys, values, attended_t, lse, normal, rstd, first_low, cross_query
    ) = run(
        functools.partial(self_forward, n, rows_block),
        [place_one, self_ranges, *input_pieces, query_segment, target_column,
         self_in_weight, self_in_bias, self_out_weight, row(self_out_bias), row(first_gain),
         row(first_shift), cross_query_weight, cross_bias],
        2,
        [low_rows, low_row_all, low_row_all, out_like((features, count), BF16), stats, wide_rows,
         statistic, low_rows, low_rows],
        [wide_scratch, values_t, query_cols, peak, peak, sums],
        20 * square, 10 << 20,
    )

    (
        layer_output, cross_keys, cross_values, cross_lse, cross_delta, unused, cross_grad, g2,
        in_grad, down_grad, cross_out_grad, feed_sums, in_bias_grad,
    ) = run(
        functools.partial(cross_and_feed, n, rows_block),
        [place_one, cross_ranges, *memory_pieces, query_segment, source_column, cotangent_rows,
         cross_query, normal, row(first_gain), row(first_shift), cross_pair_weight, cross_bias,
         cross_out_weight, row(cross_out_bias), row(second_gain), row(second_shift),
         feed_in_weight, row(feed_in_bias), feed_out_weight, row(feed_out_bias),
         row(third_gain), row(third_shift)],
        2,
        [low_rows, low_row_all, low_row_all, stats, stats, out_like((8, 128), F32), low_rows, wide_rows,
         out_like((n, hidden // n, features), BF16), out_like((n, hidden // n, features), BF16),
         out_like((n, half, features), BF16), out_like((8, features), F32), out_like((1, hidden), F32)],
        [wide_scratch, values_t, query_cols, peak, peak, sums,
         pltpu.VMEM((features, count), BF16), pltpu.VMEM((count, features), F32),
         pltpu.VMEM((count, 1), F32), pltpu.VMEM((count, features), BF16),
         pltpu.VMEM((features, count), BF16), pltpu.VMEM((count, hidden), BF16),
         pltpu.VMEM((count, hidden), F32), pltpu.VMEM((count, features), F32),
         pltpu.VMEM((count, features), BF16), pltpu.VMEM((features, count), BF16)],
        50 * square, 20 << 20,
    )

    back_scratch = [
        wide_scratch, values_t, query_cols, query_rows, query_cols, query_rows,
        pltpu.VMEM((features, count), F32), pltpu.VMEM((length, features), F32),
        pltpu.VMEM((length, features), F32), pltpu.VMEM((count, features), BF16),
    ]
    sent_like = out_like((max(n - 1, 1), count, features), BF16)
    (
        memory_own, memory_sent, cross_query_grad, cross_pair_grad, self_out_grad, self_grad,
        self_delta, g1, cross_sums,
    ) = run(
        functools.partial(cross_backward, n, rows_block),
        [place_one, cross_ranges, *memory_pieces, query_segment, source_column, cross_query,
         cross_grad, cross_keys, cross_values, cross_lse, cross_delta, g2, normal, rstd, first_low,
         row(first_gain), cross_query_weight, cross_pair_weight, self_out_weight, attended_t],
        2,
        [wide_rows, sent_like, out_like((n, half, features), BF16),
         out_like((n, 2 * half, features), BF16), out_like((n, half, features), BF16), low_rows,
         stats, wide_rows, out_like((8, features), F32)],
        back_scratch + [pltpu.VMEM((count, features), BF16)],
        30 * square, 15 << 20,
    )
    (input_own, input_sent, self_in_grad, self_sums) = run(
        functools.partial(self_backward, n, rows_block),
        [place_one, self_ranges, *input_pieces, query_segment, target_column, query, self_grad,
         keys, values, lse, self_delta, g1, self_in_weight],
        2,
        [wide_rows, sent_like, out_like((n, 3 * half, features), BF16), out_like((8, features), F32)],
        back_scratch,
        30 * square, 15 << 20,
    )

    memory_grad, input_grad = memory_own, input_own
    for step in range(1, n):
        memory_grad = memory_grad + shifted_back(memory_sent[step - 1], step).astype(F32)
        input_grad = input_grad + shifted_back(input_sent[step - 1], step).astype(F32)

    vectors = jnp.concatenate([self_sums[:2], cross_sums[:5], feed_sums[:6]], axis=0)
    count_small = vectors.shape[0]
    small = jnp.concatenate(
        [
            jnp.transpose(vectors.reshape(count_small, n, half), (1, 0, 2)).reshape(n, -1),
            in_bias_grad.reshape(n, -1),
        ],
        axis=1,
    )
    amount = small.shape[1]
    small_rows = -(-amount // (8 * WIDE)) * 8
    small = jnp.pad(small, ((0, 0), (0, small_rows * WIDE - amount))).reshape(n, small_rows, WIDE)
    parts = [in_grad, down_grad, cross_out_grad, cross_query_grad, cross_pair_grad, self_out_grad, self_in_grad]
    packed, small = reduce_all(n, groups, parts, small)
    small = small.reshape(-1)[:amount]
    plan = []
    start = 0
    shapes = []
    for part, columns in zip(parts, (hidden // features, 1, 1, 1, 2, 1, 3)):
        plan.append((start, columns))
        shapes.append(out_like((part.shape[1] // columns, columns * features), F32))
        start += part.shape[1]
    (
        feed_in_grad, feed_out_grad, cross_out_total, cross_query_total, cross_pair_total,
        self_out_total, self_in_total,
    ) = run(functools.partial(widen_kernel, plan), [packed], 0, shapes, [], 0, 12 << 20)
    rows_small = small[: count_small * half].reshape(count_small, half)
    (
        self_query_bias, self_value_bias, cross_query_bias, cross_value_bias, first_gain_grad,
        first_shift_grad, self_out_bias_grad, third_gain_grad, third_shift_grad, feed_out_bias_grad,
        second_gain_grad, second_shift_grad, cross_out_bias_grad,
    ) = [rows_small[index] for index in range(count_small)]
    return (
        layer_output[None],
        input_grad[None],
        memory_grad[None],
        self_in_total,
        jnp.stack([self_query_bias, self_value_bias]),
        self_out_total,
        self_out_bias_grad,
        first_gain_grad,
        first_shift_grad,
        cross_query_total,
        cross_pair_total,
        jnp.stack([cross_query_bias, cross_value_bias]),
        cross_out_total,
        cross_out_bias_grad,
        second_gain_grad,
        second_shift_grad,
        feed_in_grad,
        small[count_small * half :],
        feed_out_grad,
        feed_out_bias_grad,
        third_gain_grad,
        third_shift_grad,
    )


def solution(mesh):
    rows = P("dp", "blk", None)
    everywhere = P()
    split = P("blk", None)
    vector = P("blk")
    pair = P(None, "blk")
    return jax.shard_map(
        functools.partial(on_device, mesh.shape["blk"], mesh.shape["dp"]),
        mesh=mesh,
        in_specs=(rows, rows, rows, P("dp", None), P("dp", None)) + (everywhere,) * 19,
        out_specs=(
            rows, rows, rows, split, pair, split, vector, vector, vector, split, split, pair, split,
            vector, vector, vector, split, vector, split, vector, vector, vector,
        ),
        check_vma=False,
    )
```

time: 649 us -> 234 us (0.36); the launches traced: 638 us -> 235 us
  waiting for transfers between devices: 284 us -> 9.68 us
  Pallas kernels: 0 us -> 191 us
  matrix products: 169 us -> 0 us
  local copies, waits for them, and re-layouts: 63.7 us -> 9.73 us
  other arithmetic: 54.1 us -> 6.94 us
  blocking collectives: 42.9 us -> 0 us
  starting transfers between devices: 0.58 us -> 17 us
  between operations: 16.8 us -> 0.77 us
    pallas_call x0 -> x6, Pallas kernels: none -> 191 us  [the longest x5 98.3 us: run(): pl.pallas_call(body, in_specs=[sm] * smem_count + [vm] * (len(ins) - smem...]
    reduce_scatter x9 -> x0, waiting for transfers between devices: 174 us -> none  [the longest x1 34.2 us: on_device(): lax.psum_scatter(feed_out_weight_grad.astype(jnp.bfloat16), 'blk', scatte...]
    dot_general x50 -> x0, matrix products: 169 us -> none  [the longest x8 32.7 us: block_step(): jnp.einsum('qhd,khd->hqk', queries, key_block, preferred_element_type=jnp...]
    psum x1 -> x0, waiting for transfers between devices: 75.8 us -> none  [on_device(): lax.psum(shares[0].astype(jnp.bfloat16), 'dp').astype(jnp.float32)]
    psum x1 -> x0, blocking collectives: 35.9 us -> none  [on_device(): lax.psum(shares[1].astype(jnp.bfloat16), 'dp').astype(jnp.float32)]
    all_gather x2 -> x0, waiting for transfers between devices: 30.1 us -> none  [the longest x1 30.1 us: on_device(): lax.all_gather(projected[:, features:], 'blk', axis=0, tiled=True)]
    reduce_sum x18 -> x1, other arithmetic: 29.1 us -> 0.94 us  [key_ranges(): jnp.sum((key_segment[None, :] < edges[:, :1]).astype(jnp.int32), axis=1)]
    convert_element_type x20 -> x0, other arithmetic: 22.5 us -> none  [the longest x1 2.98 us: on_device(): lax.psum(shares[15].astype(jnp.bfloat16), 'dp').astype(jnp.float32)]
  transfers between devices with their start and end apart: 14 -> 4, of which waited for: 11 -> 2; matrix products, arithmetic and copies ran while one was open for 21% -> 5% of each run, Pallas kernels for 0% -> 47%
where the time goes in v1:
time: 234 us; the launch traced here: 235 us
  Pallas kernels  191 us (82%)
  starting transfers between devices  17 us (7%)
  local copies, waits for them, and re-layouts  9.73 us (4%)
  waiting for transfers between devices  9.68 us (4%)
  other arithmetic  6.94 us (3%)
    pallas_call x5, Pallas kernels, run(): pl.pallas_call(body, in_specs=[sm] * smem_count + [vm] * (len(ins) - smem...  98.3 us
    pallas_call x1, Pallas kernels, reduce_all(): pl.pallas_call(functools.partial(reduce_kernel, n, groups, chunk_rows, pa...  92.6 us
    ppermute x2, starting transfers between devices, shifted_back(): return lax.ppermute(field, 'blk', [(s, (s - step) % n) for s in range(n)])  13.9 us
    ppermute x2, waiting for transfers between devices, shifted(): return lax.ppermute(field, 'blk', [(s, (s + step) % n) for s in range(n)])  6.49 us
  transfers between devices with their start and end apart: 4, of which 2 were waited for; matrix products, arithmetic and copies ran while one was open for 5% of the time, Pallas kernels for 47%

profile of v1, /device:TPU:0, one launch (start us, length us, event | category | flops | bytes accessed | tf_op | source)
XLA Modules:
  0.0 235.0 jit_solution(12738964665717043991)
XLA Ops:
  0.7 3.0 %collective-permute-start.1 = (bf16[512,512]{1,0:T(8,128)(2,1)}, bf16[512,512]{1,0:T(8,128)(2,1)S(1)}, u32[]{:S(2)}, u32[]{:S(2)}) collective-permute-start(bf16[512,512]{1,0:T(8,128)(2,1)} %bitcast.92), channel_id=1, source_target_pairs={{0,1},{1,0},{2,3},{3,2},{4,5},{5,4},{6,7},{7,6},{8,9},{9,8},{10,11... | collective-permute-start | bytes 1572872 | tf_op jit(solution)/shard_map/ppermute | solution.py:904
  3.7 0.1 collective-permute-start
  3.7 0.7 constant_dynamic-slice_fusion.refs_2_
  4.4 0.0 copy-start.2
  4.4 0.2 slice_reduce_fusion.1
  4.6 0.9 convert_reduce_fusion.3
  5.6 0.6 pad_add_fusion.ranges_ref
  6.2 0.6 pad_add_fusion.1.ranges_ref
  6.7 1.7 copy.54.refs_3_
  8.4 1.7 copy.55.refs_3_
  10.1 6.5 %collective-permute-done.1.refs_1_ = bf16[512,512]{1,0:T(8,128)(2,1)S(1)} collective-permute-done((bf16[512,512]{1,0:T(8,128)(2,1)}, bf16[512,512]{1,0:T(8,128)(2,1)S(1)}, u32[]{:S(2)}, u32[]{:S(2)}) %collective-permute-start.1) | collective-permute-done | bytes 524320 | tf_op jit(solution)/shard_map/ppermute | solution.py:904
  16.6 0.0 copy-start.5
  16.6 0.0 copy-done.2
  16.6 0.8 copy-done.5
  17.4 11.8 %shard_map.399 = (bf16[512,512]{1,0:T(8,128)(2,1)}, bf16[1024,512]{1,0:T(8,128)(2,1)}, bf16[1024,512]{1,0:T(8,128)(2,1)}, bf16[512,512]{1,0:T(8,128)(2,1)}, f32[...) custom-call(s32[1]{0:T(128)} %bitcast.place_ref, ...), custom_call_target="tpu_custom_call" | custom-call | flops 5368709120 | bytes 10485760 | tf_op jit(solution)/shard_map/pallas_call | solution.py:210
  29.2 0.0 collective-permute-done.refs_1_
  29.2 0.0 copy-start.7
  29.2 0.8 copy-done.7
  30.0 35.9 %shard_map.400 = (bf16[512,512]{1,0:T(8,128)(2,1)}, bf16[1024,512]{1,0:T(8,128)(2,1)}, bf16[1024,512]{1,0:T(8,128)(2,1)}, f32[4,1024]{1,0:T(4,128)}, f32[4,1024]...) custom-call(s32[1]{0:T(128)} %bitcast.place_ref, ...), custom_call_target="tpu_custom_call" | custom-call | flops 13421772800 | bytes 20971520 | tf_op jit(solution)/shard_map/pallas_call | solution.py:210
  65.9 0.5 broadcast.274
  66.4 1.4 reduce.7
  67.8 27.3 %shard_map.401 = (f32[512,512]{1,0:T(8,128)}, bf16[1,512,512]{2,1,0:T(8,128)(2,1)}, bf16[2,256,512]{2,1,0:T(8,128)(2,1)}, bf16[2,512,512]{2,1,0:T(8,128)(2,1)}, ...) custom-call(s32[1]{0:T(128)} %bitcast.place_ref, ...), custom_call_target="tpu_custom_call" | custom-call | flops 8053063680 | bytes 15728640 | tf_op jit(solution)/shard_map/pallas_call | solution.py:210
  95.1 0.0 copy-start.3
  95.1 0.0 copy-start.4
  95.1 17.5 %shard_map.402 = (f32[512,512]{1,0:T(8,128)}, bf16[1,512,512]{2,1,0:T(8,128)(2,1)}, bf16[2,768,512]{2,1,0:T(8,128)(2,1)}, f32[8,512]{1,0:T(8,128)}) custom-call(s32[1]{0:T(128)} %bitcast.place_ref, s32[2,4]{1,0:T(2,128)} %pad_add_fusion.1.ranges_ref, bf16[512,512]{1,0:T(8,128)(2,1)} %bitcast.94, bf16[512,512]{1,0:T(8,128)(2,1)} %copy-done.5, ...), custom_call_target="tpu_custom_call" | custom-call | flops 8053063680 | bytes 15728640 | tf_op jit(solution)/shard_map/pallas_call | solution.py:210
  112.7 0.7 slice.99
  113.4 0.0 copy-done.3
  113.4 0.0 copy-done.4
  113.4 11.3 %collective-permute-start.2 = (bf16[512,512]{1,0:T(8,128)(2,1)}, bf16[512,512]{1,0:T(8,128)(2,1)S(1)}, u32[]{:S(2)}, u32[]{:S(2)}) collective-permute-start(bf16[512,512]{1,0:T(8,128)(2,1)} %bitcast.96), channel_id=1, source_target_pairs={{0,1},{1,0},{2,3},{3,2},{4,5},{5,4},{6,7},{7,6},{8,9},{9,8},{10,11... | collective-permute-start | bytes 1572872 | tf_op jit(solution)/shard_map/ppermute | solution.py:907
  124.8 0.6 copy.61
  125.4 0.0 copy-start.6
  125.4 92.6 %shard_map.403 = (bf16[4096,512]{1,0:T(8,128)(2,1)}, f32[16,512]{1,0:T(8,128)}) custom-call(bf16[2,1024,512]{2,1,0:T(8,128)(2,1)} %get-tuple-element.88.refs_0_, bf16[2,1024,512]{2,1,0:T(8,128)(2,1)} %get-tuple-element.89.refs_1_, bf16[2,256,512]{2,1,0:T(8,128)(2,1)} %get-tuple-element.90.refs_2_, bf16[2,256,512]{2,1,0:T(8,128)(2,1)} %get-tuple-element.91.refs_3_, ...), custom_call_target="tpu_custom_call" | custom-call | tf_op jit(solution)/shard_map/pallas_call | solution.py:841
  218.0 0.8 copy.59
  218.8 0.0 copy-done.6
  218.8 2.6 %collective-permute-start.3 = (bf16[512,512]{1,0:T(8,128)(2,1)S(1)}, bf16[512,512]{1,0:T(8,128)(2,1)S(1)}, u32[]{:S(2)}, u32[]{:S(2)}) collective-permute-start(bf16[512,512]{1,0:T(8,128)(2,1)S(1)} %bitcast.95), channel_id=1, source_target_pairs={{0,1},{1,0},{2,3},{3,2},{4,5},{5,4},{6,7},{7,6},{8,9},{9,8},{10,11... | collective-permute-start | bytes 1572872 | tf_op jit(solution)/shard_map/ppermute | solution.py:907
  221.4 0.6 fusion.1
  222.0 0.6 slice.130
  222.6 0.0 copy-start.1
  222.6 5.8 %shard_map.404 = (f32[256,2048]{1,0:T(8,128)}, f32[1024,512]{1,0:T(8,128)}, f32[256,512]{1,0:T(8,128)}, f32[256,512]{1,0:T(8,128)}, f32[256,1024]{1,0:T(8,128)},...) custom-call(bf16[4096,512]{1,0:T(8,128)(2,1)} %get-tuple-element.99.source), custom_call_target="tpu_custom_call" | custom-call | bytes 12582912 | tf_op jit(solution)/shard_map/pallas_call | solution.py:210
  228.4 0.0 copy-start
  228.4 0.6 pad_maximum_fusion.2
  228.9 0.6 pad_maximum_fusion.1
  229.5 0.0 collective-permute-done.2
  229.5 0.0 copy-done.1
  229.5 1.1 add_bitcast_fusion.1
  230.7 3.2 %collective-permute-done.3 = bf16[512,512]{1,0:T(8,128)(2,1)S(1)} collective-permute-done((bf16[512,512]{1,0:T(8,128)(2,1)S(1)}, bf16[512,512]{1,0:T(8,128)(2,1)S(1)}, u32[]{:S(2)}, u32[]{:S(2)}) %collective-permute-start.3) | collective-permute-done | bytes 524320 | tf_op jit(solution)/shard_map/ppermute | solution.py:907
  233.9 0.0 copy-done
  233.9 1.1 add_bitcast_fusion
  (6 shorter events, 0.1 us)
Async XLA Ops:
  0.7 16.0 %collective-permute-start.1 = (bf16[512,512]{1,0:T(8,128)(2,1)}, bf16[512,512]{1,0:T(8,128)(2,1)S(1)}, u32[]{:S(2)}, u32[]{:S(2)}) collective-permute-start(bf16[512,512]{1,0:T(8,128)(2,1)} %bitcast.92), channel_id=1, source_target_pairs={{0,1},{1,0},{2,3},{3,2},{4,5},{5,4},{6,7},{7,6},{8,9},{9,8},{10,11... | collective-permute-start | bytes 1572872 | tf_op jit(solution)/shard_map/ppermute | solution.py:904
  3.7 25.6 %collective-permute-start = (bf16[512,512]{1,0:T(8,128)(2,1)}, bf16[512,512]{1,0:T(8,128)(2,1)S(1)}, u32[]{:S(2)}, u32[]{:S(2)}) collective-permute-start(bf16[512,512]{1,0:T(8,128)(2,1)} %bitcast.89), channel_id=1, source_target_pairs={{0,1},{1,0},{2,3},{3,2},{4,5},{5,4},{6,7},{7,6},{8,9},{9,8},{10,11... | collective-permute-start | bytes 1572872 | tf_op jit(solution)/shard_map/ppermute | solution.py:904
  4.4 12.2 %copy-start.2 = (s32[1,512]{1,0:T(1,128)}, s32[1,512]{1,0:T(1,128)S(1)}, u32[]{:S(2)}) copy-start(s32[1,512]{1,0:T(1,128)S(1)} %constant_dynamic-slice_fusion.refs_2_) | copy-start | bytes 6148
  16.6 0.8 copy-start.5
  29.2 0.8 copy-start.7
  95.1 18.3 %copy-start.3 = (f32[8,512]{1,0:T(8,128)S(1)}, f32[8,512]{1,0:T(8,128)}, u32[]{:S(2)}) copy-start(f32[8,512]{1,0:T(8,128)} %get-tuple-element.97) | copy-start | bytes 49156
  95.1 18.3 %copy-start.4 = (f32[8,512]{1,0:T(8,128)S(1)}, f32[8,512]{1,0:T(8,128)}, u32[]{:S(2)}) copy-start(f32[8,512]{1,0:T(8,128)} %get-tuple-element.96) | copy-start | bytes 49156
  113.4 116.1 %collective-permute-start.2 = (bf16[512,512]{1,0:T(8,128)(2,1)}, bf16[512,512]{1,0:T(8,128)(2,1)S(1)}, u32[]{:S(2)}, u32[]{:S(2)}) collective-permute-start(bf16[512,512]{1,0:T(8,128)(2,1)} %bitcast.96), channel_id=1, source_target_pairs={{0,1},{1,0},{2,3},{3,2},{4,5},{5,4},{6,7},{7,6},{8,9},{9,8},{10,11... | collective-permute-start | bytes 1572872 | tf_op jit(solution)/shard_map/ppermute | solution.py:907
  125.4 93.4 %copy-start.6 = (bf16[1,512,512]{2,1,0:T(8,128)(2,1)S(1)}, bf16[1,512,512]{2,1,0:T(8,128)(2,1)}, u32[]{:S(2)}) copy-start(bf16[1,512,512]{2,1,0:T(8,128)(2,1)} %get-tuple-element.87) | copy-start | bytes 1572868
  218.8 15.0 %collective-permute-start.3 = (bf16[512,512]{1,0:T(8,128)(2,1)S(1)}, bf16[512,512]{1,0:T(8,128)(2,1)S(1)}, u32[]{:S(2)}, u32[]{:S(2)}) collective-permute-start(bf16[512,512]{1,0:T(8,128)(2,1)S(1)} %bitcast.95), channel_id=1, source_target_pairs={{0,1},{1,0},{2,3},{3,2},{4,5},{5,4},{6,7},{7,6},{8,9},{9,8},{10,11... | collective-permute-start | bytes 1572872 | tf_op jit(solution)/shard_map/ppermute | solution.py:907
  222.6 6.9 %copy-start.1 = (f32[512,512]{1,0:T(8,128)S(1)}, f32[512,512]{1,0:T(8,128)}, u32[]{:S(2)}) copy-start(f32[512,512]{1,0:T(8,128)} %get-tuple-element.84) | copy-start | bytes 3145732
  228.4 5.5 %copy-start = (f32[512,512]{1,0:T(8,128)S(1)}, f32[512,512]{1,0:T(8,128)}, u32[]{:S(2)}) copy-start(f32[512,512]{1,0:T(8,128)} %get-tuple-element.86) | copy-start | bytes 3145732

commit v2 on v1

v2 whole, which is shorter than its diff:
```python
import functools

import jax
import jax.numpy as jnp
from jax import lax
from jax.experimental import pallas as pl
from jax.experimental.pallas import tpu as pltpu
from jax.sharding import PartitionSpec as P

HEAD = 64
TILE = 128
KEYS = 256
BACK_KEYS = 256
PAIR = 2 * HEAD
WIDE = 512
SCALE = HEAD ** (-0.5)
MASKED = -1e30
F32 = jnp.float32
BF16 = jnp.bfloat16
VMEM_LIMIT = 58 << 20


def nn(left, right):
    return lax.dot_general(left, right, (((1,), (0,)), ((), ())), preferred_element_type=F32)


def nt(left, right):
    return lax.dot_general(left, right, (((1,), (1,)), ((), ())), preferred_element_type=F32)


def tn(left, right):
    return lax.dot_general(left, right, (((0,), (0,)), ((), ())), preferred_element_type=F32)


def col_sum(field):
    return jnp.sum(field, axis=0, keepdims=True)


def normalize(field):
    centre = field - jnp.mean(field, axis=-1, keepdims=True)
    spread = jnp.mean(centre * centre, axis=-1, keepdims=True)
    rstd = lax.rsqrt(spread + 1e-05)
    return centre * rstd, rstd


def normalize_back(grad, gain, normal, rstd):
    scaled = grad * gain
    mean = jnp.mean(scaled, axis=-1, keepdims=True)
    along = jnp.mean(scaled * normal, axis=-1, keepdims=True)
    return (scaled - mean - normal * along) * rstd


def gate(hidden):
    size = jnp.abs(hidden)
    bell = jnp.exp(hidden * hidden * -0.5)
    ratio = 1.0 / (1.0 + (0.3275911 * 0.7071067811865476) * size)
    series = 1.061405429 * ratio - 1.453152027
    series = series * ratio + 1.421413741
    series = series * ratio - 0.284496736
    series = series * ratio + 0.254829592
    tail = (0.5 * series) * ratio * bell
    phi = jnp.where(hidden > 0.0, 1.0 - tail, tail)
    return hidden * phi, phi + hidden * (bell * 0.3989422804014327)


def dyn(index, size):
    return pl.ds(pl.multiple_of(index * size, size), size)


def even_lanes(rows, width):
    return (lax.broadcasted_iota(jnp.int32, (rows, width), 1) // HEAD) % 2 == 0


def even_rows(rows, width):
    return (lax.broadcasted_iota(jnp.int32, (rows, width), 0) // HEAD) % 2 == 0


def split_columns(tile_t, out_ref, tile):
    chosen = even_rows(*tile_t.shape)
    blank = jnp.zeros_like(tile_t)
    out_ref[:, pl.ds(pl.multiple_of(tile * 2 * TILE, 2 * TILE), TILE)] = jnp.where(chosen, tile_t, blank)
    out_ref[:, pl.ds(pl.multiple_of(tile * 2 * TILE + TILE, TILE), TILE)] = jnp.where(
        chosen, blank, tile_t
    )


def split_rows(tile_n, out_ref, tile):
    chosen = even_lanes(*tile_n.shape)
    blank = jnp.zeros_like(tile_n)
    out_ref[pl.ds(pl.multiple_of(tile * 2 * TILE, 2 * TILE), TILE), :] = jnp.where(chosen, tile_n, blank)
    out_ref[pl.ds(pl.multiple_of(tile * 2 * TILE + TILE, TILE), TILE), :] = jnp.where(
        chosen, blank, tile_n
    )


def spread_segments(column_ref, wide_ref):
    total = column_ref.shape[0]
    step = min(total, 512)

    @pl.loop(0, total // step)
    def _(block):
        rows = dyn(block, step)
        wide_ref[rows, :] = jnp.broadcast_to(column_ref[rows, :], (step, TILE))


def key_rows(low, chunk, length, size):
    wanted = low * TILE + chunk * size
    start = pl.multiple_of(jnp.minimum(wanted, length - size), TILE)
    return pl.ds(start, size), start, wanted


def chunk_bias(query_row, key_wide_ref, tile, rows, start, wanted, offset, causal):
    size = rows.size
    key_position = start + lax.broadcasted_iota(jnp.int32, (size, TILE), 0)
    allowed = (key_wide_ref[rows, :] == query_row) & (key_position >= wanted)
    if causal:
        query_position = offset + tile * TILE + lax.broadcasted_iota(jnp.int32, (size, TILE), 1)
        allowed = allowed & (key_position <= query_position)
    return jnp.where(allowed, 0.0, MASKED)


def attend(
    tiles, ranges_ref, query_row_ref, key_wide_ref, offset, causal,
    query_cols, keys, values_t, attended_t, lse_ref, peak, total, sums, held, held_low,
):
    pairs = WIDE // PAIR

    @pl.loop(0, tiles)
    def _(tile):
        peak[...] = jnp.full(peak.shape, MASKED, F32)
        total[...] = jnp.zeros(total.shape, F32)
        sums[...] = jnp.zeros(sums.shape, F32)
        query_row = query_row_ref[:, dyn(tile, TILE)]

        low, high = ranges_ref[0, tile], ranges_ref[1, tile]

        size = held.shape[1]

        @pl.loop(0, lax.div((high - low) * TILE + size - 1, size))
        def _(chunk):
            rows, start, wanted = key_rows(low, chunk, keys.shape[0], size)
            bias = chunk_bias(query_row, key_wide_ref, tile, rows, start, wanted, offset, causal)
            bias = jnp.concatenate([bias, bias], axis=1)
            factors = []
            for pair in range(pairs):
                lanes = slice(pair * PAIR, (pair + 1) * PAIR)
                scores = nn(keys[rows, lanes], query_cols[lanes, dyn(tile, 2 * TILE)]) + bias
                held[pair] = scores
                before = peak[pair : pair + 1, :]
                after = jnp.maximum(before, jnp.max(scores, axis=0, keepdims=True))
                factors.append(jnp.exp(before - after))
                peak[pair : pair + 1, :] = after
            for pair in range(pairs):
                weights = jnp.exp(held[pair] - peak[pair : pair + 1, :])
                total[pair : pair + 1, :] = total[pair : pair + 1, :] * factors[pair] + col_sum(weights)
                held_low[pair] = weights.astype(BF16)
            for pair in range(pairs):
                factor = factors[pair]
                mixed = nn(values_t[pair * PAIR : (pair + 1) * PAIR, rows], held_low[pair])
                first = slice(pair * PAIR, pair * PAIR + HEAD)
                second = slice(pair * PAIR + HEAD, (pair + 1) * PAIR)
                sums[first, :] = sums[first, :] * factor[:, :TILE] + mixed[:HEAD, :TILE]
                sums[second, :] = sums[second, :] * factor[:, TILE:] + mixed[HEAD:, TILE:]

        for pair in range(pairs):
            amount = total[pair : pair + 1, :]
            lse_ref[pair : pair + 1, dyn(tile, 2 * TILE)] = peak[pair : pair + 1, :] + jnp.log(amount)
            share = 1.0 / amount
            first = slice(pair * PAIR, pair * PAIR + HEAD)
            second = slice(pair * PAIR + HEAD, (pair + 1) * PAIR)
            attended_t[first, dyn(tile, TILE)] = (sums[first, :] * share[:, :TILE]).astype(BF16)
            attended_t[second, dyn(tile, TILE)] = (sums[second, :] * share[:, TILE:]).astype(BF16)


def attend_back(
    tile, low, high, query_row_ref, key_wide_ref, offset, causal,
    query_cols, query_rows, grad_cols, grad_rows, keys, keys_t, values, lse_ref, delta_ref,
    query_grad_t, key_grad, value_grad, held, held_low, held_grad,
):
    pairs = WIDE // PAIR
    query_row = query_row_ref[:, dyn(tile, TILE)]
    both = dyn(tile, 2 * TILE)

    size = held.shape[1]

    @pl.loop(0, lax.div((high - low) * TILE + size - 1, size))
    def _(chunk):
        rows, start, wanted = key_rows(low, chunk, keys.shape[0], size)
        bias = chunk_bias(query_row, key_wide_ref, tile, rows, start, wanted, offset, causal)
        bias = jnp.concatenate([bias, bias], axis=1)
        for pair in range(pairs):
            lanes = slice(pair * PAIR, (pair + 1) * PAIR)
            scores = nn(keys[rows, lanes], query_cols[lanes, both]) + bias
            probs = jnp.exp(scores - lse_ref[pair : pair + 1, both])
            held[pair] = probs
            held_low[pair] = probs.astype(BF16)
        for pair in range(pairs):
            lanes = slice(pair * PAIR, (pair + 1) * PAIR)
            prob_grad = nn(values[rows, lanes], grad_cols[lanes, both])
            held_grad[pair] = (held[pair] * (prob_grad - delta_ref[pair : pair + 1, both])).astype(BF16)
        for pair in range(pairs):
            lanes = slice(pair * PAIR, (pair + 1) * PAIR)
            value_grad[rows, lanes] += nn(held_low[pair], grad_rows[both, lanes])
            key_grad[rows, lanes] += nn(held_grad[pair], query_rows[both, lanes])
            mixed = nn(keys_t[lanes, rows], held_grad[pair])
            first = slice(pair * PAIR, pair * PAIR + HEAD)
            second = slice(pair * PAIR + HEAD, (pair + 1) * PAIR)
            query_grad_t[first, dyn(tile, TILE)] += mixed[:HEAD, :TILE]
            query_grad_t[second, dyn(tile, TILE)] += mixed[HEAD:, TILE:]


def clear(ref):
    rows = ref.shape[0]
    step = min(rows, 256)

    @pl.loop(0, rows // step)
    def _(block):
        ref[dyn(block, step), :] = jnp.zeros((step, ref.shape[1]), ref.dtype)


def transpose_rows(source, target):
    @pl.loop(0, source.shape[0] // TILE)
    def _(block):
        target[:, dyn(block, TILE)] = source[dyn(block, TILE), :].T


def out_like(shape, dtype):
    return jax.ShapeDtypeStruct(shape, dtype)


def run(body, ins, smem_count, outs, scratch, flops, bytes_accessed):
    vm = pl.BlockSpec(memory_space=pltpu.VMEM)
    sm = pl.BlockSpec(memory_space=pltpu.SMEM)
    return pl.pallas_call(
        body,
        in_specs=[sm] * smem_count + [vm] * (len(ins) - smem_count),
        out_specs=[vm] * len(outs),
        out_shape=outs,
        scratch_shapes=scratch,
        cost_estimate=pl.CostEstimate(
            flops=flops, bytes_accessed=bytes_accessed, transcendentals=0
        ),
        compiler_params=pltpu.CompilerParams(vmem_limit_bytes=VMEM_LIMIT),
    )(*ins)


def self_forward(n, rows_block, place_ref, ranges_ref, *refs):
    pieces, refs = refs[:n], refs[n:]
    (
        query_segment, key_segment, weight, bias, out_weight, out_bias, gain, shift,
        cross_weight, cross_bias,
        query_out, keys, values, attended_t, lse_ref, normal_out, rstd_out, first_low, cross_query,
        wide, values_t, query_cols, peak, total, sums, held, held_low,
    ) = refs
    count = pieces[0].shape[0]
    place = place_ref[0]
    spread_segments(key_segment, wide)

    for step in range(n):
        spot = lax.rem(place + n - step, n)

        @pl.when(spot <= place)
        def _():
            @pl.loop(0, count // rows_block)
            def _(block):
                source = pieces[step][dyn(block, rows_block), :]
                rows = dyn(spot * (count // rows_block) + block, rows_block)
                keys[rows, :] = nn(source, weight[:, WIDE : 2 * WIDE]).astype(BF16)
                values[rows, :] = (nn(source, weight[:, 2 * WIDE :]) + bias[1:2, :]).astype(BF16)
                if step == 0:
                    query = (nn(source, weight[:, :WIDE]) + bias[0:1, :]).astype(BF16)
                    query_out[dyn(block, rows_block), :] = (query.astype(F32) * SCALE).astype(BF16)

        @pl.when(spot > place)
        def _():
            @pl.loop(0, count // rows_block)
            def _(block):
                rows = dyn(spot * (count // rows_block) + block, rows_block)
                keys[rows, :] = jnp.zeros((rows_block, WIDE), BF16)
                values[rows, :] = jnp.zeros((rows_block, WIDE), BF16)

    transpose_rows(values, values_t)
    tiles = count // TILE

    @pl.loop(0, tiles)
    def _(tile):
        split_columns(query_out[dyn(tile, TILE), :].T, query_cols, tile)

    attend(
        tiles, ranges_ref, query_segment, wide, place * count, True,
        query_cols, keys, values_t, attended_t, lse_ref, peak, total, sums, held, held_low,
    )

    @pl.loop(0, count // rows_block)
    def _(block):
        rows = dyn(block, rows_block)
        attended = attended_t[:, rows].T
        field = pieces[0][rows, :].astype(F32) + nn(attended, out_weight[...]) + out_bias[...]
        normal, rstd = normalize(field)
        normal_out[rows, :] = normal
        rstd_out[rows, :] = rstd
        low = (normal * gain[...] + shift[...]).astype(BF16)
        first_low[rows, :] = low
        query = (nn(low, cross_weight[...]) + cross_bias[0:1, :]).astype(BF16)
        cross_query[rows, :] = (query.astype(F32) * SCALE).astype(BF16)


def cross_and_feed(n, rows_block, place_ref, ranges_ref, *refs):
    pieces, refs = refs[:n], refs[n:]
    (
        query_segment, key_segment, cotangent, cross_query, first_normal, first_gain, first_shift,
        pair_weight, cross_bias, out_weight, out_bias, gain, shift,
        in_weight, in_bias, down_weight, down_bias, last_gain, last_shift,
        layer_output, keys, values, lse_ref, delta_ref, out_grad, grad_out, g2_out,
        in_grad, down_grad, cross_out_grad, sums_out, in_bias_grad,
        wide, values_t, query_cols, peak, total, sums, held, held_low, attended_t, second_normal, second_rstd,
        second_low, second_low_t, active, slope, third, branch, branch_t,
    ) = refs
    count = pieces[0].shape[0]
    place = place_ref[0]
    spread_segments(key_segment, wide)
    blocks = count // rows_block

    for step in range(n):
        spot = lax.rem(place + n - step, n)

        @pl.loop(0, blocks)
        def _(block):
            source = pieces[step][dyn(block, rows_block), :]
            rows = dyn(spot * blocks + block, rows_block)
            keys[rows, :] = nn(source, pair_weight[:, :WIDE]).astype(BF16)
            values[rows, :] = (nn(source, pair_weight[:, WIDE:]) + cross_bias[1:2, :]).astype(BF16)

    transpose_rows(values, values_t)
    tiles = count // TILE

    @pl.loop(0, tiles)
    def _(tile):
        split_columns(cross_query[dyn(tile, TILE), :].T, query_cols, tile)

    attend(
        tiles, ranges_ref, query_segment, wide, 0, False,
        query_cols, keys, values_t, attended_t, lse_ref, peak, total, sums, held, held_low,
    )

    @pl.loop(0, blocks)
    def _(block):
        rows = dyn(block, rows_block)
        attended = attended_t[:, rows].T
        first = first_normal[rows, :] * first_gain[...] + first_shift[...]
        field = first + nn(attended, out_weight[...]) + out_bias[...]
        normal, rstd = normalize(field)
        second_normal[rows, :] = normal
        second_rstd[rows, :] = rstd
        second = normal * gain[...] + shift[...]
        third[rows, :] = second + down_bias[...]
        low = second.astype(BF16)
        second_low[rows, :] = low
        second_low_t[:, rows] = low.T

    hidden_size = in_weight.shape[1]
    chunk_size = min(WIDE, hidden_size // n)
    chunks = hidden_size // chunk_size

    @pl.loop(0, chunks)
    def _(chunk):
        lanes = dyn(chunk, chunk_size)

        @pl.loop(0, blocks)
        def _(block):
            rows = dyn(block, rows_block)
            hidden = nn(second_low[rows, :], in_weight[:, lanes]) + in_bias[:, lanes]
            value, derivative = gate(hidden)
            value = value.astype(BF16)
            active[rows, lanes] = value
            slope[rows, lanes] = derivative.astype(slope.dtype)
            third[rows, :] += nn(value, down_weight[dyn(chunk, chunk_size), :])

    sums_out[...] = jnp.zeros(sums_out.shape, F32)
    in_bias_grad[...] = jnp.zeros(in_bias_grad.shape, F32)

    @pl.loop(0, blocks)
    def _(block):
        rows = dyn(block, rows_block)
        normal, rstd = normalize(third[rows, :])
        layer_output[rows, :] = (normal * last_gain[...] + last_shift[...]).astype(BF16)
        outer = cotangent[rows, :].astype(F32)
        grad = normalize_back(outer, last_gain[...], normal, rstd)
        third[rows, :] = grad
        low = grad.astype(BF16)
        branch[rows, :] = low
        sums_out[0:1, :] += col_sum(outer * normal)
        sums_out[1:2, :] += col_sum(outer)
        sums_out[2:3, :] += col_sum(low.astype(F32))

    half = WIDE // n
    down_half = down_weight.shape[0] // n

    @pl.loop(0, chunks)
    def _(chunk):
        lanes = dyn(chunk, chunk_size)
        share = tn(active[:, lanes], branch[...]).astype(BF16)
        per_half = down_half // chunk_size
        down_grad[lax.div(chunk, per_half), dyn(lax.rem(chunk, per_half), chunk_size), :] = share

        @pl.loop(0, blocks)
        def _(block):
            rows = dyn(block, rows_block)
            inner = nt(branch[rows, :], down_weight[dyn(chunk, chunk_size), :])
            hidden_grad = (inner * slope[rows, lanes].astype(F32)).astype(BF16)
            active[rows, lanes] = hidden_grad
            in_bias_grad[:, lanes] += col_sum(hidden_grad.astype(F32))
            third[rows, :] += nt(hidden_grad, in_weight[:, lanes])

        share = nn(second_low_t[...], active[:, lanes]).astype(BF16)
        per_block = WIDE // chunk_size
        block_rows = dyn(lax.div(chunk, per_block), half)
        block_lanes = dyn(lax.rem(chunk, per_block), chunk_size)
        for part in range(n):
            in_grad[part, block_rows, block_lanes] = share[part * half : (part + 1) * half, :]

    @pl.loop(0, blocks)
    def _(block):
        rows = dyn(block, rows_block)
        outer = third[rows, :]
        normal = second_normal[rows, :]
        grad = normalize_back(outer, gain[...], normal, second_rstd[rows, :])
        g2_out[rows, :] = grad
        low = grad.astype(BF16)
        branch[rows, :] = low
        sums_out[3:4, :] += col_sum(outer * normal)
        sums_out[4:5, :] += col_sum(outer)
        sums_out[5:6, :] += col_sum(low.astype(F32))
        grad_out[rows, :] = nt(low, out_weight[...]).astype(BF16)

    share = nn(attended_t[...], branch[...]).astype(BF16)
    for part in range(n):
        cross_out_grad[part] = share[part * half : (part + 1) * half, :]

    write_delta(tiles, grad_out, attended_t, delta_ref)


def write_delta(tiles, grad, attended_t, delta_ref):
    @pl.loop(0, tiles)
    def _(tile):
        product = grad[dyn(tile, TILE), :].astype(F32).T * attended_t[:, dyn(tile, TILE)].astype(F32)
        for pair in range(WIDE // PAIR):
            start = pair * PAIR
            delta_ref[pair : pair + 1, pl.ds(pl.multiple_of(tile * 2 * TILE, 2 * TILE), TILE)] = col_sum(
                product[start : start + HEAD, :]
            )
            delta_ref[
                pair : pair + 1, pl.ds(pl.multiple_of(tile * 2 * TILE + TILE, TILE), TILE)
            ] = col_sum(product[start + HEAD : start + PAIR, :])


def prepare_back(tiles, query, grad, query_cols, query_rows, grad_cols, grad_rows):
    @pl.loop(0, tiles)
    def _(tile):
        here = query[dyn(tile, TILE), :]
        split_columns(here.T, query_cols, tile)
        split_rows(here, query_rows, tile)
        here = grad[dyn(tile, TILE), :]
        split_columns(here.T, grad_cols, tile)
        split_rows(here, grad_rows, tile)


def query_finish(tiles, query_grad_t, query_low, sums_out, index, rounded):
    @pl.loop(0, tiles)
    def _(tile):
        rows = dyn(tile, TILE)
        wide_grad = query_grad_t[:, rows].T * SCALE
        low = wide_grad.astype(BF16)
        query_low[rows, :] = low
        sums_out[index : index + 1, :] += col_sum(low.astype(F32) if rounded else wide_grad)


def spread_parts(n, share, target, start):
    half = WIDE // n
    for part in range(n):
        target[part, start : start + half, :] = share[part * half : (part + 1) * half, :].astype(BF16)


def row_product(n, place, pieces, source):
    count = pieces[0].shape[0]
    step_rows = min(count, 512)
    share = jnp.zeros((WIDE, WIDE), F32)
    for step in range(n):
        spot = lax.rem(place + n - step, n)
        for block in range(count // step_rows):
            rows = dyn(spot * (count // step_rows) + block, step_rows)
            share += tn(
                pieces[step][block * step_rows : (block + 1) * step_rows, :], source[rows, :].astype(BF16)
            )
    return share


def pair_back(n, place, rows_block, count, step, key_grad, value_grad, weight, first, sums_out, index, write):
    blocks = count // rows_block
    spot = lax.rem(place + n - step, n)

    @pl.loop(0, blocks)
    def _(block):
        rows = dyn(spot * blocks + block, rows_block)
        key_low = key_grad[rows, :].astype(BF16)
        value_part = value_grad[rows, :]
        sums_out[index : index + 1, :] += col_sum(value_part)
        value_low = value_part.astype(BF16)
        back = nt(key_low, weight[:, first : first + WIDE]) + nt(value_low, weight[:, first + WIDE : first + 2 * WIDE])
        write(dyn(block, rows_block), back)


def first_back(
    blocks, rows_block, g2, query_low, query_weight, first_normal, first_rstd, gain, self_out_weight,
    g1, branch, self_grad, sums_out, index,
):
    @pl.loop(0, blocks)
    def _(block):
        rows = dyn(block, rows_block)
        outer = g2[rows, :] + nt(query_low[rows, :], query_weight[...])
        normal = first_normal[rows, :]
        back = normalize_back(outer, gain[...], normal, first_rstd[rows, :])
        g1[rows, :] = back
        low = back.astype(BF16)
        branch[rows, :] = low
        sums_out[index : index + 1, :] += col_sum(outer * normal)
        sums_out[index + 1 : index + 2, :] += col_sum(outer)
        sums_out[index + 2 : index + 3, :] += col_sum(low.astype(F32))
        self_grad[rows, :] = nt(low, self_out_weight[...]).astype(BF16)


def cross_backward(n, rows_block, place_ref, ranges_ref, *refs):
    pieces, refs = refs[:n], refs[n:]
    (
        query_segment, key_segment, query, grad, keys, values, lse_ref, delta_ref, g2,
        first_normal, first_rstd, first_low, gain, query_weight, pair_weight, self_out_weight,
        self_attended_t,
        own_grad, sent_grad, query_grad_w, pair_grad_w, self_out_grad, self_grad, self_delta, g1_out, sums_out,
        wide, keys_t, query_cols, query_rows, grad_cols, grad_rows, query_grad_t, key_grad, value_grad,
        held, held_low, held_grad, query_low, branch,
    ) = refs
    count = pieces[0].shape[0]
    place = place_ref[0]
    tiles = count // TILE
    blocks = count // rows_block
    half = WIDE // n
    spread_segments(key_segment, wide)
    transpose_rows(keys, keys_t)
    prepare_back(tiles, query, grad, query_cols, query_rows, grad_cols, grad_rows)
    clear(query_grad_t)
    clear(key_grad)
    clear(value_grad)

    @pl.loop(0, tiles)
    def _(tile):
        attend_back(
            tile, ranges_ref[0, tile], ranges_ref[1, tile], query_segment, wide, 0, False,
            query_cols, query_rows, grad_cols, grad_rows, keys, keys_t, values, lse_ref, delta_ref,
            query_grad_t, key_grad, value_grad, held, held_low, held_grad,
        )

    sums_out[...] = jnp.zeros(sums_out.shape, F32)
    query_finish(tiles, query_grad_t, query_low, sums_out, 0, True)
    spread_parts(n, tn(first_low[...], query_low[...]), query_grad_w, 0)
    for step in range(n):

        def write(here, back):
            if step == 0:
                own_grad[here, :] = back
            else:
                sent_grad[step - 1, here, :] = back.astype(BF16)

        pair_back(n, place, rows_block, count, step, key_grad, value_grad, pair_weight, 0, sums_out, 1, write)
    spread_parts(n, row_product(n, place, pieces, key_grad), pair_grad_w, 0)
    spread_parts(n, row_product(n, place, pieces, value_grad), pair_grad_w, half)
    first_back(
        blocks, rows_block, g2, query_low, query_weight, first_normal, first_rstd, gain, self_out_weight,
        g1_out, branch, self_grad, sums_out, 2,
    )
    spread_parts(n, nn(self_attended_t[...], branch[...]), self_out_grad, 0)
    write_delta(tiles, self_grad, self_attended_t, self_delta)


def self_backward(n, rows_block, place_ref, ranges_ref, *refs):
    pieces, refs = refs[:n], refs[n:]
    (
        query_segment, key_segment, query, grad, keys, values, lse_ref, delta_ref, g1, weight,
        own_grad, sent_grad, grad_w, sums_out,
        wide, keys_t, query_cols, query_rows, grad_cols, grad_rows, query_grad_t, key_grad, value_grad,
        held, held_low, held_grad, query_low,
    ) = refs
    count = pieces[0].shape[0]
    place = place_ref[0]
    tiles = count // TILE
    half = WIDE // n
    spread_segments(key_segment, wide)
    transpose_rows(keys, keys_t)
    prepare_back(tiles, query, grad, query_cols, query_rows, grad_cols, grad_rows)
    clear(query_grad_t)
    clear(key_grad)
    clear(value_grad)

    @pl.loop(0, tiles)
    def _(tile):
        attend_back(
            tile, ranges_ref[0, tile], ranges_ref[1, tile], query_segment, wide, place * count, True,
            query_cols, query_rows, grad_cols, grad_rows, keys, keys_t, values, lse_ref, delta_ref,
            query_grad_t, key_grad, value_grad, held, held_low, held_grad,
        )

    sums_out[...] = jnp.zeros(sums_out.shape, F32)
    query_finish(tiles, query_grad_t, query_low, sums_out, 0, False)
    for step in range(n):

        def write(here, back):
            if step == 0:
                own_grad[here, :] = back + g1[here, :] + nt(query_low[here, :], weight[:, :WIDE])
            else:
                sent_grad[step - 1, here, :] = back.astype(BF16)

        pair_back(n, place, rows_block, count, step, key_grad, value_grad, weight, WIDE, sums_out, 1, write)
    spread_parts(n, tn(pieces[0][...], query_low[...]), grad_w, 0)
    spread_parts(n, row_product(n, place, pieces, key_grad), grad_w, half)
    spread_parts(n, row_product(n, place, pieces, value_grad), grad_w, 2 * half)


CORE_RATE = 0.0018
LINK_RATE = 0.0225
LATENCY = {"core": 1.1, "x": 2.4, "y": 2.4, "z": 3.0}
MARGIN = 1.0


def plan_steps(n, chunks, extras, segments):
    free = {"core": 0.0, "x": 0.0, "y": 0.0, "z": 0.0}
    now = 0.0
    pending = []
    plan = []

    def send(link, rows, rate=LINK_RATE):
        free[link] = max(free[link], now) + rows * rate
        return free[link] + LATENCY[link]

    def execute(kind, index, step):
        nonlocal now
        now += 0.15
        if kind == "chunk":
            unused, rows, y_first, unused = chunks[index]
            if step == 0:
                ready = send("core", n * rows // 2, CORE_RATE)
            elif step in (1, 2) and (step == 1) == y_first:
                ready = send("y", (n if y_first else 1) * rows // 4)
            elif step in (1, 2):
                ready = send("x", (n - 1) * rows // (4 if y_first else 2))
            elif step in (3, 4):
                ready = send("z", rows // 4)
            elif step == 5:
                ready = send("y", rows // 4)
            elif step == 6:
                ready = send("core", rows // 2, CORE_RATE)
            else:
                return
        elif kind == "extra":
            if step == 1:
                return
            ready = send("x", extras[index][0])
        else:
            if step == 4:
                return
            ready = now + (1.5, 3.2, 3.2, 4.0)[step]
        pending.append((ready, len(pending), kind, index, step + 1))

    for number in range(len(segments) + 1):
        order = []
        last = number == len(segments)
        if not last:
            now += segments[number]
            released = [("chunk", i) for i, chunk in enumerate(chunks) if chunk[3] == number]
            released += [("extra", i) for i, extra in enumerate(extras) if extra[1] == number]
            if number == len(segments) - 1:
                released.append(("small", 0))
            for kind, index in released:
                execute(kind, index, 0)
                order.append((kind, index, 0))
        while pending:
            pending.sort()
            if not last and pending[0][0] + MARGIN > now:
                break
            ready, unused, kind, index, step = pending.pop(0)
            now = max(now, ready)
            execute(kind, index, step)
            order.append((kind, index, step))
        plan.append(order)
    return plan, now


class Reducer:
    def __init__(self, n, groups, chunks, field, total, total_out, small, small_out, buffers):
        (
            self.from_core, self.from_blk, self.from_y, self.from_z,
            self.small_core, self.small_blk, self.small_y, self.small_z,
            self.sends, self.receives, self.small_sends, self.small_receives, self.stores,
        ) = buffers
        self.n, self.chunks, self.field, self.total, self.total_out = n, chunks, field, total, total_out
        self.small, self.small_out = small, small_out
        self.depth = depth = groups // 4
        self.group = group = lax.axis_index("dp")
        self.part = part = lax.axis_index("blk")
        self.core = lax.rem(group, 2)
        self.side = lax.rem(lax.div(group, 2), 2)
        self.level = lax.div(group, 4)
        self.core_peer = (group + 1 - 2 * self.core, part)
        self.side_peer = (group + 2 - 4 * self.side, part)
        self.blk_peers = [(group, lax.rem(part + step, n)) for step in range(1, n)]
        self.z_peers = [(lax.rem(group + 4 * step, groups), part) for step in range(1, depth)]
        self.per_chunk = 4 + (n - 1) + 2 * (depth - 1)

    def enter(self):
        peers = [self.core_peer, self.side_peer] + self.blk_peers + self.z_peers
        barrier = pltpu.get_barrier_semaphore()
        for peer in peers:
            pl.semaphore_signal(barrier, inc=1, device_id=peer, device_id_type=pl.DeviceIdType.MESH)
        pl.semaphore_wait(barrier, len(peers))

    def copy(self, source, target, sem, peer):
        return pltpu.make_async_remote_copy(
            src_ref=source, dst_ref=target, send_sem=self.sends.at[sem], recv_sem=self.receives.at[sem],
            device_id=peer, device_id_type=pl.DeviceIdType.MESH,
        )

    def small_copy(self, source, target, sem, peer):
        return pltpu.make_async_remote_copy(
            src_ref=source, dst_ref=target, send_sem=self.small_sends.at[sem],
            recv_sem=self.small_receives.at[sem], device_id=peer, device_id_type=pl.DeviceIdType.MESH,
        )

    def span(self, start, size):
        return pl.ds(pl.multiple_of(start, 16), size)

    def copies(self, index, step):
        start, rows, y_first, unused = self.chunks[index]
        n, depth, part = self.n, self.depth, self.part
        half, quarter = rows // 2, rows // 4
        piece = quarter // depth
        own_half = start + self.core * half
        own_quarter = own_half + self.side * quarter
        sem = index * self.per_chunk
        if step == 0:
            theirs = self.span(start + (1 - self.core) * half, half)
            return [
                self.copy(
                    self.field.at[:, theirs], self.from_core.at[:, pl.ds(start // 2, half)], sem, self.core_peer
                )
            ]
        if step in (1, 2) and (step == 1) == y_first:
            theirs = self.span(own_half + (1 - self.side) * quarter, quarter)
            into = pl.ds(start // 4, quarter)
            if y_first:
                return [self.copy(self.field.at[:, theirs], self.from_y.at[:, into], sem + 1, self.side_peer)]
            return [self.copy(self.field.at[part, theirs], self.from_y.at[0, into], sem + 1, self.side_peer)]
        if step in (1, 2):
            if y_first:
                mine, into = self.span(own_quarter, quarter), pl.ds(start // 2, quarter)
            else:
                mine, into = self.span(own_half, half), pl.ds(start // 2, half)
            return [
                self.copy(
                    self.field.at[lax.rem(part + hop, n), mine], self.from_blk.at[hop - 1, into],
                    sem + 3 + hop, self.blk_peers[hop - 1],
                )
                for hop in range(1, n)
            ]
        if step == 3:
            copies = []
            for hop in range(1, depth):
                theirs = self.span(own_quarter + lax.rem(self.level + hop, depth) * piece, piece)
                copies.append(
                    self.copy(
                        self.field.at[part, theirs], self.from_z.at[hop - 1, pl.ds(start // 4 // depth, piece)],
                        sem + 2 + n + hop, self.z_peers[hop - 1],
                    )
                )
            return copies
        if step == 4:
            mine = self.span(own_quarter + self.level * piece, piece)
            return [
                self.copy(
                    self.total.at[mine], self.total.at[mine], sem + 1 + n + depth + hop, self.z_peers[hop - 1]
                )
                for hop in range(1, depth)
            ]
        if step == 5:
            mine = self.span(own_quarter, quarter)
            return [self.copy(self.total.at[mine], self.total.at[mine], sem + 2, self.side_peer)]
        mine = self.span(own_half, half)
        return [self.copy(self.total.at[mine], self.total.at[mine], sem + 3, self.core_peer)]

    def add(self, part, start, size, terms, result=None):
        step = min(size, 64)

        @pl.loop(0, size // step)
        def _(block):
            here = self.span(start + block * step, step)
            value = self.field[part, here, :].astype(F32)
            for ref, index, begin in terms:
                value = value + ref[index, self.span(begin + block * step, step), :].astype(F32)
            if result is None:
                self.field[part, here, :] = value.astype(BF16)
            else:
                result[here, :] = value.astype(BF16)

    def store(self, index):
        rows = pl.ds(self.chunks[index][0], self.chunks[index][1])
        return pltpu.make_async_copy(self.total.at[rows], self.total_out.at[rows], self.stores.at[index])

    def chunk_step(self, index, step):
        start, rows, y_first, unused = self.chunks[index]
        n, depth, part = self.n, self.depth, self.part
        half, quarter = rows // 2, rows // 4
        piece = quarter // depth
        own_half = start + self.core * half
        own_quarter = own_half + self.side * quarter
        if step > 0:
            for copy in self.copies(index, step - 1):
                copy.wait()
        if step == 1:
            for b in range(n):
                self.add(b, own_half, half, [(self.from_core, b, start // 2)])
        elif step in (2, 3) and (step == 2) == y_first:
            for b in range(n) if y_first else [part]:
                self.add(b, own_quarter, quarter, [(self.from_y, b if y_first else 0, start // 4)])
        elif step in (2, 3):
            begin, size = (own_quarter, quarter) if y_first else (own_half, half)
            self.add(part, begin, size, [(self.from_blk, hop, start // 2) for hop in range(n - 1)])
        elif step == 4:
            self.add(
                part, own_quarter + self.level * piece, piece,
                [(self.from_z, hop, start // 4 // depth) for hop in range(depth - 1)], self.total,
            )
        if step < 7:
            for copy in self.copies(index, step):
                copy.start()
        else:
            self.store(index).start()

    def small_copies(self, step):
        part, n = self.part, self.n
        if step == 0:
            return [self.small_copy(self.small.at[0], self.small_core, 0, self.core_peer)]
        if step == 1:
            return [
                self.small_copy(
                    self.small.at[1, lax.rem(part + hop, n)], self.small_blk.at[hop - 1], hop,
                    self.blk_peers[hop - 1],
                )
                for hop in range(1, n)
            ]
        if step == 2:
            return [self.small_copy(self.small.at[1, part], self.small_y, n, self.side_peer)]
        return [
            self.small_copy(self.small_y, self.small_z.at[hop - 1], n + hop, self.z_peers[hop - 1])
            for hop in range(1, self.depth)
        ]

    def small_step(self, step):
        part = self.part
        if step > 0:
            for copy in self.small_copies(step - 1):
                copy.wait()
        if step == 1:
            self.small[1] = self.small[0] + self.small_core[...]
        elif step == 2:
            held = self.small[1, part]
            for hop in range(self.n - 1):
                held = held + self.small_blk[hop]
            self.small[1, part] = held
        elif step == 3:
            self.small_y[...] = self.small_y[...] + self.small[1, part]
        elif step == 4:
            held = self.small_y[...]
            for hop in range(self.depth - 1):
                held = held + self.small_z[hop]
            self.small_out[...] = held
        if step < 4:
            for copy in self.small_copies(step):
                copy.start()

    def finish(self):
        for index in range(len(self.chunks)):
            self.store(index).wait()


def reducer_scratch(n, groups, chunks, rows, small_shape):
    depth = groups // 4
    per_chunk = 4 + (n - 1) + 2 * (depth - 1)
    return [
        pltpu.VMEM((n, rows // 2, WIDE), BF16),
        pltpu.VMEM((n - 1, rows // 2, WIDE), BF16),
        pltpu.VMEM((n, rows // 4, WIDE), BF16),
        pltpu.VMEM((depth - 1, rows // 4 // depth, WIDE), BF16),
        pltpu.VMEM((n, *small_shape), F32),
        pltpu.VMEM((n - 1, *small_shape), F32),
        pltpu.VMEM(small_shape, F32),
        pltpu.VMEM((depth - 1, *small_shape), F32),
        pltpu.SemaphoreType.DMA((len(chunks) * per_chunk,)),
        pltpu.SemaphoreType.DMA((len(chunks) * per_chunk,)),
        pltpu.SemaphoreType.DMA((n + depth,)),
        pltpu.SemaphoreType.DMA((n + depth,)),
        pltpu.SemaphoreType.DMA((len(chunks),)),
    ]


def reduce_kernel(n, groups, chunks, plan, part_rows, *refs):
    sources, refs = refs[: len(part_rows)], refs[len(part_rows) :]
    small_in, total_out, small_out, field, total, small, load_sem = refs[:7]
    loads = []
    start = 0
    for index, source in enumerate(sources):
        loads.append(
            pltpu.make_async_copy(source, field.at[:, pl.ds(start, part_rows[index])], load_sem.at[index])
        )
        loads[-1].start()
        start += part_rows[index]
    reducer = Reducer(n, groups, chunks, field, total, total_out, small, small_out, refs[7:])
    small[0] = small_in[...]
    reducer.enter()
    for load in loads:
        load.wait()
    for order in plan:
        for kind, index, step in order:
            if kind == "chunk":
                reducer.chunk_step(index, step)
            else:
                reducer.small_step(step)
    reducer.finish()


def reduce_all(n, groups, parts, small):
    part_rows = [part.shape[1] for part in parts]
    rows = sum(part_rows)
    chunk_rows = max(16 * groups, rows // 8)
    chunks = [(start, chunk_rows, False, 0) for start in range(0, rows, chunk_rows)]
    plan, unused = plan_steps(n, chunks, [], [0.0])
    small_shape = small.shape[1:]
    vm = pl.BlockSpec(memory_space=pltpu.VMEM)
    hbm = pl.BlockSpec(memory_space=pl.ANY)
    return pl.pallas_call(
        functools.partial(reduce_kernel, n, groups, chunks, plan, part_rows),
        in_specs=[hbm] * len(parts) + [vm],
        out_specs=[hbm, vm],
        out_shape=[out_like((rows, WIDE), BF16), out_like(small_shape, F32)],
        scratch_shapes=[
            pltpu.VMEM((n, rows, WIDE), BF16),
            pltpu.VMEM((rows, WIDE), BF16),
            pltpu.VMEM((2, n, *small_shape), F32),
            pltpu.SemaphoreType.DMA((len(parts),)),
            *reducer_scratch(n, groups, chunks, rows, small_shape),
        ],
        compiler_params=pltpu.CompilerParams(
            vmem_limit_bytes=VMEM_LIMIT, collective_id=0, has_side_effects=True
        ),
    )(*parts, small)


Y_FIRST = [letter == "y" for letter in "yyxyxyxyxxyy"]
BACK_SEGMENTS = [
    3.5, 3.2, 3.2, 3.2, 3.2, 1.5, 3.0, 3.5, 2.2,
    2.5, 2.6, 2.6, 3.2, 3.2, 1.5, 1.2, 1.2, 2.4,
]


def back_chunks(half, hidden_rows):
    released = [(2 * half, 0)] * (hidden_rows // half) + [(half, 0)]
    released += [(half, segment) for segment in (5, 6, 6, 7, 14, 15, 16)]
    chunks = []
    start = 0
    for index, (rows, segment) in enumerate(released):
        chunks.append((start, rows, Y_FIRST[index % len(Y_FIRST)], segment))
        start += rows
    return chunks


def back_kernel(n, groups, rows_block, chunks, plan, load_plan, *refs):
    feed_refs, refs = refs[:3], refs[3:]
    streamed, refs = refs[: len(load_plan)], refs[len(load_plan) :]
    (
        query_segment, memory_segment, target_segment, cross_query, cross_grad, cross_keys, cross_values,
        cross_lse, cross_delta, feed_sums, in_bias_grad, gain, first_rstd, self_lse,
        total_out, small_out, memory_grad, input_grad,
        field, total, small, sums, memory_sent, memory_got, input_sent, input_got,
        wide, keys_t, query_cols, query_rows, grad_cols, grad_rows, query_grad_t, key_grad, value_grad,
        held, held_low, held_grad, query_low, branch, self_grad, self_delta, g1,
        feed_sem, load_sem, extra_send, extra_recv,
    ) = refs[:47]
    refs = refs[47:]
    held_loads, buffers = refs[: len(load_plan)], refs[len(load_plan) :]
    count = cross_query.shape[0]
    length = cross_keys.shape[0]
    tiles = count // TILE
    blocks = count // rows_block
    half = WIDE // n
    place = lax.axis_index("blk")

    feed_loads = []
    start = 0
    for index, source in enumerate(feed_refs):
        rows = source.shape[1]
        feed_loads.append(
            pltpu.make_async_copy(source, field.at[:, pl.ds(start, rows)], feed_sem.at[index])
        )
        feed_loads[-1].start()
        start += rows
    loads = [
        pltpu.make_async_copy(source, target, load_sem.at[index])
        for index, (source, target) in enumerate(zip(streamed, held_loads))
    ]
    for load in loads:
        load.start()
    memory_pieces, held_loads = held_loads[:n], held_loads[n:]
    (
        pair_weight, first_low, query_weight, g2, first_normal, self_out_weight, self_attended_t,
        self_keys, self_values, self_query,
    ) = held_loads[:10]
    input_pieces, (self_in_weight,) = held_loads[10 : 10 + n], held_loads[10 + n :]

    reducer = Reducer(n, groups, chunks, field, total, total_out, small, small_out, buffers)
    reducer.enter()

    def extra_copies(index):
        sent, got = ((memory_sent, memory_got), (input_sent, input_got))[index]
        return [
            pltpu.make_async_remote_copy(
                src_ref=sent.at[step - 1], dst_ref=got.at[step - 1],
                send_sem=extra_send.at[index * (n - 1) + step - 1],
                recv_sem=extra_recv.at[index * (n - 1) + step - 1],
                device_id=(lax.axis_index("dp"), lax.rem(place + n - step, n)),
                device_id_type=pl.DeviceIdType.MESH,
            )
            for step in range(1, n)
        ]

    def run_steps(number):
        for kind, index, step in plan[number]:
            if kind == "chunk":
                reducer.chunk_step(index, step)
            elif kind == "small":
                reducer.small_step(step)
            elif step == 0:
                for copy in extra_copies(index):
                    copy.start()
            else:
                got, result = ((memory_got, memory_grad), (input_got, input_grad))[index]
                for copy in extra_copies(index):
                    copy.wait()

                @pl.loop(0, blocks)
                def _(block):
                    rows = dyn(block, rows_block)
                    value = result[rows, :]
                    for step in range(n - 1):
                        value = value + got[step, rows, :].astype(F32)
                    result[rows, :] = value

    def wait_loads(first, last):
        for load in loads[first:last]:
            load.wait()

    spread_segments(memory_segment, wide)
    transpose_rows(cross_keys, keys_t)
    prepare_back(tiles, cross_query, cross_grad, query_cols, query_rows, grad_cols, grad_rows)
    clear(query_grad_t)
    clear(key_grad)
    clear(value_grad)
    sums[...] = jnp.zeros(sums.shape, F32)
    for load in feed_loads:
        load.wait()
    run_steps(0)
    for tile in range(tiles):
        attend_back(
            tile, 0, length // TILE, query_segment, wide, 0, False,
            query_cols, query_rows, grad_cols, grad_rows, cross_keys, keys_t, cross_values,
            cross_lse, cross_delta, query_grad_t, key_grad, value_grad, held, held_low, held_grad,
        )
        run_steps(1 + tile)
    base = 2 * in_bias_grad.shape[1] // n + half
    wait_loads(0, n + 7)
    query_finish(tiles, query_grad_t, query_low, sums, 2, True)
    spread_parts(n, tn(first_low[...], query_low[...]), field, base)
    run_steps(5)
    spread_parts(n, row_product(n, place, memory_pieces, key_grad), field, base + half)
    spread_parts(n, row_product(n, place, memory_pieces, value_grad), field, base + 2 * half)
    run_steps(6)
    first_back(
        blocks, rows_block, g2, query_low, query_weight, first_normal, first_rstd, gain, self_out_weight,
        g1, branch, self_grad, sums, 4,
    )
    spread_parts(n, nn(self_attended_t[...], branch[...]), field, base + 3 * half)
    write_delta(tiles, self_grad, self_attended_t, self_delta)
    run_steps(7)
    for step in range(n):

        def write(here, back):
            if step == 0:
                memory_grad[here, :] = back
            else:
                memory_sent[step - 1, here, :] = back.astype(BF16)

        pair_back(n, place, rows_block, count, step, key_grad, value_grad, pair_weight, 0, sums, 3, write)
    run_steps(8)

    wait_loads(n + 7, len(loads))
    spread_segments(target_segment, wide)
    transpose_rows(self_keys, keys_t)
    prepare_back(tiles, self_query, self_grad, query_cols, query_rows, grad_cols, grad_rows)
    clear(query_grad_t)
    clear(key_grad)
    clear(value_grad)
    run_steps(9)
    for tile in range(tiles):
        attend_back(
            tile, 0, place * tiles + tile + 1, query_segment, wide, place * count, True,
            query_cols, query_rows, grad_cols, grad_rows, self_keys, keys_t, self_values,
            self_lse, self_delta, query_grad_t, key_grad, value_grad, held, held_low, held_grad,
        )
        run_steps(10 + tile)
    query_finish(tiles, query_grad_t, query_low, sums, 0, False)
    spread_parts(n, tn(input_pieces[0][...], query_low[...]), field, base + 4 * half)
    run_steps(14)
    spread_parts(n, row_product(n, place, input_pieces, key_grad), field, base + 5 * half)
    run_steps(15)
    spread_parts(n, row_product(n, place, input_pieces, value_grad), field, base + 6 * half)
    run_steps(16)
    for step in range(n):

        def write(here, back):
            if step == 0:
                input_grad[here, :] = back + g1[here, :] + nt(query_low[here, :], self_in_weight[:, :WIDE])
            else:
                input_sent[step - 1, here, :] = back.astype(BF16)

        pair_back(n, place, rows_block, count, step, key_grad, value_grad, self_in_weight, WIDE, sums, 1, write)
    small[...] = jnp.zeros(small.shape, F32)
    for part in range(n):
        here = slice(part * half, (part + 1) * half)
        small[0, part, 0:7, :] = sums[0:7, here]
        small[0, part, 7:13, :] = feed_sums[0:6, here]
        wide_half = in_bias_grad.shape[1] // n
        for row in range(wide_half // half):
            begin = part * wide_half + row * half
            small[0, part, 13 + row : 14 + row, :] = in_bias_grad[:, begin : begin + half]
    run_steps(17)
    run_steps(18)
    reducer.finish()


def back_and_reduce(n, groups, rows_block, feed_grads, streamed, resident):
    count, features = resident[3].shape
    length = n * count
    hidden_rows = feed_grads[0].shape[1]
    half = features // n
    rows = sum(part.shape[1] for part in feed_grads) + 7 * half
    chunks = back_chunks(half, hidden_rows)
    extras = [((n - 1) * count, 8), ((n - 1) * count, 17)]
    plan, unused = plan_steps(n, chunks, extras, BACK_SEGMENTS)
    small_shape = (-(-(13 + hidden_rows // half * half * n // features) // 8) * 8 + 8, half)
    vm = pl.BlockSpec(memory_space=pltpu.VMEM)
    hbm = pl.BlockSpec(memory_space=pl.ANY)
    low_rows = pltpu.VMEM((count, features), BF16)
    wide_rows = pltpu.VMEM((count, features), F32)
    columns = pltpu.VMEM((features, 2 * count), BF16)
    doubled = pltpu.VMEM((2 * count, features), BF16)
    all_wide = pltpu.VMEM((length, features), F32)
    sent = pltpu.VMEM((n - 1, count, features), BF16)
    held = (features // PAIR, BACK_KEYS, 2 * TILE)
    return pl.pallas_call(
        functools.partial(back_kernel, n, groups, rows_block, chunks, plan, [part.shape for part in streamed]),
        in_specs=[hbm] * (len(feed_grads) + len(streamed)) + [vm] * len(resident),
        out_specs=[hbm, vm, vm, vm],
        out_shape=[
            out_like((rows, WIDE), BF16), out_like(small_shape, F32),
            out_like((count, features), F32), out_like((count, features), F32),
        ],
        scratch_shapes=[
            pltpu.VMEM((n, rows, WIDE), BF16), pltpu.VMEM((rows, WIDE), BF16),
            pltpu.VMEM((2, n, *small_shape), F32), pltpu.VMEM((8, features), F32),
            sent, sent, sent, sent,
            pltpu.VMEM((length, TILE), jnp.int32), pltpu.VMEM((features, length), BF16),
            columns, doubled, columns, doubled,
            pltpu.VMEM((features, count), F32), all_wide, all_wide,
            pltpu.VMEM(held, F32), pltpu.VMEM(held, BF16), pltpu.VMEM(held, BF16),
            low_rows, low_rows, low_rows, pltpu.VMEM((features // PAIR, 2 * count), F32), wide_rows,
            pltpu.SemaphoreType.DMA((len(feed_grads),)), pltpu.SemaphoreType.DMA((len(streamed),)),
            pltpu.SemaphoreType.DMA((2 * (n - 1),)), pltpu.SemaphoreType.DMA((2 * (n - 1),)),
            *[pltpu.VMEM(part.shape, part.dtype) for part in streamed],
            *reducer_scratch(n, groups, chunks, rows, small_shape),
        ],
        compiler_params=pltpu.CompilerParams(
            vmem_limit_bytes=VMEM_LIMIT, collective_id=0, has_side_effects=True
        ),
    )(*feed_grads, *streamed, *resident)


def widen_kernel(plan, source, *outs):
    for out, (start, columns) in zip(outs, plan):
        height = out.shape[0]
        for column in range(columns):
            out[:, column * WIDE : (column + 1) * WIDE] = source[
                start + column * height : start + (column + 1) * height, :
            ].astype(F32)


def key_ranges(query_segment, key_segment, tiles, limit):
    edges = query_segment.reshape(tiles, TILE)
    low = jnp.sum((key_segment[None, :] < edges[:, :1]).astype(jnp.int32), axis=1)
    high = jnp.sum((key_segment[None, :] <= edges[:, TILE - 1 :]).astype(jnp.int32), axis=1)
    if limit is not None:
        high = jnp.minimum(high, limit)
    return jnp.stack([low // TILE, (high + TILE - 1) // TILE]).astype(jnp.int32)


def on_device(
    n, groups,
    inputs, memory, cotangent, target_segments, memory_segments,
    self_in_weight, self_in_bias, self_out_weight, self_out_bias, first_gain, first_shift,
    cross_query_weight, cross_pair_weight, cross_bias, cross_out_weight, cross_out_bias,
    second_gain, second_shift, feed_in_weight, feed_in_bias, feed_out_weight, feed_out_bias,
    third_gain, third_shift,
):
    input_rows, memory_rows, cotangent_rows = inputs[0], memory[0], cotangent[0]
    count, features = input_rows.shape
    length = n * count
    hidden = feed_in_weight.shape[1]
    rows_block = min(count, 256)
    tiles = count // TILE
    half = features // n
    place = lax.axis_index("blk").astype(jnp.int32)

    def shifted(field, step):
        return lax.ppermute(field, "blk", [(s, (s + step) % n) for s in range(n)])

    def shifted_back(field, step):
        return lax.ppermute(field, "blk", [(s, (s - step) % n) for s in range(n)])

    input_pieces = [input_rows] + [shifted(input_rows, step) for step in range(1, n)]
    memory_pieces = [memory_rows] + [shifted(memory_rows, step) for step in range(1, n)]

    target_row = target_segments[0]
    source_row = memory_segments[0]
    target_here = lax.dynamic_slice_in_dim(target_row, place * count, count, 0)
    self_ranges = key_ranges(
        target_here, target_row, tiles, place * count + TILE * (1 + jnp.arange(tiles, dtype=jnp.int32))
    )
    cross_ranges = key_ranges(target_here, source_row, tiles, None)
    place_one = place[None]
    query_segment = target_here[None, :]
    target_column = target_row[:, None]
    source_column = source_row[:, None]

    def row(vector):
        return vector[None, :]

    stats = out_like((WIDE // PAIR, 2 * count), F32)
    low_rows = out_like((count, features), BF16)
    wide_rows = out_like((count, features), F32)
    low_row_all = out_like((length, features), BF16)
    statistic = out_like((count, 1), F32)
    wide_scratch = pltpu.VMEM((length, TILE), jnp.int32)
    values_t = pltpu.VMEM((features, length), BF16)
    query_cols = pltpu.VMEM((features, 2 * count), BF16)
    query_rows = pltpu.VMEM((2 * count, features), BF16)
    peak = pltpu.VMEM((8, 2 * TILE), F32)
    sums = pltpu.VMEM((features, TILE), F32)
    held = pltpu.VMEM((features // PAIR, KEYS, 2 * TILE), F32)
    held_low = pltpu.VMEM((features // PAIR, KEYS, 2 * TILE), BF16)
    square = 2 * count * features * features

    (
        query, keys, values, attended_t, lse, normal, rstd, first_low, cross_query
    ) = run(
        functools.partial(self_forward, n, rows_block),
        [place_one, self_ranges, *input_pieces, query_segment, target_column,
         self_in_weight, self_in_bias, self_out_weight, row(self_out_bias), row(first_gain),
         row(first_shift), cross_query_weight, cross_bias],
        2,
        [low_rows, low_row_all, low_row_all, out_like((features, count), BF16), stats, wide_rows,
         statistic, low_rows, low_rows],
        [wide_scratch, values_t, query_cols, peak, peak, sums, held, held_low],
        20 * square, 10 << 20,
    )

    (
        layer_output, cross_keys, cross_values, cross_lse, cross_delta, unused, cross_grad, g2,
        in_grad, down_grad, cross_out_grad, feed_sums, in_bias_grad,
    ) = run(
        functools.partial(cross_and_feed, n, rows_block),
        [place_one, cross_ranges, *memory_pieces, query_segment, source_column, cotangent_rows,
         cross_query, normal, row(first_gain), row(first_shift), cross_pair_weight, cross_bias,
         cross_out_weight, row(cross_out_bias), row(second_gain), row(second_shift),
         feed_in_weight, row(feed_in_bias), feed_out_weight, row(feed_out_bias),
         row(third_gain), row(third_shift)],
        2,
        [low_rows, low_row_all, low_row_all, stats, stats, out_like((8, 128), F32), low_rows, wide_rows,
         out_like((n, hidden // n, features), BF16), out_like((n, hidden // n, features), BF16),
         out_like((n, half, features), BF16), out_like((8, features), F32), out_like((1, hidden), F32)],
        [wide_scratch, values_t, query_cols, peak, peak, sums, held, held_low,
         pltpu.VMEM((features, count), BF16), pltpu.VMEM((count, features), F32),
         pltpu.VMEM((count, 1), F32), pltpu.VMEM((count, features), BF16),
         pltpu.VMEM((features, count), BF16), pltpu.VMEM((count, hidden), BF16),
         pltpu.VMEM((count, hidden), F32), pltpu.VMEM((count, features), F32),
         pltpu.VMEM((count, features), BF16), pltpu.VMEM((features, count), BF16)],
        50 * square, 20 << 20,
    )

    if length <= 1024 and half % TILE == 0:
        packed, small, memory_grad, input_grad = back_and_reduce(
            n, groups, rows_block,
            [in_grad, down_grad, cross_out_grad],
            [*memory_pieces, cross_pair_weight, first_low, cross_query_weight, g2, normal, self_out_weight,
             attended_t, keys, values, query, *input_pieces, self_in_weight],
            [query_segment, source_column, target_column, cross_query, cross_grad, cross_keys, cross_values,
             cross_lse, cross_delta, feed_sums, in_bias_grad, row(first_gain), rstd, lse],
        )
        count_small = 13
        small = small.reshape(-1)[: count_small * half + hidden // n]
    else:
        back_scratch = [
            wide_scratch, values_t, query_cols, query_rows, query_cols, query_rows,
            pltpu.VMEM((features, count), F32), pltpu.VMEM((length, features), F32),
            pltpu.VMEM((length, features), F32), held, held_low, held_low, pltpu.VMEM((count, features), BF16),
        ]
        sent_like = out_like((max(n - 1, 1), count, features), BF16)
        (
            memory_own, memory_sent, cross_query_grad, cross_pair_grad, self_out_grad, self_grad,
            self_delta, g1, cross_sums,
        ) = run(
            functools.partial(cross_backward, n, rows_block),
            [place_one, cross_ranges, *memory_pieces, query_segment, source_column, cross_query,
             cross_grad, cross_keys, cross_values, cross_lse, cross_delta, g2, normal, rstd, first_low,
             row(first_gain), cross_query_weight, cross_pair_weight, self_out_weight, attended_t],
            2,
            [wide_rows, sent_like, out_like((n, half, features), BF16),
             out_like((n, 2 * half, features), BF16), out_like((n, half, features), BF16), low_rows,
             stats, wide_rows, out_like((8, features), F32)],
            back_scratch + [pltpu.VMEM((count, features), BF16)],
            30 * square, 15 << 20,
        )
        (input_own, input_sent, self_in_grad, self_sums) = run(
            functools.partial(self_backward, n, rows_block),
            [place_one, self_ranges, *input_pieces, query_segment, target_column, query, self_grad,
             keys, values, lse, self_delta, g1, self_in_weight],
            2,
            [wide_rows, sent_like, out_like((n, 3 * half, features), BF16), out_like((8, features), F32)],
            back_scratch,
            30 * square, 15 << 20,
        )

        memory_grad, input_grad = memory_own, input_own
        for step in range(1, n):
            memory_grad = memory_grad + shifted_back(memory_sent[step - 1], step).astype(F32)
            input_grad = input_grad + shifted_back(input_sent[step - 1], step).astype(F32)

        vectors = jnp.concatenate([self_sums[:2], cross_sums[:5], feed_sums[:6]], axis=0)
        count_small = vectors.shape[0]
        small = jnp.concatenate(
            [
                jnp.transpose(vectors.reshape(count_small, n, half), (1, 0, 2)).reshape(n, -1),
                in_bias_grad.reshape(n, -1),
            ],
            axis=1,
        )
        amount = small.shape[1]
        small_rows = -(-amount // (8 * WIDE)) * 8
        small = jnp.pad(small, ((0, 0), (0, small_rows * WIDE - amount))).reshape(n, small_rows, WIDE)
        packed, small = reduce_all(
            n, groups,
            [in_grad, down_grad, cross_out_grad, cross_query_grad, cross_pair_grad, self_out_grad, self_in_grad],
            small,
        )
        small = small.reshape(-1)[:amount]
    plan = []
    start = 0
    shapes = []
    for height, columns in (
        (half, hidden // features), (hidden // n, 1), (half, 1), (half, 1), (half, 2), (half, 1), (half, 3)
    ):
        plan.append((start, columns))
        shapes.append(out_like((height, columns * features), F32))
        start += height * columns
    (
        feed_in_grad, feed_out_grad, cross_out_total, cross_query_total, cross_pair_total,
        self_out_total, self_in_total,
    ) = run(functools.partial(widen_kernel, plan), [packed], 0, shapes, [], 0, 12 << 20)
    rows_small = small[: count_small * half].reshape(count_small, half)
    (
        self_query_bias, self_value_bias, cross_query_bias, cross_value_bias, first_gain_grad,
        first_shift_grad, self_out_bias_grad, third_gain_grad, third_shift_grad, feed_out_bias_grad,
        second_gain_grad, second_shift_grad, cross_out_bias_grad,
    ) = [rows_small[index] for index in range(count_small)]
    return (
        layer_output[None],
        input_grad[None],
        memory_grad[None],
        self_in_total,
        jnp.stack([self_query_bias, self_value_bias]),
        self_out_total,
        self_out_bias_grad,
        first_gain_grad,
        first_shift_grad,
        cross_query_total,
        cross_pair_total,
        jnp.stack([cross_query_bias, cross_value_bias]),
        cross_out_total,
        cross_out_bias_grad,
        second_gain_grad,
        second_shift_grad,
        feed_in_grad,
        small[count_small * half :],
        feed_out_grad,
        feed_out_bias_grad,
        third_gain_grad,
        third_shift_grad,
    )


def solution(mesh):
    rows = P("dp", "blk", None)
    everywhere = P()
    split = P("blk", None)
    vector = P("blk")
    pair = P(None, "blk")
    return jax.shard_map(
        functools.partial(on_device, mesh.shape["blk"], mesh.shape["dp"]),
        mesh=mesh,
        in_specs=(rows, rows, rows, P("dp", None), P("dp", None)) + (everywhere,) * 19,
        out_specs=(
            rows, rows, rows, split, pair, split, vector, vector, vector, split, split, pair, split,
            vector, vector, vector, split, vector, split, vector, vector, vector,
        ),
        check_vma=False,
    )
```

time: 234 us -> 191 us (0.82)
  Pallas kernels: 191 us -> 156 us
  starting transfers between devices: 17 us -> 3.08 us
  waiting for transfers between devices: 9.68 us -> 16.8 us
  other arithmetic: 6.94 us -> 2.11 us
    pallas_call x5 -> x3, Pallas kernels: 98.3 us -> 53 us  [run(): pl.pallas_call(body, in_specs=[sm] * smem_count + [vm] * (len(ins) - smem...]
    ppermute x2 -> x0, starting transfers between devices: 13.9 us -> none  [shifted_back(): return lax.ppermute(field, 'blk', [(s, (s - step) % n) for s in range(n)])]
    pallas_call x1, Pallas kernels: 92.6 us -> 103 us  [back_and_reduce(): pl.pallas_call(functools.partial(back_kernel, n, groups, rows_block, chun...]
    ppermute x2, waiting for transfers between devices: 6.49 us -> 16.8 us  [shifted(): return lax.ppermute(field, 'blk', [(s, (s + step) % n) for s in range(n)])]
    ppermute x2 -> x0, waiting for transfers between devices: 3.19 us -> none  [shifted_back(): return lax.ppermute(field, 'blk', [(s, (s - step) % n) for s in range(n)])]
    unnamed x18 -> x14, local copies, waits for them, and re-layouts: 3.01 us -> 4.84 us
  transfers between devices with their start and end apart: 4 -> 2, of which waited for: 2 -> 1; matrix products, arithmetic and copies ran while one was open for 5% -> 3% of each run, Pallas kernels for 47% -> 6%
where the time goes in v2:
time: 191 us
  Pallas kernels  156 us (82%)
  waiting for transfers between devices  16.8 us (9%)
  local copies, waits for them, and re-layouts  12 us (6%)
  starting transfers between devices  3.08 us (2%)
  other arithmetic  2.11 us (1%)
    pallas_call x1, Pallas kernels, back_and_reduce(): pl.pallas_call(functools.partial(back_kernel, n, groups, rows_block, chun...  103 us
    pallas_call x3, Pallas kernels, run(): pl.pallas_call(body, in_specs=[sm] * smem_count + [vm] * (len(ins) - smem...  53 us
    ppermute x2, waiting for transfers between devices, shifted(): return lax.ppermute(field, 'blk', [(s, (s + step) % n) for s in range(n)])  16.8 us
    unnamed x14, local copies, waits for them, and re-layouts  4.84 us
  transfers between devices with their start and end apart: 2, of which 1 were waited for; matrix products, arithmetic and copies ran while one was open for 3% of the time, Pallas kernels for 6%

profile of v2, /device:TPU:0, one launch (start us, length us, event | category | flops | bytes accessed | tf_op | source)
XLA Modules:
  0.0 190.9 jit_solution(10459248477172859405)
XLA Ops:
  0.7 3.0 %collective-permute-start = (bf16[512,512]{1,0:T(8,128)(2,1)}, bf16[512,512]{1,0:T(8,128)(2,1)S(1)}, u32[]{:S(2)}, u32[]{:S(2)}) collective-permute-start(bf16[512,512]{1,0:T(8,128)(2,1)} %bitcast.66), channel_id=1, source_target_pairs={{0,1},{1,0},{2,3},{3,2},{4,5},{5,4},{6,7},{7,6},{8,9},{9,8},{10,11... | collective-permute-start | bytes 1572872 | tf_op jit(solution)/shard_map/ppermute | solution.py:1238
  3.7 0.1 collective-permute-start.1
  3.7 0.7 constant_dynamic-slice_fusion.refs_2_.refs_18_
  4.4 0.0 copy-start.4
  4.4 0.2 slice_reduce_fusion.1
  4.6 0.9 convert_reduce_fusion.3
  5.6 0.6 pad_add_fusion.ranges_ref
  6.2 0.6 pad_add_fusion.1.ranges_ref
  6.7 1.7 copy.55.refs_3_.refs_19_
  8.4 1.8 copy.54.refs_3_.refs_20_
  10.2 16.8 %collective-permute-done.1.refs_1_.refs_16_ = bf16[512,512]{1,0:T(8,128)(2,1)S(1)} collective-permute-done((bf16[512,512]{1,0:T(8,128)(2,1)}, bf16[512,512]{1,0:T(8,128)(2,1)S(1)}, u32[]{:S(2)}, u32[]{:S(2)}) %collective-permute-start.1) | collective-permute-done | bytes 524320 | tf_op jit(solution)/shard_map/ppermute | solution.py:1238
  27.0 0.0 copy-start.3
  27.0 0.0 copy-done.4
  27.0 0.8 copy-done.3
  27.8 11.2 %shard_map.399 = (bf16[512,512]{1,0:T(8,128)(2,1)}, bf16[1024,512]{1,0:T(8,128)(2,1)}, bf16[1024,512]{1,0:T(8,128)(2,1)}, bf16[512,512]{1,0:T(8,128)(2,1)}, f32[...) custom-call(s32[1]{0:T(128)} %bitcast.place_ref, ...), custom_call_target="tpu_custom_call" | custom-call | flops 5368709120 | bytes 10485760 | tf_op jit(solution)/shard_map/pallas_call | solution.py:234
  39.1 0.0 collective-permute-done.refs_1_.refs_4_
  39.1 0.0 copy-start.2
  39.1 0.8 copy-done.2
  39.9 36.0 %shard_map.400 = (bf16[512,512]{1,0:T(8,128)(2,1)}, bf16[1024,512]{1,0:T(8,128)(2,1)}, bf16[1024,512]{1,0:T(8,128)(2,1)}, f32[4,1024]{1,0:T(4,128)}, f32[4,1024]...) custom-call(s32[1]{0:T(128)} %bitcast.place_ref, ...), custom_call_target="tpu_custom_call" | custom-call | flops 13421772800 | bytes 20971520 | tf_op jit(solution)/shard_map/pallas_call | solution.py:234
  75.8 103.2 %shard_map.401 = (bf16[4096,512]{1,0:T(8,128)(2,1)}, f32[32,256]{1,0:T(8,128)}, f32[512,512]{1,0:T(8,128)}, f32[512,512]{1,0:T(8,128)}) custom-call(bf16[2,1024,512]{2,1,0:T(8,128)(2,1)} %get-tuple-element.57.refs_0_, bf16[2,1024,512]{2,1,0:T(8,128)(2,1)} %get-tuple-element.58.refs_1_, bf16[2,256,512]{2,1,0:T(8,128)(2,1)} %get-tuple-element.59.refs_2_, ...), custom_call_target="tpu_custom_call" | custom-call | tf_op jit(solution)/shard_map/pallas_call | solution.py:1174
  179.0 1.4 fusion.2
  180.4 1.5 fusion.1
  181.9 0.7 slice_bitcast_fusion
  182.6 0.0 copy-start.1
  182.6 5.8 %shard_map.402 = (f32[256,2048]{1,0:T(8,128)}, f32[1024,512]{1,0:T(8,128)}, f32[256,512]{1,0:T(8,128)}, f32[256,512]{1,0:T(8,128)}, f32[256,1024]{1,0:T(8,128)},...) custom-call(bf16[4096,512]{1,0:T(8,128)(2,1)} %get-tuple-element.77.source), custom_call_target="tpu_custom_call" | custom-call | bytes 12582912 | tf_op jit(solution)/shard_map/pallas_call | solution.py:234
  188.3 0.0 copy-start
  188.3 0.6 copy.58
  188.9 0.0 copy-done.1
  188.9 1.0 copy.61
  189.9 0.0 copy-done
  189.9 1.0 copy.62
  (2 shorter events, 0.0 us)
Async XLA Ops:
  0.7 38.4 %collective-permute-start = (bf16[512,512]{1,0:T(8,128)(2,1)}, bf16[512,512]{1,0:T(8,128)(2,1)S(1)}, u32[]{:S(2)}, u32[]{:S(2)}) collective-permute-start(bf16[512,512]{1,0:T(8,128)(2,1)} %bitcast.66), channel_id=1, source_target_pairs={{0,1},{1,0},{2,3},{3,2},{4,5},{5,4},{6,7},{7,6},{8,9},{9,8},{10,11... | collective-permute-start | bytes 1572872 | tf_op jit(solution)/shard_map/ppermute | solution.py:1238
  3.7 23.4 %collective-permute-start.1 = (bf16[512,512]{1,0:T(8,128)(2,1)}, bf16[512,512]{1,0:T(8,128)(2,1)S(1)}, u32[]{:S(2)}, u32[]{:S(2)}) collective-permute-start(bf16[512,512]{1,0:T(8,128)(2,1)} %bitcast.69), channel_id=1, source_target_pairs={{0,1},{1,0},{2,3},{3,2},{4,5},{5,4},{6,7},{7,6},{8,9},{9,8},{10,11... | collective-permute-start | bytes 1572872 | tf_op jit(solution)/shard_map/ppermute | solution.py:1238
  4.4 22.6 %copy-start.4 = (s32[1,512]{1,0:T(1,128)}, s32[1,512]{1,0:T(1,128)S(1)}, u32[]{:S(2)}) copy-start(s32[1,512]{1,0:T(1,128)S(1)} %constant_dynamic-slice_fusion.refs_2_.refs_18_) | copy-start | bytes 6148
  27.0 0.8 copy-start.3
  39.1 0.8 copy-start.2
  182.6 6.4 %copy-start.1 = (f32[512,512]{1,0:T(8,128)S(1)}, f32[512,512]{1,0:T(8,128)}, u32[]{:S(2)}) copy-start(f32[512,512]{1,0:T(8,128)} %get-tuple-element.75) | copy-start | bytes 3145732
  188.3 1.6 copy-start

commit v3 on v2

--- a/solution.py
+++ b/solution.py
@@ -17,7 +17,7 @@
 MASKED = -1e30
 F32 = jnp.float32
 BF16 = jnp.bfloat16
-VMEM_LIMIT = 58 << 20
+VMEM_LIMIT = 62 << 20
 
 
 def nn(left, right):
@@ -173,12 +173,12 @@
 
 
 def attend_back(
-    tile, low, high, query_row_ref, key_wide_ref, offset, causal,
+    tile, low, high, query_row_ref, first_query, key_wide_ref, offset, causal,
     query_cols, query_rows, grad_cols, grad_rows, keys, keys_t, values, lse_ref, delta_ref,
     query_grad_t, key_grad, value_grad, held, held_low, held_grad,
 ):
     pairs = WIDE // PAIR
-    query_row = query_row_ref[:, dyn(tile, TILE)]
+    query_row = query_row_ref[:, pl.ds(pl.multiple_of(first_query + tile * TILE, TILE), TILE)]
     both = dyn(tile, 2 * TILE)
 
     size = held.shape[1]
@@ -554,7 +554,7 @@
     @pl.loop(0, tiles)
     def _(tile):
         attend_back(
-            tile, ranges_ref[0, tile], ranges_ref[1, tile], query_segment, wide, 0, False,
+            tile, ranges_ref[0, tile], ranges_ref[1, tile], query_segment, 0, wide, 0, False,
             query_cols, query_rows, grad_cols, grad_rows, keys, keys_t, values, lse_ref, delta_ref,
             query_grad_t, key_grad, value_grad, held, held_low, held_grad,
         )
@@ -603,7 +603,7 @@
     @pl.loop(0, tiles)
     def _(tile):
         attend_back(
-            tile, ranges_ref[0, tile], ranges_ref[1, tile], query_segment, wide, place * count, True,
+            tile, ranges_ref[0, tile], ranges_ref[1, tile], query_segment, 0, wide, place * count, True,
             query_cols, query_rows, grad_cols, grad_rows, keys, keys_t, values, lse_ref, delta_ref,
             query_grad_t, key_grad, value_grad, held, held_low, held_grad,
         )
@@ -635,6 +635,7 @@
     now = 0.0
     pending = []
     plan = []
+    crossed = set()
 
     def send(link, rows, rate=LINK_RATE):
         free[link] = max(free[link], now) + rows * rate
@@ -650,6 +651,7 @@
             elif step in (1, 2) and (step == 1) == y_first:
                 ready = send("y", (n if y_first else 1) * rows // 4)
             elif step in (1, 2):
+                crossed.add(index)
                 ready = send("x", (n - 1) * rows // (4 if y_first else 2))
             elif step in (3, 4):
                 ready = send("z", rows // 4)
@@ -660,9 +662,10 @@
             else:
                 return
         elif kind == "extra":
-            if step == 1:
+            if step == 2:
                 return
-            ready = send("x", extras[index][0])
+            rows = extras[index][0]
+            ready = send("core", rows, CORE_RATE) if step == 0 else send("x", rows // 2)
         else:
             if step == 4:
                 return
@@ -676,16 +679,20 @@
             now += segments[number]
             released = [("chunk", i) for i, chunk in enumerate(chunks) if chunk[3] == number]
             released += [("extra", i) for i, extra in enumerate(extras) if extra[1] == number]
-            if number == len(segments) - 1:
+            if number == max(len(segments) - 2, 0):
                 released.append(("small", 0))
             for kind, index in released:
                 execute(kind, index, 0)
                 order.append((kind, index, 0))
         while pending:
             pending.sort()
-            if not last and pending[0][0] + MARGIN > now:
+            first = 0
+            if len(crossed) < len(chunks):
+                while first < len(pending) and pending[first][2:] == ("extra", pending[first][3], 1):
+                    first += 1
+            if first == len(pending) or (not last and pending[first][0] + MARGIN > now):
                 break
-            ready, unused, kind, index, step = pending.pop(0)
+            ready, unused, kind, index, step = pending.pop(first)
             now = max(now, ready)
             execute(kind, index, step)
             order.append((kind, index, step))
@@ -714,12 +721,20 @@
         self.z_peers = [(lax.rem(group + 4 * step, groups), part) for step in range(1, depth)]
         self.per_chunk = 4 + (n - 1) + 2 * (depth - 1)
 
-    def enter(self):
+    def enter(self, far_peer=None, has_far=None):
         peers = [self.core_peer, self.side_peer] + self.blk_peers + self.z_peers
         barrier = pltpu.get_barrier_semaphore()
         for peer in peers:
             pl.semaphore_signal(barrier, inc=1, device_id=peer, device_id_type=pl.DeviceIdType.MESH)
-        pl.semaphore_wait(barrier, len(peers))
+        if far_peer is not None:
+
+            @pl.when(has_far)
+            def _():
+                pl.semaphore_signal(barrier, inc=1, device_id=far_peer, device_id_type=pl.DeviceIdType.MESH)
+
+            pl.semaphore_wait(barrier, jnp.where(has_far, len(peers) + 1, len(peers)))
+        else:
+            pl.semaphore_wait(barrier, len(peers))
 
     def copy(self, source, target, sem, peer):
         return pltpu.make_async_remote_copy(
@@ -963,14 +978,14 @@
 
 Y_FIRST = [letter == "y" for letter in "yyxyxyxyxxyy"]
 BACK_SEGMENTS = [
-    3.5, 3.2, 3.2, 3.2, 3.2, 1.5, 3.0, 3.5, 2.2,
-    2.5, 2.6, 2.6, 3.2, 3.2, 1.5, 1.2, 1.2, 2.4,
+    3.5, 3.2, 3.2, 3.2, 3.2, 1.5, 3.0, 3.5,
+    2.5, 2.6, 2.6, 3.2, 3.2, 1.5, 1.2, 1.2, 2.4, 2.2,
 ]
 
 
 def back_chunks(half, hidden_rows):
     released = [(2 * half, 0)] * (hidden_rows // half) + [(half, 0)]
-    released += [(half, segment) for segment in (5, 6, 6, 7, 14, 15, 16)]
+    released += [(half, segment) for segment in (5, 6, 6, 7, 13, 14, 15)]
     chunks = []
     start = 0
     for index, (rows, segment) in enumerate(released):
@@ -983,10 +998,10 @@
     feed_refs, refs = refs[:3], refs[3:]
     streamed, refs = refs[: len(load_plan)], refs[len(load_plan) :]
     (
-        query_segment, memory_segment, target_segment, cross_query, cross_grad, cross_keys, cross_values,
+        target_row, memory_row, cross_query, cross_grad, cross_keys, cross_values,
         cross_lse, cross_delta, feed_sums, in_bias_grad, gain, first_rstd, self_lse,
         total_out, small_out, memory_grad, input_grad,
-        field, total, small, sums, memory_sent, memory_got, input_sent, input_got,
+        field, total, small, sums, memory_sent, memory_got, input_sent, input_got, pair_low,
         wide, keys_t, query_cols, query_rows, grad_cols, grad_rows, query_grad_t, key_grad, value_grad,
         held, held_low, held_grad, query_low, branch, self_grad, self_delta, g1,
         feed_sem, load_sem, extra_send, extra_recv,
@@ -998,7 +1013,10 @@
     tiles = count // TILE
     blocks = count // rows_block
     half = WIDE // n
-    place = lax.axis_index("blk")
+    group, part = lax.axis_index("dp"), lax.axis_index("blk")
+    place = lax.rem(group, 2)
+    away = place != part
+    owner = (group - place + part, place)
 
     feed_loads = []
     start = 0
@@ -1015,28 +1033,55 @@
     ]
     for load in loads:
         load.start()
-    memory_pieces, held_loads = held_loads[:n], held_loads[n:]
+    memory_pieces = [held_loads[0].at[step] for step in range(n)]
+    held_loads = held_loads[1:]
     (
         pair_weight, first_low, query_weight, g2, first_normal, self_out_weight, self_attended_t,
         self_keys, self_values, self_query,
     ) = held_loads[:10]
-    input_pieces, (self_in_weight,) = held_loads[10 : 10 + n], held_loads[10 + n :]
+    input_pieces = [held_loads[10].at[step] for step in range(n)]
+    self_in_weight = held_loads[11]
 
     reducer = Reducer(n, groups, chunks, field, total, total_out, small, small_out, buffers)
-    reducer.enter()
-
-    def extra_copies(index):
-        sent, got = ((memory_sent, memory_got), (input_sent, input_got))[index]
-        return [
-            pltpu.make_async_remote_copy(
-                src_ref=sent.at[step - 1], dst_ref=got.at[step - 1],
-                send_sem=extra_send.at[index * (n - 1) + step - 1],
-                recv_sem=extra_recv.at[index * (n - 1) + step - 1],
-                device_id=(lax.axis_index("dp"), lax.rem(place + n - step, n)),
-                device_id_type=pl.DeviceIdType.MESH,
-            )
-            for step in range(1, n)
-        ]
+    reducer.enter(owner, away)
+
+    extras = ((memory_sent, memory_got, memory_grad), (input_sent, input_got, input_grad))
+
+    def extra_copy(index, hop):
+        sent, got, unused = extras[index]
+        return pltpu.make_async_remote_copy(
+            src_ref=sent.at[hop], dst_ref=got.at[hop],
+            send_sem=extra_send.at[2 * index + hop], recv_sem=extra_recv.at[2 * index + hop],
+            device_id=reducer.core_peer if hop == 0 else owner, device_id_type=pl.DeviceIdType.MESH,
+        )
+
+    def extra_step(index, step):
+        sent, got, result = extras[index]
+        if step == 0:
+            extra_copy(index, 0).start()
+        elif step == 1:
+            extra_copy(index, 0).wait()
+
+            @pl.loop(0, blocks)
+            def _(block):
+                rows = dyn(block, rows_block)
+                value = result[rows, :] + got[0, rows, :].astype(F32)
+                result[rows, :] = value
+                sent[1, rows, :] = value.astype(BF16)
+
+            @pl.when(away)
+            def _():
+                extra_copy(index, 1).start()
+        else:
+
+            @pl.when(away)
+            def _():
+                extra_copy(index, 1).wait()
+
+                @pl.loop(0, blocks)
+                def _(block):
+                    rows = dyn(block, rows_block)
+                    result[rows, :] = got[1, rows, :].astype(F32)
 
     def run_steps(number):
         for kind, index, step in plan[number]:
@@ -1044,27 +1089,14 @@
                 reducer.chunk_step(index, step)
             elif kind == "small":
                 reducer.small_step(step)
-            elif step == 0:
-                for copy in extra_copies(index):
-                    copy.start()
             else:
-                got, result = ((memory_got, memory_grad), (input_got, input_grad))[index]
-                for copy in extra_copies(index):
-                    copy.wait()
-
-                @pl.loop(0, blocks)
-                def _(block):
-                    rows = dyn(block, rows_block)
-                    value = result[rows, :]
-                    for step in range(n - 1):
-                        value = value + got[step, rows, :].astype(F32)
-                    result[rows, :] = value
+                extra_step(index, step)
 
     def wait_loads(first, last):
         for load in loads[first:last]:
             load.wait()
 
-    spread_segments(memory_segment, wide)
+    spread_row(memory_row, wide)
     transpose_rows(cross_keys, keys_t)
     prepare_back(tiles, cross_query, cross_grad, query_cols, query_rows, grad_cols, grad_rows)
     clear(query_grad_t)
@@ -1076,18 +1108,29 @@
     run_steps(0)
     for tile in range(tiles):
         attend_back(
-            tile, 0, length // TILE, query_segment, wide, 0, False,
+            tile, 0, length // TILE, target_row, place * count, wide, place * count, False,
             query_cols, query_rows, grad_cols, grad_rows, cross_keys, keys_t, cross_values,
             cross_lse, cross_delta, query_grad_t, key_grad, value_grad, held, held_low, held_grad,
         )
         run_steps(1 + tile)
     base = 2 * in_bias_grad.shape[1] // n + half
-    wait_loads(0, n + 7)
+    wait_loads(0, 8)
     query_finish(tiles, query_grad_t, query_low, sums, 2, True)
     spread_parts(n, tn(first_low[...], query_low[...]), field, base)
     run_steps(5)
-    spread_parts(n, row_product(n, place, memory_pieces, key_grad), field, base + half)
-    spread_parts(n, row_product(n, place, memory_pieces, value_grad), field, base + 2 * half)
+    for side, source in ((0, key_grad), (1, value_grad)):
+
+        @pl.loop(0, length // rows_block)
+        def _(block):
+            rows = dyn(block, rows_block)
+            value = source[rows, :]
+            pair_low[side, rows, :] = value.astype(BF16)
+            if side == 1:
+                sums[3:4, :] += col_sum(value)
+
+        spread_parts(
+            n, row_product(n, place, memory_pieces, pair_low.at[side]), field, base + half + side * half
+        )
     run_steps(6)
     first_back(
         blocks, rows_block, g2, query_low, query_weight, first_normal, first_rstd, gain, self_out_weight,
@@ -1096,46 +1139,36 @@
     spread_parts(n, nn(self_attended_t[...], branch[...]), field, base + 3 * half)
     write_delta(tiles, self_grad, self_attended_t, self_delta)
     run_steps(7)
-    for step in range(n):
-
-        def write(here, back):
-            if step == 0:
-                memory_grad[here, :] = back
-            else:
-                memory_sent[step - 1, here, :] = back.astype(BF16)
-
-        pair_back(n, place, rows_block, count, step, key_grad, value_grad, pair_weight, 0, sums, 3, write)
-    run_steps(8)
-
-    wait_loads(n + 7, len(loads))
-    spread_segments(target_segment, wide)
+
+    wait_loads(8, len(loads))
+    spread_row(target_row, wide)
     transpose_rows(self_keys, keys_t)
     prepare_back(tiles, self_query, self_grad, query_cols, query_rows, grad_cols, grad_rows)
     clear(query_grad_t)
     clear(key_grad)
     clear(value_grad)
-    run_steps(9)
+    run_steps(8)
     for tile in range(tiles):
         attend_back(
-            tile, 0, place * tiles + tile + 1, query_segment, wide, place * count, True,
+            tile, 0, place * tiles + tile + 1, target_row, place * count, wide, place * count, True,
             query_cols, query_rows, grad_cols, grad_rows, self_keys, keys_t, self_values,
             self_lse, self_delta, query_grad_t, key_grad, value_grad, held, held_low, held_grad,
         )
-        run_steps(10 + tile)
+        run_steps(9 + tile)
     query_finish(tiles, query_grad_t, query_low, sums, 0, False)
     spread_parts(n, tn(input_pieces[0][...], query_low[...]), field, base + 4 * half)
+    run_steps(13)
+    spread_parts(n, row_product(n, place, input_pieces, key_grad), field, base + 5 * half)
     run_steps(14)
-    spread_parts(n, row_product(n, place, input_pieces, key_grad), field, base + 5 * half)
+    spread_parts(n, row_product(n, place, input_pieces, value_grad), field, base + 6 * half)
     run_steps(15)
-    spread_parts(n, row_product(n, place, input_pieces, value_grad), field, base + 6 * half)
-    run_steps(16)
     for step in range(n):
 
         def write(here, back):
             if step == 0:
                 input_grad[here, :] = back + g1[here, :] + nt(query_low[here, :], self_in_weight[:, :WIDE])
             else:
-                input_sent[step - 1, here, :] = back.astype(BF16)
+                input_sent[0, here, :] = back.astype(BF16)
 
         pair_back(n, place, rows_block, count, step, key_grad, value_grad, self_in_weight, WIDE, sums, 1, write)
     small[...] = jnp.zeros(small.shape, F32)
@@ -1147,19 +1180,32 @@
         for row in range(wide_half // half):
             begin = part * wide_half + row * half
             small[0, part, 13 + row : 14 + row, :] = in_bias_grad[:, begin : begin + half]
+    run_steps(16)
+    for step in range(n):
+        spot = lax.rem(place + n - step, n)
+
+        @pl.loop(0, blocks)
+        def _(block):
+            rows, here = dyn(spot * blocks + block, rows_block), dyn(block, rows_block)
+            back = nt(pair_low[0, rows, :], pair_weight[:, :WIDE]) + nt(pair_low[1, rows, :], pair_weight[:, WIDE:])
+            if step == 0:
+                memory_grad[here, :] = back
+            else:
+                memory_sent[0, here, :] = back.astype(BF16)
+
     run_steps(17)
     run_steps(18)
     reducer.finish()
 
 
 def back_and_reduce(n, groups, rows_block, feed_grads, streamed, resident):
-    count, features = resident[3].shape
+    count, features = resident[2].shape
     length = n * count
     hidden_rows = feed_grads[0].shape[1]
     half = features // n
     rows = sum(part.shape[1] for part in feed_grads) + 7 * half
     chunks = back_chunks(half, hidden_rows)
-    extras = [((n - 1) * count, 8), ((n - 1) * count, 17)]
+    extras = [(count, 17), (count, 16)]
     plan, unused = plan_steps(n, chunks, extras, BACK_SEGMENTS)
     small_shape = (-(-(13 + hidden_rows // half * half * n // features) // 8) * 8 + 8, half)
     vm = pl.BlockSpec(memory_space=pltpu.VMEM)
@@ -1169,7 +1215,7 @@
     columns = pltpu.VMEM((features, 2 * count), BF16)
     doubled = pltpu.VMEM((2 * count, features), BF16)
     all_wide = pltpu.VMEM((length, features), F32)
-    sent = pltpu.VMEM((n - 1, count, features), BF16)
+    sent = pltpu.VMEM((2, count, features), BF16)
     held = (features // PAIR, BACK_KEYS, 2 * TILE)
     return pl.pallas_call(
         functools.partial(back_kernel, n, groups, rows_block, chunks, plan, [part.shape for part in streamed]),
@@ -1182,14 +1228,14 @@
         scratch_shapes=[
             pltpu.VMEM((n, rows, WIDE), BF16), pltpu.VMEM((rows, WIDE), BF16),
             pltpu.VMEM((2, n, *small_shape), F32), pltpu.VMEM((8, features), F32),
-            sent, sent, sent, sent,
+            sent, sent, sent, sent, pltpu.VMEM((2, length, features), BF16),
             pltpu.VMEM((length, TILE), jnp.int32), pltpu.VMEM((features, length), BF16),
             columns, doubled, columns, doubled,
             pltpu.VMEM((features, count), F32), all_wide, all_wide,
             pltpu.VMEM(held, F32), pltpu.VMEM(held, BF16), pltpu.VMEM(held, BF16),
             low_rows, low_rows, low_rows, pltpu.VMEM((features // PAIR, 2 * count), F32), wide_rows,
             pltpu.SemaphoreType.DMA((len(feed_grads),)), pltpu.SemaphoreType.DMA((len(streamed),)),
-            pltpu.SemaphoreType.DMA((2 * (n - 1),)), pltpu.SemaphoreType.DMA((2 * (n - 1),)),
+            pltpu.SemaphoreType.DMA((4,)), pltpu.SemaphoreType.DMA((4,)),
             *[pltpu.VMEM(part.shape, part.dtype) for part in streamed],
             *reducer_scratch(n, groups, chunks, rows, small_shape),
         ],
@@ -1199,6 +1245,410 @@
     )(*feed_grads, *streamed, *resident)
 
 
+def spread_row(row_ref, wide_ref):
+    @pl.loop(0, row_ref.shape[1] // TILE)
+    def _(block):
+        wide_ref[dyn(block, TILE), :] = jnp.broadcast_to(row_ref[:, dyn(block, TILE)], (TILE, TILE)).T
+
+
+def attend_whole(
+    tiles, query_row_ref, first_query, key_wide_ref, causal, query_cols, keys, values_t, attended_t, lse_ref,
+    held, held_low,
+):
+    pairs = WIDE // PAIR
+    length = keys.shape[0]
+
+    @pl.loop(0, tiles)
+    def _(tile):
+        begin = pl.multiple_of(first_query + tile * TILE, TILE)
+        allowed = key_wide_ref[...] == query_row_ref[:, pl.ds(begin, TILE)]
+        if causal:
+            key_position = lax.broadcasted_iota(jnp.int32, (length, TILE), 0)
+            query_position = begin + lax.broadcasted_iota(jnp.int32, (length, TILE), 1)
+            allowed = allowed & (key_position <= query_position)
+        bias = jnp.where(allowed, 0.0, MASKED)
+        bias = jnp.concatenate([bias, bias], axis=1)
+        both = dyn(tile, 2 * TILE)
+        peaks, shares = [], []
+        for pair in range(pairs):
+            lanes = slice(pair * PAIR, (pair + 1) * PAIR)
+            scores = nn(keys[:, lanes], query_cols[lanes, both]) + bias
+            held[pair] = scores
+            peaks.append(jnp.max(scores, axis=0, keepdims=True))
+        for pair in range(pairs):
+            weights = jnp.exp(held[pair] - peaks[pair])
+            total = col_sum(weights)
+            held_low[pair] = weights.astype(BF16)
+            lse_ref[pair : pair + 1, both] = peaks[pair] + jnp.log(total)
+            shares.append(1.0 / total)
+        for pair in range(pairs):
+            share = shares[pair]
+            mixed = nn(values_t[pair * PAIR : (pair + 1) * PAIR, :], held_low[pair])
+            first = slice(pair * PAIR, pair * PAIR + HEAD)
+            second = slice(pair * PAIR + HEAD, (pair + 1) * PAIR)
+            attended_t[first, dyn(tile, TILE)] = (mixed[:HEAD, :TILE] * share[:, :TILE]).astype(BF16)
+            attended_t[second, dyn(tile, TILE)] = (mixed[HEAD:, TILE:] * share[:, TILE:]).astype(BF16)
+
+
+FORWARD_LOADS = 7
+FORWARD_STORES = 16
+
+
+def forward_kernel(n, groups, rows_block, *refs):
+    (
+        inputs, memory, cotangent, *weights_in
+    ) = refs[: 3 + FORWARD_LOADS]
+    refs = refs[3 + FORWARD_LOADS :]
+    (
+        target_here, memory_here, in_bias, self_out_bias, first_gain, first_shift, cross_bias, cross_out_bias,
+        second_gain, second_shift, feed_bias, down_bias, last_gain, last_shift,
+    ) = refs[:14]
+    refs = refs[14:]
+    stores_out, refs = refs[:FORWARD_STORES], refs[FORWARD_STORES:]
+    (
+        layer_output, lse_one, lse_two, delta_ref, first_rstd, sums_out, in_bias_grad, target_row, memory_row,
+    ) = refs[:9]
+    refs = refs[9:]
+    held_weights, refs = refs[:FORWARD_LOADS], refs[FORWARD_LOADS:]
+    held_stores, refs = refs[:FORWARD_STORES], refs[FORWARD_STORES:]
+    (
+        self_in_weight, self_out_weight, cross_weight, pair_weight, cross_out_weight, in_weight, down_weight
+    ) = held_weights
+    (
+        input_pieces, memory_pieces, query_low, keys, values, attended_one, first_normal, first_low, cross_query,
+        cross_keys, cross_values, grad_out, g2_out, in_grad, down_grad, cross_out_grad,
+    ) = held_stores
+    (
+        cot, output_low, output_got, target_there, memory_there, wide, values_t, query_cols, held, held_low,
+        attended_two, second_normal, second_rstd, second_low, second_low_t, active, slope, third, branch,
+        load_sem, store_sem, own_sem, far_send, far_recv, core_send, core_recv,
+    ) = refs
+    count = inputs.shape[0]
+    tiles = count // TILE
+    blocks = count // rows_block
+    half = WIDE // n
+    group, part = lax.axis_index("dp"), lax.axis_index("blk")
+    place = lax.rem(group, 2)
+    away = place != part
+    owner = (group - place + part, place)
+    core_peer = (group + 1 - 2 * place, part)
+    mesh_type = pl.DeviceIdType.MESH
+
+    loads = [
+        pltpu.make_async_copy(source, target, load_sem.at[index])
+        for index, (source, target) in enumerate(zip(weights_in, held_weights))
+    ]
+    for load in loads:
+        load.start()
+    barrier = pltpu.get_barrier_semaphore()
+    pl.semaphore_signal(barrier, inc=1, device_id=core_peer, device_id_type=mesh_type)
+
+    @pl.when(away)
+    def _():
+        pl.semaphore_signal(barrier, inc=1, device_id=owner, device_id_type=mesh_type)
+
+    pl.semaphore_wait(barrier, jnp.where(away, 2, 1))
+
+    pieces_of = (count // 2, count // 2)
+    arrivals = []
+    for index, (source, target) in enumerate(((inputs, input_pieces), (memory, memory_pieces))):
+        for block in range(2):
+            rows = pl.ds(block * (count // 2), count // 2)
+            arrivals.append((source.at[rows], target.at[0, rows], 2 * index + block))
+    arrivals.append((cotangent, cot, 4))
+
+    def far_copy(entry):
+        source, target, sem = entry
+        return pltpu.make_async_remote_copy(
+            src_ref=source, dst_ref=target, send_sem=far_send.at[sem], recv_sem=far_recv.at[sem],
+            device_id=owner, device_id_type=mesh_type,
+        )
+
+    def own_copy(entry):
+        source, target, sem = entry
+        return pltpu.make_async_copy(source, target, own_sem.at[sem])
+
+    def core_copy(source, target, sem):
+        return pltpu.make_async_remote_copy(
+            src_ref=source, dst_ref=target, send_sem=core_send.at[sem], recv_sem=core_recv.at[sem],
+            device_id=core_peer, device_id_type=mesh_type,
+        )
+
+    @pl.when(away)
+    def _():
+        for entry in arrivals:
+            far_copy(entry).start()
+
+    @pl.when(jnp.logical_not(away))
+    def _():
+        for entry in arrivals:
+            own_copy(entry).start()
+
+    def arrive(entry):
+        @pl.when(away)
+        def _():
+            far_copy(entry).wait()
+
+        @pl.when(jnp.logical_not(away))
+        def _():
+            own_copy(entry).wait()
+
+    def forward_copy(index):
+        held_piece = (input_pieces, memory_pieces)[index // 2]
+        rows = pl.ds((index % 2) * (count // 2), count // 2)
+        return core_copy(held_piece.at[0, rows], held_piece.at[1, rows], index)
+
+    segment_copies = [
+        core_copy(target_here, target_there, 4), core_copy(memory_here, memory_there, 5)
+    ]
+    for copy in segment_copies:
+        copy.start()
+
+    stores = {}
+
+    def store(index):
+        stores[index] = pltpu.make_async_copy(held_stores[index], stores_out[index], store_sem.at[index])
+        stores[index].start()
+
+    for copy in segment_copies:
+        copy.wait()
+    target_row[...] = jnp.where(away, target_there[...], target_here[...])
+    memory_row[...] = jnp.where(away, memory_there[...], memory_here[...])
+    spread_row(target_row, wide)
+    loads[0].wait()
+
+    def project(piece, block, spot):
+        rows = slice(block * (count // 2), (block + 1) * (count // 2))
+        source = input_pieces[piece, rows, :]
+        here = dyn(spot * 2 + block, count // 2)
+        keys[here, :] = nn(source, self_in_weight[:, WIDE : 2 * WIDE]).astype(BF16)
+        value = (nn(source, self_in_weight[:, 2 * WIDE :]) + in_bias[1:2, :]).astype(BF16)
+        values[here, :] = value
+        values_t[:, here] = value.T
+        if piece == 0:
+            query = (nn(source, self_in_weight[:, :WIDE]) + in_bias[0:1, :]).astype(BF16)
+            query = (query.astype(F32) * SCALE).astype(BF16)
+            query_low[rows, :] = query
+            for tile in range(count // 2 // TILE):
+                split_columns(
+                    query[tile * TILE : (tile + 1) * TILE, :].T, query_cols, block * (count // 2 // TILE) + tile
+                )
+
+    for block in range(2):
+        arrive(arrivals[block])
+        forward_copy(block).start()
+        project(0, block, place)
+    for block in range(2):
+        forward_copy(block).wait()
+        project(1, block, 1 - place)
+    store(0)
+    store(2)
+    store(3)
+    store(4)
+    attend_whole(
+        tiles, target_row, place * count, wide, True, query_cols, keys, values_t, attended_one, lse_one,
+        held, held_low,
+    )
+    store(5)
+    for load in loads[1:4]:
+        load.wait()
+    for block in range(2):
+        arrive(arrivals[2 + block])
+        forward_copy(2 + block).start()
+
+    @pl.loop(0, blocks)
+    def _(block):
+        rows = dyn(block, rows_block)
+        attended = attended_one[:, rows].T
+        field = input_pieces[0, rows, :].astype(F32) + nn(attended, self_out_weight[...]) + self_out_bias[...]
+        normal, rstd = normalize(field)
+        first_normal[rows, :] = normal
+        first_rstd[rows, :] = rstd
+        low = (normal * first_gain[...] + first_shift[...]).astype(BF16)
+        first_low[rows, :] = low
+        query = (nn(low, cross_weight[...]) + cross_bias[0:1, :]).astype(BF16)
+        query = (query.astype(F32) * SCALE).astype(BF16)
+        cross_query[rows, :] = query
+        for tile in range(rows_block // TILE):
+            split_columns(
+                query[tile * TILE : (tile + 1) * TILE, :].T, query_cols, block * (rows_block // TILE) + tile
+            )
+
+    store(6)
+    store(7)
+    store(8)
+
+    def project_memory(piece, block, spot):
+        rows = slice(block * (count // 2), (block + 1) * (count // 2))
+        source = memory_pieces[piece, rows, :]
+        here = dyn(spot * 2 + block, count // 2)
+        cross_keys[here, :] = nn(source, pair_weight[:, :WIDE]).astype(BF16)
+        value = (nn(source, pair_weight[:, WIDE:]) + cross_bias[1:2, :]).astype(BF16)
+        cross_values[here, :] = value
+        values_t[:, here] = value.T
+
+    for block in range(2):
+        project_memory(0, block, place)
+    for block in range(2):
+        forward_copy(2 + block).wait()
+        project_memory(1, block, 1 - place)
+    store(1)
+    store(9)
+    store(10)
+    spread_row(memory_row, wide)
+    attend_whole(
+        tiles, target_row, place * count, wide, False, query_cols, cross_keys, values_t, attended_two, lse_two,
+        held, held_low,
+    )
+    for load in loads[4:]:
+        load.wait()
+
+    @pl.loop(0, blocks)
+    def _(block):
+        rows = dyn(block, rows_block)
+        attended = attended_two[:, rows].T
+        first = first_normal[rows, :] * first_gain[...] + first_shift[...]
+        field = first + nn(attended, cross_out_weight[...]) + cross_out_bias[...]
+        normal, rstd = normalize(field)
+        second_normal[rows, :] = normal
+        second_rstd[rows, :] = rstd
+        second = normal * second_gain[...] + second_shift[...]
+        third[rows, :] = second + down_bias[...]
+        low = second.astype(BF16)
+        second_low[rows, :] = low
+        second_low_t[:, rows] = low.T
+
+    chunks, chunk_size = in_weight.shape[1] // WIDE, WIDE
+    arrive(arrivals[4])
+
+    @pl.loop(0, chunks)
+    def _(chunk):
+        lanes = dyn(chunk, chunk_size)
+        hidden = nn(second_low[...], in_weight[:, lanes]) + feed_bias[:, lanes]
+        value, derivative = gate(hidden)
+        value = value.astype(BF16)
+        active[:, lanes] = value
+        slope[:, lanes] = derivative
+        third[...] += nn(value, down_weight[lanes, :])
+
+    sums_out[...] = jnp.zeros(sums_out.shape, F32)
+
+    @pl.loop(0, blocks)
+    def _(block):
+        rows = dyn(block, rows_block)
+        normal, rstd = normalize(third[rows, :])
+        output_low[rows, :] = (normal * last_gain[...] + last_shift[...]).astype(BF16)
+        outer = cot[rows, :].astype(F32)
+        grad = normalize_back(outer, last_gain[...], normal, rstd)
+        third[rows, :] = grad
+        low = grad.astype(BF16)
+        branch[rows, :] = low
+        sums_out[0:1, :] += col_sum(outer * normal)
+        sums_out[1:2, :] += col_sum(outer)
+        sums_out[2:3, :] += col_sum(low.astype(F32))
+
+    output_copy = (output_low, output_got, 5)
+
+    @pl.when(away)
+    def _():
+        far_copy(output_copy).start()
+
+    per_half = chunks // n
+
+    @pl.loop(0, chunks)
+    def _(chunk):
+        lanes = dyn(chunk, chunk_size)
+        share = tn(active[:, lanes], branch[...]).astype(BF16)
+        down_grad[lax.div(chunk, per_half), dyn(lax.rem(chunk, per_half), chunk_size), :] = share
+        inner = nt(branch[...], down_weight[lanes, :])
+        hidden_grad = (inner * slope[:, lanes]).astype(BF16)
+        in_bias_grad[:, lanes] = col_sum(hidden_grad.astype(F32))
+        third[...] += nt(hidden_grad, in_weight[:, lanes])
+        share = nn(second_low_t[...], hidden_grad).astype(BF16)
+        for b in range(n):
+            in_grad[b, dyn(chunk, half), :] = share[b * half : (b + 1) * half, :]
+
+    store(13)
+    store(14)
+
+    @pl.loop(0, blocks)
+    def _(block):
+        rows = dyn(block, rows_block)
+        outer = third[rows, :]
+        normal = second_normal[rows, :]
+        grad = normalize_back(outer, second_gain[...], normal, second_rstd[rows, :])
+        g2_out[rows, :] = grad
+        low = grad.astype(BF16)
+        branch[rows, :] = low
+        sums_out[3:4, :] += col_sum(outer * normal)
+        sums_out[4:5, :] += col_sum(outer)
+        sums_out[5:6, :] += col_sum(low.astype(F32))
+        grad_out[rows, :] = nt(low, cross_out_weight[...]).astype(BF16)
+
+    store(11)
+    store(12)
+    spread_parts(n, nn(attended_two[...], branch[...]), cross_out_grad, 0)
+    store(15)
+    write_delta(tiles, grad_out, attended_two, delta_ref)
+
+    @pl.when(away)
+    def _():
+        far_copy(output_copy).wait()
+        layer_output[...] = output_got[...]
+
+    @pl.when(jnp.logical_not(away))
+    def _():
+        layer_output[...] = output_low[...]
+
+    for index in range(FORWARD_STORES):
+        stores[index].wait()
+
+
+def forward_all(n, groups, rows_block, activations, weights, resident):
+    count, features = activations[0].shape
+    length = n * count
+    hidden = weights[5].shape[1]
+    half = features // n
+    vm = pl.BlockSpec(memory_space=pltpu.VMEM)
+    hbm = pl.BlockSpec(memory_space=pl.ANY)
+    low, wide, every = (count, features), (count, features), (length, features)
+    stored = [
+        ((2, *low), BF16), ((2, *low), BF16), (low, BF16), (every, BF16), (every, BF16), ((features, count), BF16),
+        (wide, F32), (low, BF16), (low, BF16), (every, BF16), (every, BF16), (low, BF16), (wide, F32),
+        ((n, hidden // n, features), BF16), ((n, hidden // n, features), BF16), ((n, half, features), BF16),
+    ]
+    stats = out_like((features // PAIR, 2 * count), F32)
+    row_like = out_like((1, length), jnp.int32)
+    row_scratch = pltpu.VMEM((1, length), jnp.int32)
+    held = (features // PAIR, length, 2 * TILE)
+    low_rows, wide_rows = pltpu.VMEM(low, BF16), pltpu.VMEM(wide, F32)
+    return pl.pallas_call(
+        functools.partial(forward_kernel, n, groups, rows_block),
+        in_specs=[hbm] * (len(activations) + len(weights)) + [vm] * len(resident),
+        out_specs=[hbm] * len(stored) + [vm] * 9,
+        out_shape=[out_like(*entry) for entry in stored] + [
+            out_like(low, BF16), stats, stats, stats, out_like((count, 1), F32), out_like((8, features), F32),
+            out_like((1, hidden), F32), row_like, row_like,
+        ],
+        scratch_shapes=[
+            *[pltpu.VMEM(weight.shape, weight.dtype) for weight in weights],
+            *[pltpu.VMEM(*entry) for entry in stored],
+            low_rows, low_rows, low_rows, row_scratch, row_scratch,
+            pltpu.VMEM((length, TILE), jnp.int32), pltpu.VMEM((features, length), BF16),
+            pltpu.VMEM((features, 2 * count), BF16), pltpu.VMEM(held, F32), pltpu.VMEM(held, BF16),
+            pltpu.VMEM((features, count), BF16), wide_rows, pltpu.VMEM((count, 1), F32), low_rows,
+            pltpu.VMEM((features, count), BF16), pltpu.VMEM((count, hidden), BF16),
+            pltpu.VMEM((count, hidden), F32), wide_rows, low_rows,
+            pltpu.SemaphoreType.DMA((len(weights),)), pltpu.SemaphoreType.DMA((len(stored),)),
+            pltpu.SemaphoreType.DMA((5,)), pltpu.SemaphoreType.DMA((6,)), pltpu.SemaphoreType.DMA((6,)),
+            pltpu.SemaphoreType.DMA((6,)), pltpu.SemaphoreType.DMA((6,)),
+        ],
+        compiler_params=pltpu.CompilerParams(
+            vmem_limit_bytes=VMEM_LIMIT, collective_id=1, has_side_effects=True
+        ),
+    )(*activations, *weights, *resident)
+
+
 def widen_kernel(plan, source, *outs):
     for out, (start, columns) in zip(outs, plan):
         height = out.shape[0]
@@ -1217,23 +1667,23 @@
     return jnp.stack([low // TILE, (high + TILE - 1) // TILE]).astype(jnp.int32)
 
 
-def on_device(
-    n, groups,
-    inputs, memory, cotangent, target_segments, memory_segments,
+def apart(
+    n, groups, rows_block, input_rows, memory_rows, cotangent_rows, target_segments, memory_segments,
     self_in_weight, self_in_bias, self_out_weight, self_out_bias, first_gain, first_shift,
     cross_query_weight, cross_pair_weight, cross_bias, cross_out_weight, cross_out_bias,
     second_gain, second_shift, feed_in_weight, feed_in_bias, feed_out_weight, feed_out_bias,
     third_gain, third_shift,
 ):
-    input_rows, memory_rows, cotangent_rows = inputs[0], memory[0], cotangent[0]
     count, features = input_rows.shape
     length = n * count
     hidden = feed_in_weight.shape[1]
-    rows_block = min(count, 256)
     tiles = count // TILE
     half = features // n
     place = lax.axis_index("blk").astype(jnp.int32)
 
+    def row(vector):
+        return vector[None, :]
+
     def shifted(field, step):
         return lax.ppermute(field, "blk", [(s, (s + step) % n) for s in range(n)])
 
@@ -1242,9 +1692,7 @@
 
     input_pieces = [input_rows] + [shifted(input_rows, step) for step in range(1, n)]
     memory_pieces = [memory_rows] + [shifted(memory_rows, step) for step in range(1, n)]
-
-    target_row = target_segments[0]
-    source_row = memory_segments[0]
+    target_row, source_row = target_segments[0], memory_segments[0]
     target_here = lax.dynamic_slice_in_dim(target_row, place * count, count, 0)
     self_ranges = key_ranges(
         target_here, target_row, tiles, place * count + TILE * (1 + jnp.arange(tiles, dtype=jnp.int32))
@@ -1254,9 +1702,6 @@
     query_segment = target_here[None, :]
     target_column = target_row[:, None]
     source_column = source_row[:, None]
-
-    def row(vector):
-        return vector[None, :]
 
     stats = out_like((WIDE // PAIR, 2 * count), F32)
     low_rows = out_like((count, features), BF16)
@@ -1310,72 +1755,115 @@
         50 * square, 20 << 20,
     )
 
-    if length <= 1024 and half % TILE == 0:
+    back_scratch = [
+        wide_scratch, values_t, query_cols, query_rows, query_cols, query_rows,
+        pltpu.VMEM((features, count), F32), pltpu.VMEM((length, features), F32),
+        pltpu.VMEM((length, features), F32), held, held_low, held_low, pltpu.VMEM((count, features), BF16),
+    ]
+    sent_like = out_like((max(n - 1, 1), count, features), BF16)
+    (
+        memory_own, memory_sent, cross_query_grad, cross_pair_grad, self_out_grad, self_grad,
+        self_delta, g1, cross_sums,
+    ) = run(
+        functools.partial(cross_backward, n, rows_block),
+        [place_one, cross_ranges, *memory_pieces, query_segment, source_column, cross_query,
+         cross_grad, cross_keys, cross_values, cross_lse, cross_delta, g2, normal, rstd, first_low,
+         row(first_gain), cross_query_weight, cross_pair_weight, self_out_weight, attended_t],
+        2,
+        [wide_rows, sent_like, out_like((n, half, features), BF16),
+         out_like((n, 2 * half, features), BF16), out_like((n, half, features), BF16), low_rows,
+         stats, wide_rows, out_like((8, features), F32)],
+        back_scratch + [pltpu.VMEM((count, features), BF16)],
+        30 * square, 15 << 20,
+    )
+    (input_own, input_sent, self_in_grad, self_sums) = run(
+        functools.partial(self_backward, n, rows_block),
+        [place_one, self_ranges, *input_pieces, query_segment, target_column, query, self_grad,
+         keys, values, lse, self_delta, g1, self_in_weight],
+        2,
+        [wide_rows, sent_like, out_like((n, 3 * half, features), BF16), out_like((8, features), F32)],
+        back_scratch,
+        30 * square, 15 << 20,
+    )
+
+    memory_grad, input_grad = memory_own, input_own
+    for step in range(1, n):
+        memory_grad = memory_grad + shifted_back(memory_sent[step - 1], step).astype(F32)
+        input_grad = input_grad + shifted_back(input_sent[step - 1], step).astype(F32)
+
+    vectors = jnp.concatenate([self_sums[:2], cross_sums[:5], feed_sums[:6]], axis=0)
+    count_small = vectors.shape[0]
+    small = jnp.concatenate(
+        [
+            jnp.transpose(vectors.reshape(count_small, n, half), (1, 0, 2)).reshape(n, -1),
+            in_bias_grad.reshape(n, -1),
+        ],
+        axis=1,
+    )
+    amount = small.shape[1]
+    small_rows = -(-amount // (8 * WIDE)) * 8
+    small = jnp.pad(small, ((0, 0), (0, small_rows * WIDE - amount))).reshape(n, small_rows, WIDE)
+    packed, small = reduce_all(
+        n, groups,
+        [in_grad, down_grad, cross_out_grad, cross_query_grad, cross_pair_grad, self_out_grad, self_in_grad],
+        small,
+    )
+    small = small.reshape(-1)[:amount]
+    return packed, small, memory_grad, input_grad, layer_output, count_small
+
+
+def on_device(
+    n, groups,
+    inputs, memory, cotangent, target_segments, memory_segments,
+    self_in_weight, self_in_bias, self_out_weight, self_out_bias, first_gain, first_shift,
+    cross_query_weight, cross_pair_weight, cross_bias, cross_out_weight, cross_out_bias,
+    second_gain, second_shift, feed_in_weight, feed_in_bias, feed_out_weight, feed_out_bias,
+    third_gain, third_shift,
+):
+    input_rows, memory_rows, cotangent_rows = inputs[0], memory[0], cotangent[0]
+    count, features = input_rows.shape
+    length = n * count
+    hidden = feed_in_weight.shape[1]
+    rows_block = min(count, 256)
+    tiles = count // TILE
+    half = features // n
+    near = n == 2 and groups % 4 == 0 and length <= 1024 and half % TILE == 0
+
+    def row(vector):
+        return vector[None, :]
+
+    if near:
+        (
+            input_pieces, memory_pieces, query, keys, values, attended_t, normal, first_low, cross_query,
+            cross_keys, cross_values, cross_grad, g2, in_grad, down_grad, cross_out_grad,
+            layer_output, lse, cross_lse, cross_delta, rstd, feed_sums, in_bias_grad, target_row, memory_row,
+        ) = forward_all(
+            n, groups, rows_block,
+            [input_rows, memory_rows, cotangent_rows],
+            [self_in_weight, self_out_weight, cross_query_weight, cross_pair_weight, cross_out_weight,
+             feed_in_weight, feed_out_weight],
+            [target_segments, memory_segments, self_in_bias, row(self_out_bias), row(first_gain),
+             row(first_shift), cross_bias, row(cross_out_bias), row(second_gain), row(second_shift),
+             row(feed_in_bias), row(feed_out_bias), row(third_gain), row(third_shift)],
+        )
         packed, small, memory_grad, input_grad = back_and_reduce(
             n, groups, rows_block,
             [in_grad, down_grad, cross_out_grad],
-            [*memory_pieces, cross_pair_weight, first_low, cross_query_weight, g2, normal, self_out_weight,
-             attended_t, keys, values, query, *input_pieces, self_in_weight],
-            [query_segment, source_column, target_column, cross_query, cross_grad, cross_keys, cross_values,
+            [memory_pieces, cross_pair_weight, first_low, cross_query_weight, g2, normal, self_out_weight,
+             attended_t, keys, values, query, input_pieces, self_in_weight],
+            [target_row, memory_row, cross_query, cross_grad, cross_keys, cross_values,
              cross_lse, cross_delta, feed_sums, in_bias_grad, row(first_gain), rstd, lse],
         )
         count_small = 13
         small = small.reshape(-1)[: count_small * half + hidden // n]
     else:
-        back_scratch = [
-            wide_scratch, values_t, query_cols, query_rows, query_cols, query_rows,
-            pltpu.VMEM((features, count), F32), pltpu.VMEM((length, features), F32),
-            pltpu.VMEM((length, features), F32), held, held_low, held_low, pltpu.VMEM((count, features), BF16),
-        ]
-        sent_like = out_like((max(n - 1, 1), count, features), BF16)
-        (
-            memory_own, memory_sent, cross_query_grad, cross_pair_grad, self_out_grad, self_grad,
-            self_delta, g1, cross_sums,
-        ) = run(
-            functools.partial(cross_backward, n, rows_block),
-            [place_one, cross_ranges, *memory_pieces, query_segment, source_column, cross_query,
-             cross_grad, cross_keys, cross_values, cross_lse, cross_delta, g2, normal, rstd, first_low,
-             row(first_gain), cross_query_weight, cross_pair_weight, self_out_weight, attended_t],
-            2,
-            [wide_rows, sent_like, out_like((n, half, features), BF16),
-             out_like((n, 2 * half, features), BF16), out_like((n, half, features), BF16), low_rows,
-             stats, wide_rows, out_like((8, features), F32)],
-            back_scratch + [pltpu.VMEM((count, features), BF16)],
-            30 * square, 15 << 20,
+        packed, small, memory_grad, input_grad, layer_output, count_small = apart(
+            n, groups, rows_block, input_rows, memory_rows, cotangent_rows, target_segments, memory_segments,
+            self_in_weight, self_in_bias, self_out_weight, self_out_bias, first_gain, first_shift,
+            cross_query_weight, cross_pair_weight, cross_bias, cross_out_weight, cross_out_bias,
+            second_gain, second_shift, feed_in_weight, feed_in_bias, feed_out_weight, feed_out_bias,
+            third_gain, third_shift,
         )
-        (input_own, input_sent, self_in_grad, self_sums) = run(
-            functools.partial(self_backward, n, rows_block),
-            [place_one, self_ranges, *input_pieces, query_segment, target_column, query, self_grad,
-             keys, values, lse, self_delta, g1, self_in_weight],
-            2,
-            [wide_rows, sent_like, out_like((n, 3 * half, features), BF16), out_like((8, features), F32)],
-            back_scratch,
-            30 * square, 15 << 20,
-        )
-
-        memory_grad, input_grad = memory_own, input_own
-        for step in range(1, n):
-            memory_grad = memory_grad + shifted_back(memory_sent[step - 1], step).astype(F32)
-            input_grad = input_grad + shifted_back(input_sent[step - 1], step).astype(F32)
-
-        vectors = jnp.concatenate([self_sums[:2], cross_sums[:5], feed_sums[:6]], axis=0)
-        count_small = vectors.shape[0]
-        small = jnp.concatenate(
-            [
-                jnp.transpose(vectors.reshape(count_small, n, half), (1, 0, 2)).reshape(n, -1),
-                in_bias_grad.reshape(n, -1),
-            ],
-            axis=1,
-        )
-        amount = small.shape[1]
-        small_rows = -(-amount // (8 * WIDE)) * 8
-        small = jnp.pad(small, ((0, 0), (0, small_rows * WIDE - amount))).reshape(n, small_rows, WIDE)
-        packed, small = reduce_all(
-            n, groups,
-            [in_grad, down_grad, cross_out_grad, cross_query_grad, cross_pair_grad, self_out_grad, self_in_grad],
-            small,
-        )
-        small = small.reshape(-1)[:amount]
     plan = []
     start = 0
     shapes = []

time: 191 us -> 155 us (0.81)
  waiting for transfers between devices: 16.8 us -> 0 us
  Pallas kernels: 156 us -> 147 us
  local copies, waits for them, and re-layouts: 12 us -> 6.91 us
  starting transfers between devices: 3.08 us -> 0 us
  other arithmetic: 2.11 us -> 0 us
    pallas_call x0 -> x1, Pallas kernels: none -> 48.2 us  [forward_all(): pl.pallas_call(functools.partial(forward_kernel, n, groups, rows_block),...]
    pallas_call x3 -> x1, Pallas kernels: 53 us -> 5.78 us  [run(): pl.pallas_call(body, in_specs=[sm] * smem_count + [vm] * (len(ins) - smem...]
    ppermute x2 -> x0, waiting for transfers between devices: 16.8 us -> none  [shifted(): return lax.ppermute(field, 'blk', [(s, (s + step) % n) for s in range(n)])]
    pallas_call x1, Pallas kernels: 103 us -> 92.8 us  [back_and_reduce(): pl.pallas_call(functools.partial(back_kernel, n, groups, rows_block, chun...]
    another operation x2 -> x0, local copies, waits for them, and re-layouts: 3.46 us -> none  [the longest x1 1.76 us: on_device(): target_column = target_row[:, None]]
    ppermute x2 -> x0, starting transfers between devices: 3.08 us -> none  [shifted(): return lax.ppermute(field, 'blk', [(s, (s + step) % n) for s in range(n)])]
    unnamed x14 -> x11, local copies, waits for them, and re-layouts: 4.84 us -> 4.06 us
  transfers between devices with their start and end apart: 2 -> 0, of which waited for: 1 -> 0; matrix products, arithmetic and copies ran while one was open for 3% -> 0% of each run, Pallas kernels for 6% -> 0%
where the time goes in v3:
time: 155 us; the launch traced here: 154 us
  Pallas kernels  147 us (95%)
  local copies, waits for them, and re-layouts  6.91 us (4%)
    pallas_call x1, Pallas kernels, back_and_reduce(): pl.pallas_call(functools.partial(back_kernel, n, groups, rows_block, chun...  92.8 us
    pallas_call x1, Pallas kernels, forward_all(): pl.pallas_call(functools.partial(forward_kernel, n, groups, rows_block),...  48.2 us
    pallas_call x1, Pallas kernels, run(): pl.pallas_call(body, in_specs=[sm] * smem_count + [vm] * (len(ins) - smem...  5.78 us
    unnamed x11, local copies, waits for them, and re-layouts  4.06 us

profile of v3, /device:TPU:0, one launch (start us, length us, event | category | flops | bytes accessed | tf_op | source)
XLA Modules:
  0.0 154.4 jit_solution(5179408972644747878)
XLA Ops:
  0.7 48.2 %shard_map.399 = (bf16[2,512,512]{2,1,0:T(8,128)(2,1)}, bf16[2,512,512]{2,1,0:T(8,128)(2,1)}, bf16[512,512]{1,0:T(8,128)(2,1)}, bf16[1024,512]{1,0:T(8,128)(2,1)...) custom-call(bf16[512,512]{1,0:T(8,128)(2,1)} %bitcast.30, ...), custom_call_target="tpu_custom_call" | custom-call | tf_op jit(solution)/shard_map/pallas_call | solution.py:1625
  48.9 92.8 %shard_map.400 = (bf16[4096,512]{1,0:T(8,128)(2,1)}, f32[32,256]{1,0:T(8,128)}, f32[512,512]{1,0:T(8,128)}, f32[512,512]{1,0:T(8,128)}) custom-call(bf16[2,1024,512]{2,1,0:T(8,128)(2,1)} %get-tuple-element.59.refs_0_, bf16[2,1024,512]{2,1,0:T(8,128)(2,1)} %get-tuple-element.60.refs_1_, bf16[2,256,512]{2,1,0:T(8,128)(2,1)} %get-tuple-element.61.refs_2_, ...), custom_call_target="tpu_custom_call" | custom-call | tf_op jit(solution)/shard_map/pallas_call | solution.py:1220
  141.7 0.7 slice_bitcast_fusion
  142.5 0.6 copy.46
  143.1 1.4 fusion.1
  144.4 1.5 fusion
  145.9 0.0 copy-start.2
  145.9 0.0 copy-start.1
  145.9 5.8 %shard_map.401 = (f32[256,2048]{1,0:T(8,128)}, f32[1024,512]{1,0:T(8,128)}, f32[256,512]{1,0:T(8,128)}, f32[256,512]{1,0:T(8,128)}, f32[256,1024]{1,0:T(8,128)},...) custom-call(bf16[4096,512]{1,0:T(8,128)(2,1)} %get-tuple-element.85.source), custom_call_target="tpu_custom_call" | custom-call | bytes 12582912 | tf_op jit(solution)/shard_map/pallas_call | solution.py:234
  151.7 0.0 copy-start
  151.7 0.0 copy-done.2
  151.7 0.8 copy.50
  152.5 0.0 copy-done.1
  152.5 1.0 copy.51
  153.5 0.0 copy-done
  153.5 1.0 copy.52
Async XLA Ops:
  145.9 5.8 %copy-start.2 = (bf16[512,512]{1,0:T(8,128)(2,1)S(1)}, bf16[512,512]{1,0:T(8,128)(2,1)}, u32[]{:S(2)}) copy-start(bf16[512,512]{1,0:T(8,128)(2,1)} %get-tuple-element.58) | copy-start | bytes 1572868
  145.9 6.6 %copy-start.1 = (f32[512,512]{1,0:T(8,128)S(1)}, f32[512,512]{1,0:T(8,128)}, u32[]{:S(2)}) copy-start(f32[512,512]{1,0:T(8,128)} %get-tuple-element.83) | copy-start | bytes 3145732
  151.7 1.8 %copy-start = (f32[512,512]{1,0:T(8,128)S(1)}, f32[512,512]{1,0:T(8,128)}, u32[]{:S(2)}) copy-start(f32[512,512]{1,0:T(8,128)} %get-tuple-element.84) | copy-start | bytes 3145732

commit v4 on v3

--- a/solution.py
+++ b/solution.py
@@ -626,8 +626,8 @@
 
 CORE_RATE = 0.0018
 LINK_RATE = 0.0225
-LATENCY = {"core": 1.1, "x": 2.4, "y": 2.4, "z": 3.0}
-MARGIN = 1.0
+LATENCY = {"core": 1.0, "x": 2.2, "y": 2.2, "z": 2.6}
+MARGIN = 0.5
 
 
 def plan_steps(n, chunks, extras, segments):
@@ -669,7 +669,8 @@
         else:
             if step == 4:
                 return
-            ready = now + (1.5, 3.2, 3.2, 4.0)[step]
+            link, rows = (("core", 64), ("x", 32), ("y", 32), ("z", 128))[step]
+            ready = send(link, rows, CORE_RATE if link == "core" else LINK_RATE)
         pending.append((ready, len(pending), kind, index, step + 1))
 
     for number in range(len(segments) + 1):
@@ -721,7 +722,7 @@
         self.z_peers = [(lax.rem(group + 4 * step, groups), part) for step in range(1, depth)]
         self.per_chunk = 4 + (n - 1) + 2 * (depth - 1)
 
-    def enter(self, far_peer=None, has_far=None):
+    def greet(self, far_peer=None, has_far=None):
         peers = [self.core_peer, self.side_peer] + self.blk_peers + self.z_peers
         barrier = pltpu.get_barrier_semaphore()
         for peer in peers:
@@ -732,9 +733,12 @@
             def _():
                 pl.semaphore_signal(barrier, inc=1, device_id=far_peer, device_id_type=pl.DeviceIdType.MESH)
 
-            pl.semaphore_wait(barrier, jnp.where(has_far, len(peers) + 1, len(peers)))
+            self.greetings = jnp.where(has_far, len(peers) + 1, len(peers))
         else:
-            pl.semaphore_wait(barrier, len(peers))
+            self.greetings = len(peers)
+
+    def enter(self):
+        pl.semaphore_wait(pltpu.get_barrier_semaphore(), self.greetings)
 
     def copy(self, source, target, sem, peer):
         return pltpu.make_async_remote_copy(
@@ -937,6 +941,7 @@
         start += part_rows[index]
     reducer = Reducer(n, groups, chunks, field, total, total_out, small, small_out, refs[7:])
     small[0] = small_in[...]
+    reducer.greet()
     reducer.enter()
     for load in loads:
         load.wait()
@@ -976,15 +981,14 @@
     )(*parts, small)
 
 
-Y_FIRST = [letter == "y" for letter in "yyxyxyxyxxyy"]
+Y_FIRST = [letter == "y" for letter in "yxxyyxyyyyyyyxxx"]
 BACK_SEGMENTS = [
-    3.5, 3.2, 3.2, 3.2, 3.2, 1.5, 3.0, 3.5,
-    2.5, 2.6, 2.6, 3.2, 3.2, 1.5, 1.2, 1.2, 2.4, 2.2,
+    3.2, 2.9, 2.9, 2.9, 2.9, 1.4, 2.8, 3.2, 2.3, 2.4, 2.4, 2.9, 2.9, 1.4, 1.1, 1.1, 2.2, 2.0,
 ]
 
 
 def back_chunks(half, hidden_rows):
-    released = [(2 * half, 0)] * (hidden_rows // half) + [(half, 0)]
+    released = [(half, 0)] * (2 * hidden_rows // half + 1)
     released += [(half, segment) for segment in (5, 6, 6, 7, 13, 14, 15)]
     chunks = []
     start = 0
@@ -1000,13 +1004,13 @@
     (
         target_row, memory_row, cross_query, cross_grad, cross_keys, cross_values,
         cross_lse, cross_delta, feed_sums, in_bias_grad, gain, first_rstd, self_lse,
-        total_out, small_out, memory_grad, input_grad,
-        field, total, small, sums, memory_sent, memory_got, input_sent, input_got, pair_low,
+        total_out, small_out, memory_out, input_out,
+        field, total, small, sums, memory_grad, input_grad, memory_sent, memory_got, input_sent, input_got, pair_low,
         wide, keys_t, query_cols, query_rows, grad_cols, grad_rows, query_grad_t, key_grad, value_grad,
         held, held_low, held_grad, query_low, branch, self_grad, self_delta, g1,
-        feed_sem, load_sem, extra_send, extra_recv,
-    ) = refs[:47]
-    refs = refs[47:]
+        feed_sem, load_sem, extra_send, extra_recv, extra_store,
+    ) = refs[:50]
+    refs = refs[50:]
     held_loads, buffers = refs[: len(load_plan)], refs[len(load_plan) :]
     count = cross_query.shape[0]
     length = cross_keys.shape[0]
@@ -1043,20 +1047,26 @@
     self_in_weight = held_loads[11]
 
     reducer = Reducer(n, groups, chunks, field, total, total_out, small, small_out, buffers)
-    reducer.enter(owner, away)
-
-    extras = ((memory_sent, memory_got, memory_grad), (input_sent, input_got, input_grad))
+    reducer.greet(owner, away)
+
+    extras = (
+        (memory_sent, memory_got, memory_grad, memory_out), (input_sent, input_got, input_grad, input_out)
+    )
 
     def extra_copy(index, hop):
-        sent, got, unused = extras[index]
+        sent, got, *unused = extras[index]
         return pltpu.make_async_remote_copy(
             src_ref=sent.at[hop], dst_ref=got.at[hop],
             send_sem=extra_send.at[2 * index + hop], recv_sem=extra_recv.at[2 * index + hop],
             device_id=reducer.core_peer if hop == 0 else owner, device_id_type=pl.DeviceIdType.MESH,
         )
 
+    def extra_store_copy(index, from_owner):
+        sent, got, unused, out = extras[index]
+        return pltpu.make_async_copy((got if from_owner else sent).at[1], out, extra_store.at[index])
+
     def extra_step(index, step):
-        sent, got, result = extras[index]
+        sent, got, result, unused = extras[index]
         if step == 0:
             extra_copy(index, 0).start()
         elif step == 1:
@@ -1066,22 +1076,21 @@
             def _(block):
                 rows = dyn(block, rows_block)
                 value = result[rows, :] + got[0, rows, :].astype(F32)
-                result[rows, :] = value
                 sent[1, rows, :] = value.astype(BF16)
 
             @pl.when(away)
             def _():
                 extra_copy(index, 1).start()
+
+            @pl.when(jnp.logical_not(away))
+            def _():
+                extra_store_copy(index, False).start()
         else:
 
             @pl.when(away)
             def _():
                 extra_copy(index, 1).wait()
-
-                @pl.loop(0, blocks)
-                def _(block):
-                    rows = dyn(block, rows_block)
-                    result[rows, :] = got[1, rows, :].astype(F32)
+                extra_store_copy(index, True).start()
 
     def run_steps(number):
         for kind, index, step in plan[number]:
@@ -1105,6 +1114,7 @@
     sums[...] = jnp.zeros(sums.shape, F32)
     for load in feed_loads:
         load.wait()
+    reducer.enter()
     run_steps(0)
     for tile in range(tiles):
         attend_back(
@@ -1195,6 +1205,16 @@
 
     run_steps(17)
     run_steps(18)
+    for index in range(2):
+
+        @pl.when(away)
+        def _():
+            extra_store_copy(index, True).wait()
+
+        @pl.when(jnp.logical_not(away))
+        def _():
+            extra_store_copy(index, False).wait()
+
     reducer.finish()
 
 
@@ -1220,22 +1240,22 @@
     return pl.pallas_call(
         functools.partial(back_kernel, n, groups, rows_block, chunks, plan, [part.shape for part in streamed]),
         in_specs=[hbm] * (len(feed_grads) + len(streamed)) + [vm] * len(resident),
-        out_specs=[hbm, vm, vm, vm],
+        out_specs=[hbm, vm, hbm, hbm],
         out_shape=[
             out_like((rows, WIDE), BF16), out_like(small_shape, F32),
-            out_like((count, features), F32), out_like((count, features), F32),
+            out_like((count, features), BF16), out_like((count, features), BF16),
         ],
         scratch_shapes=[
             pltpu.VMEM((n, rows, WIDE), BF16), pltpu.VMEM((rows, WIDE), BF16),
             pltpu.VMEM((2, n, *small_shape), F32), pltpu.VMEM((8, features), F32),
-            sent, sent, sent, sent, pltpu.VMEM((2, length, features), BF16),
+            wide_rows, wide_rows, sent, sent, sent, sent, pltpu.VMEM((2, length, features), BF16),
             pltpu.VMEM((length, TILE), jnp.int32), pltpu.VMEM((features, length), BF16),
             columns, doubled, columns, doubled,
             pltpu.VMEM((features, count), F32), all_wide, all_wide,
             pltpu.VMEM(held, F32), pltpu.VMEM(held, BF16), pltpu.VMEM(held, BF16),
             low_rows, low_rows, low_rows, pltpu.VMEM((features // PAIR, 2 * count), F32), wide_rows,
             pltpu.SemaphoreType.DMA((len(feed_grads),)), pltpu.SemaphoreType.DMA((len(streamed),)),
-            pltpu.SemaphoreType.DMA((4,)), pltpu.SemaphoreType.DMA((4,)),
+            pltpu.SemaphoreType.DMA((4,)), pltpu.SemaphoreType.DMA((4,)), pltpu.SemaphoreType.DMA((2,)),
             *[pltpu.VMEM(part.shape, part.dtype) for part in streamed],
             *reducer_scratch(n, groups, chunks, rows, small_shape),
         ],
@@ -1658,6 +1678,103 @@
             ].astype(F32)
 
 
+def finish_kernel(plan, packed, *refs):
+    count = len(plan)
+    input_low, memory_low, output_low, small, *refs = refs
+    (
+        *weights, input_grad, memory_grad, layer_output, self_bias, cross_bias, feed_bias,
+    ) = refs[: count + 6]
+    refs = refs[count + 6 :]
+    vectors, refs = refs[:9], refs[9:]
+    held, refs = refs[:count], refs[count:]
+    wide, refs = refs[:count], refs[count:]
+    input_held, memory_held, output_held, input_wide, memory_wide, load_sem, store_sem = refs
+
+    def load(index):
+        start, columns = plan[index]
+        return pltpu.make_async_copy(
+            packed.at[pl.ds(start, held[index].shape[0])], held[index], load_sem.at[index]
+        )
+
+    extra = [
+        pltpu.make_async_copy(input_low, input_held, load_sem.at[count]),
+        pltpu.make_async_copy(memory_low, memory_held, load_sem.at[count + 1]),
+    ]
+    output = pltpu.make_async_copy(output_low, output_held, load_sem.at[count + 2])
+    loads = [load(index) for index in range(count)]
+    for copy in loads + extra + [output]:
+        copy.start()
+    stores = [pltpu.make_async_copy(output_held, layer_output, store_sem.at[count + 2])]
+    output.wait()
+    stores[0].start()
+    for index, (start, columns) in enumerate(plan):
+        loads[index].wait()
+        height = wide[index].shape[0]
+
+        @pl.loop(0, height // 64)
+        def _(block):
+            for column in range(columns):
+                here = pl.ds(pl.multiple_of(column * height + block * 64, 64), 64)
+                wide[index][dyn(block, 64), column * WIDE : (column + 1) * WIDE] = held[index][here, :].astype(F32)
+
+        stores.append(pltpu.make_async_copy(wide[index], weights[index], store_sem.at[index]))
+        stores[-1].start()
+    for index, (source, target, result) in enumerate(
+        ((input_held, input_wide, input_grad), (memory_held, memory_wide, memory_grad))
+    ):
+        extra[index].wait()
+
+        @pl.loop(0, target.shape[0] // 128)
+        def _(block):
+            target[dyn(block, 128), :] = source[dyn(block, 128), :].astype(F32)
+
+        stores.append(pltpu.make_async_copy(target, result, store_sem.at[count + index]))
+        stores[-1].start()
+    self_bias[...] = small[0:2, :]
+    cross_bias[...] = small[2:4, :]
+    for index, vector in enumerate(vectors):
+        vector[...] = small[4 + index, :]
+    half = small.shape[1]
+    for row in range(feed_bias.shape[0] // half):
+        feed_bias[row * half : (row + 1) * half] = small[13 + row, :]
+    for copy in stores:
+        copy.wait()
+
+
+def finish_all(n, packed, small, input_low, memory_low, layer_output, hidden):
+    count, features = input_low.shape
+    half = features // n
+    plan, shapes, parts = [], [], []
+    start = 0
+    for height, columns in (
+        (half, hidden // features), (hidden // n, 1), (half, 1), (half, 1), (half, 2), (half, 1), (half, 3)
+    ):
+        plan.append((start, columns))
+        parts.append((height * columns, features))
+        shapes.append((height, columns * features))
+        start += height * columns
+    vm = pl.BlockSpec(memory_space=pltpu.VMEM)
+    hbm = pl.BlockSpec(memory_space=pl.ANY)
+    wide = (count, features)
+    return pl.pallas_call(
+        functools.partial(finish_kernel, plan),
+        in_specs=[hbm] * 4 + [vm],
+        out_specs=[hbm] * (len(plan) + 3) + [vm] * 12,
+        out_shape=[out_like(shape, F32) for shape in shapes] + [
+            out_like(wide, F32), out_like(wide, F32), out_like(wide, BF16),
+            out_like((2, half), F32), out_like((2, half), F32), out_like((hidden // n,), F32),
+        ] + [out_like((half,), F32)] * 9,
+        scratch_shapes=[pltpu.VMEM(shape, BF16) for shape in parts]
+        + [pltpu.VMEM(shape, F32) for shape in shapes]
+        + [
+            pltpu.VMEM(wide, BF16), pltpu.VMEM(wide, BF16), pltpu.VMEM(wide, BF16), pltpu.VMEM(wide, F32),
+            pltpu.VMEM(wide, F32),
+            pltpu.SemaphoreType.DMA((len(plan) + 3,)), pltpu.SemaphoreType.DMA((len(plan) + 3,)),
+        ],
+        compiler_params=pltpu.CompilerParams(vmem_limit_bytes=VMEM_LIMIT),
+    )(packed, input_low, memory_low, layer_output, small)
+
+
 def key_ranges(query_segment, key_segment, tiles, limit):
     edges = query_segment.reshape(tiles, TILE)
     low = jnp.sum((key_segment[None, :] < edges[:, :1]).astype(jnp.int32), axis=1)
@@ -1854,8 +1971,13 @@
             [target_row, memory_row, cross_query, cross_grad, cross_keys, cross_values,
              cross_lse, cross_delta, feed_sums, in_bias_grad, row(first_gain), rstd, lse],
         )
-        count_small = 13
-        small = small.reshape(-1)[: count_small * half + hidden // n]
+        (
+            feed_in_grad, feed_out_grad, cross_out_total, cross_query_total, cross_pair_total,
+            self_out_total, self_in_total, input_grad, memory_grad, layer_output, self_bias_grad,
+            cross_bias_grad, in_bias_total, first_gain_grad, first_shift_grad, self_out_bias_grad,
+            third_gain_grad, third_shift_grad, feed_out_bias_grad, second_gain_grad, second_shift_grad,
+            cross_out_bias_grad,
+        ) = finish_all(n, packed, small, input_grad, memory_grad, layer_output, hidden)
     else:
         packed, small, memory_grad, input_grad, layer_output, count_small = apart(
             n, groups, rows_block, input_rows, memory_rows, cotangent_rows, target_segments, memory_segments,
@@ -1864,44 +1986,47 @@
             second_gain, second_shift, feed_in_weight, feed_in_bias, feed_out_weight, feed_out_bias,
             third_gain, third_shift,
         )
-    plan = []
-    start = 0
-    shapes = []
-    for height, columns in (
-        (half, hidden // features), (hidden // n, 1), (half, 1), (half, 1), (half, 2), (half, 1), (half, 3)
-    ):
-        plan.append((start, columns))
-        shapes.append(out_like((height, columns * features), F32))
-        start += height * columns
-    (
-        feed_in_grad, feed_out_grad, cross_out_total, cross_query_total, cross_pair_total,
-        self_out_total, self_in_total,
-    ) = run(functools.partial(widen_kernel, plan), [packed], 0, shapes, [], 0, 12 << 20)
-    rows_small = small[: count_small * half].reshape(count_small, half)
-    (
-        self_query_bias, self_value_bias, cross_query_bias, cross_value_bias, first_gain_grad,
-        first_shift_grad, self_out_bias_grad, third_gain_grad, third_shift_grad, feed_out_bias_grad,
-        second_gain_grad, second_shift_grad, cross_out_bias_grad,
-    ) = [rows_small[index] for index in range(count_small)]
+        plan = []
+        start = 0
+        shapes = []
+        for height, columns in (
+            (half, hidden // features), (hidden // n, 1), (half, 1), (half, 1), (half, 2), (half, 1), (half, 3)
+        ):
+            plan.append((start, columns))
+            shapes.append(out_like((height, columns * features), F32))
+            start += height * columns
+        (
+            feed_in_grad, feed_out_grad, cross_out_total, cross_query_total, cross_pair_total,
+            self_out_total, self_in_total,
+        ) = run(functools.partial(widen_kernel, plan), [packed], 0, shapes, [], 0, 12 << 20)
+        rows_small = small[: count_small * half].reshape(count_small, half)
+        (
+            self_query_bias, self_value_bias, cross_query_bias, cross_value_bias, first_gain_grad,
+            first_shift_grad, self_out_bias_grad, third_gain_grad, third_shift_grad, feed_out_bias_grad,
+            second_gain_grad, second_shift_grad, cross_out_bias_grad,
+        ) = [rows_small[index] for index in range(count_small)]
+        self_bias_grad = jnp.stack([self_query_bias, self_value_bias])
+        cross_bias_grad = jnp.stack([cross_query_bias, cross_value_bias])
+        in_bias_total = small[count_small * half :]
     return (
         layer_output[None],
         input_grad[None],
         memory_grad[None],
         self_in_total,
-        jnp.stack([self_query_bias, self_value_bias]),
+        self_bias_grad,
         self_out_total,
         self_out_bias_grad,
         first_gain_grad,
         first_shift_grad,
         cross_query_total,
         cross_pair_total,
-        jnp.stack([cross_query_bias, cross_value_bias]),
+        cross_bias_grad,
         cross_out_total,
         cross_out_bias_grad,
         second_gain_grad,
         second_shift_grad,
         feed_in_grad,
-        small[count_small * half :],
+        in_bias_total,
         feed_out_grad,
         feed_out_bias_grad,
         third_gain_grad,

time: 155 us -> 144 us (0.929)
  local copies, waits for them, and re-layouts: 6.91 us -> 0 us
  Pallas kernels: 147 us -> 143 us
    pallas_call x1, Pallas kernels: 92.8 us -> 86.3 us  [back_and_reduce(): pl.pallas_call(functools.partial(back_kernel, n, groups, rows_block, chun...]
    unnamed x11 -> x0, local copies, waits for them, and re-layouts: 4.06 us -> none
    pallas_call x1, Pallas kernels: 5.78 us -> 8.29 us  [finish_all(): pl.pallas_call(functools.partial(finish_kernel, plan), in_specs=[hbm] * 4...]
where the time goes in v4:
time: 144 us
  Pallas kernels  143 us (99%)
    pallas_call x1, Pallas kernels, back_and_reduce(): pl.pallas_call(functools.partial(back_kernel, n, groups, rows_block, chun...  86.3 us
    pallas_call x1, Pallas kernels, forward_all(): pl.pallas_call(functools.partial(forward_kernel, n, groups, rows_block),...  48.1 us
    pallas_call x1, Pallas kernels, finish_all(): pl.pallas_call(functools.partial(finish_kernel, plan), in_specs=[hbm] * 4...  8.29 us

profile of v4, /device:TPU:0, one launch (start us, length us, event | category | flops | bytes accessed | tf_op | source)
XLA Modules:
  0.0 143.6 jit_solution(15765910882092126438)
XLA Ops:
  0.7 48.1 %shard_map.399 = (bf16[2,512,512]{2,1,0:T(8,128)(2,1)}, bf16[2,512,512]{2,1,0:T(8,128)(2,1)}, bf16[512,512]{1,0:T(8,128)(2,1)}, bf16[1024,512]{1,0:T(8,128)(2,1)...) custom-call(bf16[512,512]{1,0:T(8,128)(2,1)} %bitcast.16, ...), custom_call_target="tpu_custom_call" | custom-call | tf_op jit(solution)/shard_map/pallas_call | solution.py:1645
  48.8 86.3 %shard_map.400 = (bf16[4096,512]{1,0:T(8,128)(2,1)}, f32[32,256]{1,0:T(8,128)}, bf16[512,512]{1,0:T(8,128)(2,1)}, bf16[512,512]{1,0:T(8,128)(2,1)}) custom-call(bf16[2,1024,512]{2,1,0:T(8,128)(2,1)} %get-tuple-element.73.refs_0_, bf16[2,1024,512]{2,1,0:T(8,128)(2,1)} %get-tuple-element.74.refs_1_, bf16[2,256,512]{2,1,0:T(8,128)(2,1)} %get-tuple-element.75.refs_2_, ...), custom_call_target="tpu_custom_call" | custom-call | tf_op jit(solution)/shard_map/pallas_call | solution.py:1240
  135.1 8.3 %shard_map.401 = (f32[256,2048]{1,0:T(8,128)}, f32[1024,512]{1,0:T(8,128)}, f32[256,512]{1,0:T(8,128)}, f32[256,512]{1,0:T(8,128)}, f32[256,1024]{1,0:T(8,128)},...) custom-call(bf16[4096,512]{1,0:T(8,128)(2,1)} %get-tuple-element.97., ...), custom_call_target="tpu_custom_call" | custom-call | tf_op jit(solution)/shard_map/pallas_call | solution.py:1759

commit v5 on v4

--- a/solution.py
+++ b/solution.py
@@ -51,14 +51,13 @@
 
 
 def gate(hidden):
-    size = jnp.abs(hidden)
-    bell = jnp.exp(hidden * hidden * -0.5)
-    ratio = 1.0 / (1.0 + (0.3275911 * 0.7071067811865476) * size)
-    series = 1.061405429 * ratio - 1.453152027
-    series = series * ratio + 1.421413741
-    series = series * ratio - 0.284496736
-    series = series * ratio + 0.254829592
-    tail = (0.5 * series) * ratio * bell
+    bell = jnp.exp2(hidden * hidden * (-0.5 * 1.4426950408889634))
+    ratio = 1.0 / (1.0 + (0.3275911 * 0.7071067811865476) * jnp.abs(hidden))
+    series = (0.5 * 1.061405429) * ratio - 0.5 * 1.453152027
+    series = series * ratio + 0.5 * 1.421413741
+    series = series * ratio - 0.5 * 0.284496736
+    series = series * ratio + 0.5 * 0.254829592
+    tail = series * ratio * bell
     phi = jnp.where(hidden > 0.0, 1.0 - tail, tail)
     return hidden * phi, phi + hidden * (bell * 0.3989422804014327)
 
@@ -630,7 +629,7 @@
 MARGIN = 0.5
 
 
-def plan_steps(n, chunks, extras, segments):
+def plan_steps(n, chunks, extras, smalls, segments):
     free = {"core": 0.0, "x": 0.0, "y": 0.0, "z": 0.0}
     now = 0.0
     pending = []
@@ -669,7 +668,8 @@
         else:
             if step == 4:
                 return
-            link, rows = (("core", 64), ("x", 32), ("y", 32), ("z", 128))[step]
+            rows = smalls[index][0]
+            link, rows = (("core", n * rows), ("x", rows), ("y", rows), ("z", 4 * rows))[step]
             ready = send(link, rows, CORE_RATE if link == "core" else LINK_RATE)
         pending.append((ready, len(pending), kind, index, step + 1))
 
@@ -680,8 +680,7 @@
             now += segments[number]
             released = [("chunk", i) for i, chunk in enumerate(chunks) if chunk[3] == number]
             released += [("extra", i) for i, extra in enumerate(extras) if extra[1] == number]
-            if number == max(len(segments) - 2, 0):
-                released.append(("small", 0))
+            released += [("small", i) for i, small in enumerate(smalls) if small[1] == number]
             for kind, index in released:
                 execute(kind, index, 0)
                 order.append((kind, index, 0))
@@ -702,14 +701,14 @@
 
 
 class Reducer:
-    def __init__(self, n, groups, chunks, field, total, total_out, small, small_out, buffers):
+    def __init__(self, n, groups, chunks, field, total, total_out, small, small_out, small_spans, buffers):
         (
             self.from_core, self.from_blk, self.from_y, self.from_z,
             self.small_core, self.small_blk, self.small_y, self.small_z,
             self.sends, self.receives, self.small_sends, self.small_receives, self.stores,
         ) = buffers
         self.n, self.chunks, self.field, self.total, self.total_out = n, chunks, field, total, total_out
-        self.small, self.small_out = small, small_out
+        self.small, self.small_out, self.small_spans = small, small_out, small_spans
         self.depth = depth = groups // 4
         self.group = group = lax.axis_index("dp")
         self.part = part = lax.axis_index("blk")
@@ -861,46 +860,53 @@
         else:
             self.store(index).start()
 
-    def small_copies(self, step):
+    def small_copies(self, index, step):
         part, n = self.part, self.n
+        rows = pl.ds(*self.small_spans[index])
+        first = index * (n + self.depth)
         if step == 0:
-            return [self.small_copy(self.small.at[0], self.small_core, 0, self.core_peer)]
+            return [self.small_copy(self.small.at[0, :, rows], self.small_core.at[:, rows], first, self.core_peer)]
         if step == 1:
             return [
                 self.small_copy(
-                    self.small.at[1, lax.rem(part + hop, n)], self.small_blk.at[hop - 1], hop,
+                    self.small.at[1, lax.rem(part + hop, n), rows], self.small_blk.at[hop - 1, rows], first + hop,
                     self.blk_peers[hop - 1],
                 )
                 for hop in range(1, n)
             ]
         if step == 2:
-            return [self.small_copy(self.small.at[1, part], self.small_y, n, self.side_peer)]
+            return [
+                self.small_copy(self.small.at[1, part, rows], self.small_y.at[rows], first + n, self.side_peer)
+            ]
         return [
-            self.small_copy(self.small_y, self.small_z.at[hop - 1], n + hop, self.z_peers[hop - 1])
+            self.small_copy(
+                self.small_y.at[rows], self.small_z.at[hop - 1, rows], first + n + hop, self.z_peers[hop - 1]
+            )
             for hop in range(1, self.depth)
         ]
 
-    def small_step(self, step):
+    def small_step(self, index, step):
         part = self.part
+        rows = pl.ds(*self.small_spans[index])
         if step > 0:
-            for copy in self.small_copies(step - 1):
+            for copy in self.small_copies(index, step - 1):
                 copy.wait()
         if step == 1:
-            self.small[1] = self.small[0] + self.small_core[...]
+            self.small[1, :, rows] = self.small[0, :, rows] + self.small_core[:, rows]
         elif step == 2:
-            held = self.small[1, part]
+            held = self.small[1, part, rows]
             for hop in range(self.n - 1):
-                held = held + self.small_blk[hop]
-            self.small[1, part] = held
+                held = held + self.small_blk[hop, rows]
+            self.small[1, part, rows] = held
         elif step == 3:
-            self.small_y[...] = self.small_y[...] + self.small[1, part]
+            self.small_y[rows] = self.small_y[rows] + self.small[1, part, rows]
         elif step == 4:
-            held = self.small_y[...]
+            held = self.small_y[rows]
             for hop in range(self.depth - 1):
-                held = held + self.small_z[hop]
-            self.small_out[...] = held
+                held = held + self.small_z[hop, rows]
+            self.small_out[rows] = held
         if step < 4:
-            for copy in self.small_copies(step):
+            for copy in self.small_copies(index, step):
                 copy.start()
 
     def finish(self):
@@ -922,8 +928,8 @@
         pltpu.VMEM((depth - 1, *small_shape), F32),
         pltpu.SemaphoreType.DMA((len(chunks) * per_chunk,)),
         pltpu.SemaphoreType.DMA((len(chunks) * per_chunk,)),
-        pltpu.SemaphoreType.DMA((n + depth,)),
-        pltpu.SemaphoreType.DMA((n + depth,)),
+        pltpu.SemaphoreType.DMA((2 * (n + depth),)),
+        pltpu.SemaphoreType.DMA((2 * (n + depth),)),
         pltpu.SemaphoreType.DMA((len(chunks),)),
     ]
 
@@ -939,7 +945,8 @@
         )
         loads[-1].start()
         start += part_rows[index]
-    reducer = Reducer(n, groups, chunks, field, total, total_out, small, small_out, refs[7:])
+    spans = [(0, small_in.shape[1])]
+    reducer = Reducer(n, groups, chunks, field, total, total_out, small, small_out, spans, refs[7:])
     small[0] = small_in[...]
     reducer.greet()
     reducer.enter()
@@ -950,7 +957,7 @@
             if kind == "chunk":
                 reducer.chunk_step(index, step)
             else:
-                reducer.small_step(step)
+                reducer.small_step(index, step)
     reducer.finish()
 
 
@@ -959,7 +966,7 @@
     rows = sum(part_rows)
     chunk_rows = max(16 * groups, rows // 8)
     chunks = [(start, chunk_rows, False, 0) for start in range(0, rows, chunk_rows)]
-    plan, unused = plan_steps(n, chunks, [], [0.0])
+    plan, unused = plan_steps(n, chunks, [], [(small.shape[1], 0)], [0.0])
     small_shape = small.shape[1:]
     vm = pl.BlockSpec(memory_space=pltpu.VMEM)
     hbm = pl.BlockSpec(memory_space=pl.ANY)
@@ -981,15 +988,15 @@
     )(*parts, small)
 
 
-Y_FIRST = [letter == "y" for letter in "yxxyyxyyyyyyyxxx"]
+Y_FIRST = [letter == "y" for letter in "xyyyyxxyyyyyyxyx"]
 BACK_SEGMENTS = [
-    3.2, 2.9, 2.9, 2.9, 2.9, 1.4, 2.8, 3.2, 2.3, 2.4, 2.4, 2.9, 2.9, 1.4, 1.1, 1.1, 2.2, 2.0,
+    1.6, 1.6, 2.9, 2.9, 2.9, 2.9, 1.4, 2.8, 3.2, 2.3, 2.4, 2.4, 2.9, 2.9, 1.4, 1.1, 1.1,
 ]
 
 
 def back_chunks(half, hidden_rows):
     released = [(half, 0)] * (2 * hidden_rows // half + 1)
-    released += [(half, segment) for segment in (5, 6, 6, 7, 13, 14, 15)]
+    released += [(half, segment) for segment in (6, 7, 7, 8, 14, 15, 16)]
     chunks = []
     start = 0
     for index, (rows, segment) in enumerate(released):
@@ -1002,15 +1009,15 @@
     feed_refs, refs = refs[:3], refs[3:]
     streamed, refs = refs[: len(load_plan)], refs[len(load_plan) :]
     (
-        target_row, memory_row, cross_query, cross_grad, cross_keys, cross_values,
+        target_row, memory_row, cross_query, cross_grad, cross_keys,
         cross_lse, cross_delta, feed_sums, in_bias_grad, gain, first_rstd, self_lse,
         total_out, small_out, memory_out, input_out,
         field, total, small, sums, memory_grad, input_grad, memory_sent, memory_got, input_sent, input_got, pair_low,
         wide, keys_t, query_cols, query_rows, grad_cols, grad_rows, query_grad_t, key_grad, value_grad,
         held, held_low, held_grad, query_low, branch, self_grad, self_delta, g1,
         feed_sem, load_sem, extra_send, extra_recv, extra_store,
-    ) = refs[:50]
-    refs = refs[50:]
+    ) = refs[:49]
+    refs = refs[49:]
     held_loads, buffers = refs[: len(load_plan)], refs[len(load_plan) :]
     count = cross_query.shape[0]
     length = cross_keys.shape[0]
@@ -1037,8 +1044,9 @@
     ]
     for load in loads:
         load.start()
-    memory_pieces = [held_loads[0].at[step] for step in range(n)]
-    held_loads = held_loads[1:]
+    cross_values = held_loads[0]
+    memory_pieces = [held_loads[1].at[step] for step in range(n)]
+    held_loads = held_loads[2:]
     (
         pair_weight, first_low, query_weight, g2, first_normal, self_out_weight, self_attended_t,
         self_keys, self_values, self_query,
@@ -1046,7 +1054,8 @@
     input_pieces = [held_loads[10].at[step] for step in range(n)]
     self_in_weight = held_loads[11]
 
-    reducer = Reducer(n, groups, chunks, field, total, total_out, small, small_out, buffers)
+    spans = [(0, 8), (8, small_out.shape[0] - 8)]
+    reducer = Reducer(n, groups, chunks, field, total, total_out, small, small_out, spans, buffers)
     reducer.greet(owner, away)
 
     extras = (
@@ -1097,7 +1106,7 @@
             if kind == "chunk":
                 reducer.chunk_step(index, step)
             elif kind == "small":
-                reducer.small_step(step)
+                reducer.small_step(index, step)
             else:
                 extra_step(index, step)
 
@@ -1107,27 +1116,29 @@
 
     spread_row(memory_row, wide)
     transpose_rows(cross_keys, keys_t)
+    for load in feed_loads:
+        load.wait()
+    reducer.enter()
+    run_steps(0)
     prepare_back(tiles, cross_query, cross_grad, query_cols, query_rows, grad_cols, grad_rows)
     clear(query_grad_t)
     clear(key_grad)
     clear(value_grad)
     sums[...] = jnp.zeros(sums.shape, F32)
-    for load in feed_loads:
-        load.wait()
-    reducer.enter()
-    run_steps(0)
+    run_steps(1)
+    wait_loads(0, 1)
     for tile in range(tiles):
         attend_back(
             tile, 0, length // TILE, target_row, place * count, wide, place * count, False,
             query_cols, query_rows, grad_cols, grad_rows, cross_keys, keys_t, cross_values,
             cross_lse, cross_delta, query_grad_t, key_grad, value_grad, held, held_low, held_grad,
         )
-        run_steps(1 + tile)
+        run_steps(2 + tile)
     base = 2 * in_bias_grad.shape[1] // n + half
-    wait_loads(0, 8)
+    wait_loads(1, 9)
     query_finish(tiles, query_grad_t, query_low, sums, 2, True)
     spread_parts(n, tn(first_low[...], query_low[...]), field, base)
-    run_steps(5)
+    run_steps(6)
     for side, source in ((0, key_grad), (1, value_grad)):
 
         @pl.loop(0, length // rows_block)
@@ -1141,70 +1152,78 @@
         spread_parts(
             n, row_product(n, place, memory_pieces, pair_low.at[side]), field, base + half + side * half
         )
-    run_steps(6)
+    run_steps(7)
     first_back(
         blocks, rows_block, g2, query_low, query_weight, first_normal, first_rstd, gain, self_out_weight,
         g1, branch, self_grad, sums, 4,
     )
     spread_parts(n, nn(self_attended_t[...], branch[...]), field, base + 3 * half)
     write_delta(tiles, self_grad, self_attended_t, self_delta)
-    run_steps(7)
-
-    wait_loads(8, len(loads))
+    small[...] = jnp.zeros(small.shape, F32)
+    wide_half = in_bias_grad.shape[1] // n
+    for b in range(n):
+        here = slice(b * half, (b + 1) * half)
+        small[0, b, 8:13, :] = sums[2:7, here]
+        small[0, b, 13:19, :] = feed_sums[0:6, here]
+        for row in range(wide_half // half):
+            begin = b * wide_half + row * half
+            small[0, b, 19 + row : 20 + row, :] = in_bias_grad[:, begin : begin + half]
+    run_steps(8)
+
+    wait_loads(9, len(loads))
     spread_row(target_row, wide)
     transpose_rows(self_keys, keys_t)
     prepare_back(tiles, self_query, self_grad, query_cols, query_rows, grad_cols, grad_rows)
     clear(query_grad_t)
     clear(key_grad)
     clear(value_grad)
-    run_steps(8)
+    run_steps(9)
     for tile in range(tiles):
         attend_back(
             tile, 0, place * tiles + tile + 1, target_row, place * count, wide, place * count, True,
             query_cols, query_rows, grad_cols, grad_rows, self_keys, keys_t, self_values,
             self_lse, self_delta, query_grad_t, key_grad, value_grad, held, held_low, held_grad,
         )
-        run_steps(9 + tile)
+        run_steps(10 + tile)
     query_finish(tiles, query_grad_t, query_low, sums, 0, False)
     spread_parts(n, tn(input_pieces[0][...], query_low[...]), field, base + 4 * half)
-    run_steps(13)
+    run_steps(14)
     spread_parts(n, row_product(n, place, input_pieces, key_grad), field, base + 5 * half)
-    run_steps(14)
+    run_steps(15)
     spread_parts(n, row_product(n, place, input_pieces, value_grad), field, base + 6 * half)
-    run_steps(15)
+    run_steps(16)
+    number = 17
     for step in range(n):
-
-        def write(here, back):
+        spot = lax.rem(place + n - step, n)
+        for block in range(blocks):
+            rows = dyn(spot * blocks + block, rows_block)
+            here = slice(block * rows_block, (block + 1) * rows_block)
+            key_low, value_part = key_grad[rows, :].astype(BF16), value_grad[rows, :]
+            sums[1:2, :] += col_sum(value_part)
+            back = nt(key_low, self_in_weight[:, WIDE : 2 * WIDE])
+            back += nt(value_part.astype(BF16), self_in_weight[:, 2 * WIDE :])
             if step == 0:
                 input_grad[here, :] = back + g1[here, :] + nt(query_low[here, :], self_in_weight[:, :WIDE])
             else:
                 input_sent[0, here, :] = back.astype(BF16)
-
-        pair_back(n, place, rows_block, count, step, key_grad, value_grad, self_in_weight, WIDE, sums, 1, write)
-    small[...] = jnp.zeros(small.shape, F32)
-    for part in range(n):
-        here = slice(part * half, (part + 1) * half)
-        small[0, part, 0:7, :] = sums[0:7, here]
-        small[0, part, 7:13, :] = feed_sums[0:6, here]
-        wide_half = in_bias_grad.shape[1] // n
-        for row in range(wide_half // half):
-            begin = part * wide_half + row * half
-            small[0, part, 13 + row : 14 + row, :] = in_bias_grad[:, begin : begin + half]
-    run_steps(16)
+            if step == n - 1 and block == blocks - 1:
+                for b in range(n):
+                    small[0, b, 0:2, :] = sums[0:2, b * half : (b + 1) * half]
+            run_steps(number)
+            number += 1
     for step in range(n):
         spot = lax.rem(place + n - step, n)
-
-        @pl.loop(0, blocks)
-        def _(block):
-            rows, here = dyn(spot * blocks + block, rows_block), dyn(block, rows_block)
+        for block in range(blocks):
+            rows = dyn(spot * blocks + block, rows_block)
+            here = slice(block * rows_block, (block + 1) * rows_block)
             back = nt(pair_low[0, rows, :], pair_weight[:, :WIDE]) + nt(pair_low[1, rows, :], pair_weight[:, WIDE:])
             if step == 0:
                 memory_grad[here, :] = back
             else:
                 memory_sent[0, here, :] = back.astype(BF16)
-
-    run_steps(17)
-    run_steps(18)
+            run_steps(number)
+            number += 1
+    run_steps(number)
     for index in range(2):
 
         @pl.when(away)
@@ -1225,9 +1244,13 @@
     half = features // n
     rows = sum(part.shape[1] for part in feed_grads) + 7 * half
     chunks = back_chunks(half, hidden_rows)
-    extras = [(count, 17), (count, 16)]
-    plan, unused = plan_steps(n, chunks, extras, BACK_SEGMENTS)
-    small_shape = (-(-(13 + hidden_rows // half * half * n // features) // 8) * 8 + 8, half)
+    steps = n * (count // rows_block)
+    segments = BACK_SEGMENTS + [2.2 / steps] * steps + [2.0 / steps] * steps
+    last = len(segments) - 1
+    extras = [(count, last), (count, last - steps)]
+    smalls = [(8, last - steps), (16, 8)]
+    plan, unused = plan_steps(n, chunks, extras, smalls, segments)
+    small_shape = (-(-(19 + hidden_rows // half) // 8) * 8, half)
     vm = pl.BlockSpec(memory_space=pltpu.VMEM)
     hbm = pl.BlockSpec(memory_space=pl.ANY)
     low_rows = pltpu.VMEM((count, features), BF16)
@@ -1439,14 +1462,15 @@
 
     def project(piece, block, spot):
         rows = slice(block * (count // 2), (block + 1) * (count // 2))
-        source = input_pieces[piece, rows, :]
+        first = 0 if piece == 0 else WIDE
+        field = nn(input_pieces[piece, rows, :], self_in_weight[:, first:])
         here = dyn(spot * 2 + block, count // 2)
-        keys[here, :] = nn(source, self_in_weight[:, WIDE : 2 * WIDE]).astype(BF16)
-        value = (nn(source, self_in_weight[:, 2 * WIDE :]) + in_bias[1:2, :]).astype(BF16)
+        keys[here, :] = field[:, WIDE - first : 2 * WIDE - first].astype(BF16)
+        value = (field[:, 2 * WIDE - first :] + in_bias[1:2, :]).astype(BF16)
         values[here, :] = value
         values_t[:, here] = value.T
         if piece == 0:
-            query = (nn(source, self_in_weight[:, :WIDE]) + in_bias[0:1, :]).astype(BF16)
+            query = (field[:, :WIDE] + in_bias[0:1, :]).astype(BF16)
             query = (query.astype(F32) * SCALE).astype(BF16)
             query_low[rows, :] = query
             for tile in range(count // 2 // TILE):
@@ -1498,20 +1522,18 @@
     store(7)
     store(8)
 
-    def project_memory(piece, block, spot):
-        rows = slice(block * (count // 2), (block + 1) * (count // 2))
-        source = memory_pieces[piece, rows, :]
-        here = dyn(spot * 2 + block, count // 2)
-        cross_keys[here, :] = nn(source, pair_weight[:, :WIDE]).astype(BF16)
-        value = (nn(source, pair_weight[:, WIDE:]) + cross_bias[1:2, :]).astype(BF16)
+    def project_memory(piece, spot):
+        field = nn(memory_pieces[piece], pair_weight[...])
+        here = dyn(spot, count)
+        cross_keys[here, :] = field[:, :WIDE].astype(BF16)
+        value = (field[:, WIDE:] + cross_bias[1:2, :]).astype(BF16)
         cross_values[here, :] = value
         values_t[:, here] = value.T
 
-    for block in range(2):
-        project_memory(0, block, place)
+    project_memory(0, place)
     for block in range(2):
         forward_copy(2 + block).wait()
-        project_memory(1, block, 1 - place)
+    project_memory(1, 1 - place)
     store(1)
     store(9)
     store(10)
@@ -1541,9 +1563,9 @@
     chunks, chunk_size = in_weight.shape[1] // WIDE, WIDE
     arrive(arrivals[4])
 
-    @pl.loop(0, chunks)
+    @pl.loop(0, chunks // 2)
     def _(chunk):
-        lanes = dyn(chunk, chunk_size)
+        lanes = dyn(chunk, 2 * chunk_size)
         hidden = nn(second_low[...], in_weight[:, lanes]) + feed_bias[:, lanes]
         value, derivative = gate(hidden)
         value = value.astype(BF16)
@@ -1643,7 +1665,7 @@
     held = (features // PAIR, length, 2 * TILE)
     low_rows, wide_rows = pltpu.VMEM(low, BF16), pltpu.VMEM(wide, F32)
     return pl.pallas_call(
-        functools.partial(forward_kernel, n, groups, rows_block),
+        functools.partial(forward_kernel, n, groups, count),
         in_specs=[hbm] * (len(activations) + len(weights)) + [vm] * len(resident),
         out_specs=[hbm] * len(stored) + [vm] * 9,
         out_shape=[out_like(*entry) for entry in stored] + [
@@ -1702,12 +1724,14 @@
     ]
     output = pltpu.make_async_copy(output_low, output_held, load_sem.at[count + 2])
     loads = [load(index) for index in range(count)]
-    for copy in loads + extra + [output]:
+    order = sorted(range(count), key=lambda index: held[index].shape[0])
+    for index in order:
+        loads[index].start()
+    for copy in extra + [output]:
         copy.start()
-    stores = [pltpu.make_async_copy(output_held, layer_output, store_sem.at[count + 2])]
-    output.wait()
-    stores[0].start()
-    for index, (start, columns) in enumerate(plan):
+    stores = []
+    for index in order:
+        start, columns = plan[index]
         loads[index].wait()
         height = wide[index].shape[0]
 
@@ -1730,13 +1754,16 @@
 
         stores.append(pltpu.make_async_copy(target, result, store_sem.at[count + index]))
         stores[-1].start()
+    output.wait()
+    stores.append(pltpu.make_async_copy(output_held, layer_output, store_sem.at[count + 2]))
+    stores[-1].start()
     self_bias[...] = small[0:2, :]
-    cross_bias[...] = small[2:4, :]
+    cross_bias[...] = small[8:10, :]
     for index, vector in enumerate(vectors):
-        vector[...] = small[4 + index, :]
+        vector[...] = small[10 + index, :]
     half = small.shape[1]
     for row in range(feed_bias.shape[0] // half):
-        feed_bias[row * half : (row + 1) * half] = small[13 + row, :]
+        feed_bias[row * half : (row + 1) * half] = small[19 + row, :]
     for copy in stores:
         copy.wait()
 
@@ -1966,9 +1993,9 @@
         packed, small, memory_grad, input_grad = back_and_reduce(
             n, groups, rows_block,
             [in_grad, down_grad, cross_out_grad],
-            [memory_pieces, cross_pair_weight, first_low, cross_query_weight, g2, normal, self_out_weight,
+            [cross_values, memory_pieces, cross_pair_weight, first_low, cross_query_weight, g2, normal, self_out_weight,
              attended_t, keys, values, query, input_pieces, self_in_weight],
-            [target_row, memory_row, cross_query, cross_grad, cross_keys, cross_values,
+            [target_row, memory_row, cross_query, cross_grad, cross_keys,
              cross_lse, cross_delta, feed_sums, in_bias_grad, row(first_gain), rstd, lse],
         )
         (

time: 144 us -> 140 us (0.972)
  Pallas kernels: 143 us -> 139 us
    pallas_call x1, Pallas kernels: 48.1 us -> 46 us  [forward_all(): pl.pallas_call(functools.partial(forward_kernel, n, groups, count), in_sp...]
where the time goes in v5:
time: 140 us
  Pallas kernels  139 us (99%)
    pallas_call x1, Pallas kernels, back_and_reduce(): pl.pallas_call(functools.partial(back_kernel, n, groups, rows_block, chun...  86.1 us
    pallas_call x1, Pallas kernels, forward_all(): pl.pallas_call(functools.partial(forward_kernel, n, groups, count), in_sp...  46 us
    pallas_call x1, Pallas kernels, finish_all(): pl.pallas_call(functools.partial(finish_kernel, plan), in_specs=[hbm] * 4...  6.88 us

profile of v5, /device:TPU:0, one launch (start us, length us, event | category | flops | bytes accessed | tf_op | source)
XLA Modules:
  0.0 139.8 jit_solution(1050288486952552284)
XLA Ops:
  0.7 46.0 %shard_map.399 = (bf16[2,512,512]{2,1,0:T(8,128)(2,1)}, bf16[2,512,512]{2,1,0:T(8,128)(2,1)}, bf16[512,512]{1,0:T(8,128)(2,1)}, bf16[1024,512]{1,0:T(8,128)(2,1)...) custom-call(bf16[512,512]{1,0:T(8,128)(2,1)} %bitcast.16, ...), custom_call_target="tpu_custom_call" | custom-call | tf_op jit(solution)/shard_map/pallas_call | solution.py:1667
  46.6 86.1 %shard_map.400 = (bf16[4096,512]{1,0:T(8,128)(2,1)}, f32[24,256]{1,0:T(8,128)}, bf16[512,512]{1,0:T(8,128)(2,1)}, bf16[512,512]{1,0:T(8,128)(2,1)}) custom-call(bf16[2,1024,512]{2,1,0:T(8,128)(2,1)} %get-tuple-element.73.refs_0_, bf16[2,1024,512]{2,1,0:T(8,128)(2,1)} %get-tuple-element.74.refs_1_, bf16[2,256,512]{2,1,0:T(8,128)(2,1)} %get-tuple-element.75.refs_2_, ...), custom_call_target="tpu_custom_call" | custom-call | tf_op jit(solution)/shard_map/pallas_call | solution.py:1263
  132.8 6.9 %shard_map.401 = (f32[256,2048]{1,0:T(8,128)}, f32[1024,512]{1,0:T(8,128)}, f32[256,512]{1,0:T(8,128)}, f32[256,512]{1,0:T(8,128)}, f32[256,1024]{1,0:T(8,128)},...) custom-call(bf16[4096,512]{1,0:T(8,128)(2,1)} %get-tuple-element.97., ...), custom_call_target="tpu_custom_call" | custom-call | tf_op jit(solution)/shard_map/pallas_call | solution.py:1786

commit v6 on v5

--- a/solution.py
+++ b/solution.py
@@ -174,7 +174,7 @@
 def attend_back(
     tile, low, high, query_row_ref, first_query, key_wide_ref, offset, causal,
     query_cols, query_rows, grad_cols, grad_rows, keys, keys_t, values, lse_ref, delta_ref,
-    query_grad_t, key_grad, value_grad, held, held_low, held_grad,
+    query_grad_t, key_grad, value_grad, held, held_low, held_grad, fresh=False,
 ):
     pairs = WIDE // PAIR
     query_row = query_row_ref[:, pl.ds(pl.multiple_of(first_query + tile * TILE, TILE), TILE)]
@@ -199,8 +199,10 @@
             held_grad[pair] = (held[pair] * (prob_grad - delta_ref[pair : pair + 1, both])).astype(BF16)
         for pair in range(pairs):
             lanes = slice(pair * PAIR, (pair + 1) * PAIR)
-            value_grad[rows, lanes] += nn(held_low[pair], grad_rows[both, lanes])
-            key_grad[rows, lanes] += nn(held_grad[pair], query_rows[both, lanes])
+            value_part = nn(held_low[pair], grad_rows[both, lanes])
+            key_part = nn(held_grad[pair], query_rows[both, lanes])
+            value_grad[rows, lanes] = value_part if fresh else value_grad[rows, lanes] + value_part
+            key_grad[rows, lanes] = key_part if fresh else key_grad[rows, lanes] + key_part
             mixed = nn(keys_t[lanes, rows], held_grad[pair])
             first = slice(pair * PAIR, pair * PAIR + HEAD)
             second = slice(pair * PAIR + HEAD, (pair + 1) * PAIR)
@@ -990,7 +992,7 @@
 
 Y_FIRST = [letter == "y" for letter in "xyyyyxxyyyyyyxyx"]
 BACK_SEGMENTS = [
-    1.6, 1.6, 2.9, 2.9, 2.9, 2.9, 1.4, 2.8, 3.2, 2.3, 2.4, 2.4, 2.9, 2.9, 1.4, 1.1, 1.1,
+    1.5, 1.3, 2.9, 2.9, 2.9, 2.9, 1.4, 2.8, 3.2, 1.9, 2.4, 2.4, 2.9, 2.9, 1.4, 1.1, 1.1,
 ]
 
 
@@ -1122,8 +1124,6 @@
     run_steps(0)
     prepare_back(tiles, cross_query, cross_grad, query_cols, query_rows, grad_cols, grad_rows)
     clear(query_grad_t)
-    clear(key_grad)
-    clear(value_grad)
     sums[...] = jnp.zeros(sums.shape, F32)
     run_steps(1)
     wait_loads(0, 1)
@@ -1131,7 +1131,7 @@
         attend_back(
             tile, 0, length // TILE, target_row, place * count, wide, place * count, False,
             query_cols, query_rows, grad_cols, grad_rows, cross_keys, keys_t, cross_values,
-            cross_lse, cross_delta, query_grad_t, key_grad, value_grad, held, held_low, held_grad,
+            cross_lse, cross_delta, query_grad_t, key_grad, value_grad, held, held_low, held_grad, tile == 0,
         )
         run_steps(2 + tile)
     base = 2 * in_bias_grad.shape[1] // n + half
@@ -1145,6 +1145,7 @@
         def _(block):
             rows = dyn(block, rows_block)
             value = source[rows, :]
+            source[rows, :] = jnp.zeros(value.shape, F32)
             pair_low[side, rows, :] = value.astype(BF16)
             if side == 1:
                 sums[3:4, :] += col_sum(value)
@@ -1175,8 +1176,6 @@
     transpose_rows(self_keys, keys_t)
     prepare_back(tiles, self_query, self_grad, query_cols, query_rows, grad_cols, grad_rows)
     clear(query_grad_t)
-    clear(key_grad)
-    clear(value_grad)
     run_steps(9)
     for tile in range(tiles):
         attend_back(
@@ -1362,8 +1361,8 @@
         cross_keys, cross_values, grad_out, g2_out, in_grad, down_grad, cross_out_grad,
     ) = held_stores
     (
-        cot, output_low, output_got, target_there, memory_there, wide, values_t, query_cols, held, held_low,
-        attended_two, second_normal, second_rstd, second_low, second_low_t, active, slope, third, branch,
+        cot, output_low, output_got, target_there, memory_there, wide, values_t, cross_values_t, query_cols, held,
+        held_low, attended_two, second_normal, second_rstd, second_low, second_low_t, active, slope, third, branch,
         load_sem, store_sem, own_sem, far_send, far_recv, core_send, core_recv,
     ) = refs
     count = inputs.shape[0]
@@ -1462,15 +1461,17 @@
 
     def project(piece, block, spot):
         rows = slice(block * (count // 2), (block + 1) * (count // 2))
-        first = 0 if piece == 0 else WIDE
-        field = nn(input_pieces[piece, rows, :], self_in_weight[:, first:])
+        source = input_pieces[piece, rows, :]
+        field = nn(source, self_in_weight[:, WIDE:])
         here = dyn(spot * 2 + block, count // 2)
-        keys[here, :] = field[:, WIDE - first : 2 * WIDE - first].astype(BF16)
-        value = (field[:, 2 * WIDE - first :] + in_bias[1:2, :]).astype(BF16)
+        keys[here, :] = field[:, :WIDE].astype(BF16)
+        value = (field[:, WIDE:] + in_bias[1:2, :]).astype(BF16)
         values[here, :] = value
         values_t[:, here] = value.T
-        if piece == 0:
-            query = (field[:, :WIDE] + in_bias[0:1, :]).astype(BF16)
+
+        @pl.when(piece == 0)
+        def _():
+            query = (nn(source, self_in_weight[:, :WIDE]) + in_bias[0:1, :]).astype(BF16)
             query = (query.astype(F32) * SCALE).astype(BF16)
             query_low[rows, :] = query
             for tile in range(count // 2 // TILE):
@@ -1478,13 +1479,51 @@
                     query[tile * TILE : (tile + 1) * TILE, :].T, query_cols, block * (count // 2 // TILE) + tile
                 )
 
+    def project_memory(piece, spot):
+        field = nn(memory_pieces[piece], pair_weight[...])
+        here = dyn(spot, count)
+        cross_keys[here, :] = field[:, :WIDE].astype(BF16)
+        value = (field[:, WIDE:] + cross_bias[1:2, :]).astype(BF16)
+        cross_values[here, :] = value
+        cross_values_t[:, here] = value.T
+
+    early = jnp.where(away, 1, 0)
+
+    @pl.when(jnp.logical_not(away))
+    def _():
+        for index in range(4):
+            own_copy(arrivals[index]).wait()
+            forward_copy(index).start()
+
+    @pl.when(away)
+    def _():
+        for index in range(2):
+            forward_copy(index).wait_recv()
+
     for block in range(2):
-        arrive(arrivals[block])
-        forward_copy(block).start()
-        project(0, block, place)
+        project(early, block, part)
+    loads[3].wait()
+
+    @pl.when(away)
+    def _():
+        for index in range(2, 4):
+            forward_copy(index).wait_recv()
+
+    project_memory(early, part)
     for block in range(2):
-        forward_copy(block).wait()
-        project(1, block, 1 - place)
+
+        @pl.when(away)
+        def _():
+            far_copy(arrivals[block]).wait()
+            forward_copy(block).start()
+
+        @pl.when(jnp.logical_not(away))
+        def _():
+            forward_copy(block).wait_recv()
+
+        project(1 - early, block, 1 - part)
+    for index in range(2):
+        forward_copy(index).wait_send()
     store(0)
     store(2)
     store(3)
@@ -1494,11 +1533,14 @@
         held, held_low,
     )
     store(5)
-    for load in loads[1:4]:
+    for load in loads[1:3]:
         load.wait()
-    for block in range(2):
-        arrive(arrivals[2 + block])
-        forward_copy(2 + block).start()
+
+    @pl.when(away)
+    def _():
+        for index in range(2, 4):
+            far_copy(arrivals[index]).wait()
+            forward_copy(index).start()
 
     @pl.loop(0, blocks)
     def _(block):
@@ -1522,24 +1564,20 @@
     store(7)
     store(8)
 
-    def project_memory(piece, spot):
-        field = nn(memory_pieces[piece], pair_weight[...])
-        here = dyn(spot, count)
-        cross_keys[here, :] = field[:, :WIDE].astype(BF16)
-        value = (field[:, WIDE:] + cross_bias[1:2, :]).astype(BF16)
-        cross_values[here, :] = value
-        values_t[:, here] = value.T
-
-    project_memory(0, place)
-    for block in range(2):
-        forward_copy(2 + block).wait()
-    project_memory(1, 1 - place)
+    @pl.when(jnp.logical_not(away))
+    def _():
+        for index in range(2, 4):
+            forward_copy(index).wait_recv()
+
+    project_memory(1 - early, 1 - part)
+    for index in range(2, 4):
+        forward_copy(index).wait_send()
     store(1)
     store(9)
     store(10)
     spread_row(memory_row, wide)
     attend_whole(
-        tiles, target_row, place * count, wide, False, query_cols, cross_keys, values_t, attended_two, lse_two,
+        tiles, target_row, place * count, wide, False, query_cols, cross_keys, cross_values_t, attended_two, lse_two,
         held, held_low,
     )
     for load in loads[4:]:
@@ -1677,7 +1715,7 @@
             *[pltpu.VMEM(*entry) for entry in stored],
             low_rows, low_rows, low_rows, row_scratch, row_scratch,
             pltpu.VMEM((length, TILE), jnp.int32), pltpu.VMEM((features, length), BF16),
-            pltpu.VMEM((features, 2 * count), BF16), pltpu.VMEM(held, F32), pltpu.VMEM(held, BF16),
+            pltpu.VMEM((features, length), BF16), pltpu.VMEM((features, 2 * count), BF16), pltpu.VMEM(held, F32), pltpu.VMEM(held, BF16),
             pltpu.VMEM((features, count), BF16), wide_rows, pltpu.VMEM((count, 1), F32), low_rows,
             pltpu.VMEM((features, count), BF16), pltpu.VMEM((count, hidden), BF16),
             pltpu.VMEM((count, hidden), F32), wide_rows, low_rows,

time: 140 us -> 139 us (level)
  Pallas kernels: 139 us -> 137 us
where the time goes in v6:
time: 139 us; the launch traced here: 138 us
  Pallas kernels  137 us (99%)
    pallas_call x1, Pallas kernels, back_and_reduce(): pl.pallas_call(functools.partial(back_kernel, n, groups, rows_block, chun...  85.1 us
    pallas_call x1, Pallas kernels, forward_all(): pl.pallas_call(functools.partial(forward_kernel, n, groups, count), in_sp...  45.4 us
    pallas_call x1, Pallas kernels, finish_all(): pl.pallas_call(functools.partial(finish_kernel, plan), in_specs=[hbm] * 4...  6.88 us

profile of v6, /device:TPU:0, one launch (start us, length us, event | category | flops | bytes accessed | tf_op | source)
XLA Modules:
  0.0 138.3 jit_solution(11735916137337654252)
XLA Ops:
  0.7 45.4 %shard_map.399 = (bf16[2,512,512]{2,1,0:T(8,128)(2,1)}, bf16[2,512,512]{2,1,0:T(8,128)(2,1)}, bf16[512,512]{1,0:T(8,128)(2,1)}, bf16[1024,512]{1,0:T(8,128)(2,1)...) custom-call(bf16[512,512]{1,0:T(8,128)(2,1)} %bitcast.16, ...), custom_call_target="tpu_custom_call" | custom-call | tf_op jit(solution)/shard_map/pallas_call | solution.py:1705
  46.1 85.1 %shard_map.400 = (bf16[4096,512]{1,0:T(8,128)(2,1)}, f32[24,256]{1,0:T(8,128)}, bf16[512,512]{1,0:T(8,128)(2,1)}, bf16[512,512]{1,0:T(8,128)(2,1)}) custom-call(bf16[2,1024,512]{2,1,0:T(8,128)(2,1)} %get-tuple-element.73.refs_0_, bf16[2,1024,512]{2,1,0:T(8,128)(2,1)} %get-tuple-element.74.refs_1_, bf16[2,256,512]{2,1,0:T(8,128)(2,1)} %get-tuple-element.75.refs_2_, ...), custom_call_target="tpu_custom_call" | custom-call | tf_op jit(solution)/shard_map/pallas_call | solution.py:1262
  131.2 6.9 %shard_map.401 = (f32[256,2048]{1,0:T(8,128)}, f32[1024,512]{1,0:T(8,128)}, f32[256,512]{1,0:T(8,128)}, f32[256,512]{1,0:T(8,128)}, f32[256,1024]{1,0:T(8,128)},...) custom-call(bf16[4096,512]{1,0:T(8,128)(2,1)} %get-tuple-element.97., ...), custom_call_target="tpu_custom_call" | custom-call | tf_op jit(solution)/shard_map/pallas_call | solution.py:1824

commit v7 on v6

--- a/solution.py
+++ b/solution.py
@@ -10,7 +10,7 @@
 HEAD = 64
 TILE = 128
 KEYS = 256
-BACK_KEYS = 256
+BACK_KEYS = 512
 PAIR = 2 * HEAD
 WIDE = 512
 SCALE = HEAD ** (-0.5)
@@ -1171,6 +1171,7 @@
             small[0, b, 19 + row : 20 + row, :] = in_bias_grad[:, begin : begin + half]
     run_steps(8)
 
+    narrow = [ref.at[:, pl.ds(0, KEYS)] for ref in (held, held_low, held_grad)]
     wait_loads(9, len(loads))
     spread_row(target_row, wide)
     transpose_rows(self_keys, keys_t)
@@ -1181,7 +1182,7 @@
         attend_back(
             tile, 0, place * tiles + tile + 1, target_row, place * count, wide, place * count, True,
             query_cols, query_rows, grad_cols, grad_rows, self_keys, keys_t, self_values,
-            self_lse, self_delta, query_grad_t, key_grad, value_grad, held, held_low, held_grad,
+            self_lse, self_delta, query_grad_t, key_grad, value_grad, *narrow,
         )
         run_steps(10 + tile)
     query_finish(tiles, query_grad_t, query_low, sums, 0, False)

time: 139 us -> 138 us (level)
  no operation moved by 1% of the time
where the time goes in v7:
time: 138 us
  Pallas kernels  137 us (99%)
    pallas_call x1, Pallas kernels, back_and_reduce(): pl.pallas_call(functools.partial(back_kernel, n, groups, rows_block, chun...  84.9 us
    pallas_call x1, Pallas kernels, forward_all(): pl.pallas_call(functools.partial(forward_kernel, n, groups, count), in_sp...  45.4 us
    pallas_call x1, Pallas kernels, finish_all(): pl.pallas_call(functools.partial(finish_kernel, plan), in_specs=[hbm] * 4...  6.88 us

profile of v7, /device:TPU:0, one launch (start us, length us, event | category | flops | bytes accessed | tf_op | source)
XLA Modules:
  0.0 138.1 jit_solution(9112614167564651416)
XLA Ops:
  0.7 45.4 %shard_map.399 = (bf16[2,512,512]{2,1,0:T(8,128)(2,1)}, bf16[2,512,512]{2,1,0:T(8,128)(2,1)}, bf16[512,512]{1,0:T(8,128)(2,1)}, bf16[1024,512]{1,0:T(8,128)(2,1)...) custom-call(bf16[512,512]{1,0:T(8,128)(2,1)} %bitcast.16, ...), custom_call_target="tpu_custom_call" | custom-call | tf_op jit(solution)/shard_map/pallas_call | solution.py:1706
  46.1 84.9 %shard_map.400 = (bf16[4096,512]{1,0:T(8,128)(2,1)}, f32[24,256]{1,0:T(8,128)}, bf16[512,512]{1,0:T(8,128)(2,1)}, bf16[512,512]{1,0:T(8,128)(2,1)}) custom-call(bf16[2,1024,512]{2,1,0:T(8,128)(2,1)} %get-tuple-element.73.refs_0_, bf16[2,1024,512]{2,1,0:T(8,128)(2,1)} %get-tuple-element.74.refs_1_, bf16[2,256,512]{2,1,0:T(8,128)(2,1)} %get-tuple-element.75.refs_2_, ...), custom_call_target="tpu_custom_call" | custom-call | tf_op jit(solution)/shard_map/pallas_call | solution.py:1263
  131.0 6.9 %shard_map.401 = (f32[256,2048]{1,0:T(8,128)}, f32[1024,512]{1,0:T(8,128)}, f32[256,512]{1,0:T(8,128)}, f32[256,512]{1,0:T(8,128)}, f32[256,1024]{1,0:T(8,128)},...) custom-call(bf16[4096,512]{1,0:T(8,128)(2,1)} %get-tuple-element.97., ...), custom_call_target="tpu_custom_call" | custom-call | tf_op jit(solution)/shard_map/pallas_call | solution.py:1825
